TPU v7x, 256 devices: a whole 4x4x8 slice. The times are simulated.
256 devices in a mesh: lon: 4 (over x), lat: 4 (over y), lev: 16 (over z, core).
Axes of the slice: x: 4, y: 4, z: 8, core: 2. Of those that a mesh axis runs over, the one named last changes fastest.
Arguments:
- control: float32 [6, 48, 256, 512], P(None, 'lev', 'lat', 'lon'), may hold values from -6 to 6
- vertical: float32 [6, 48, 48], replicated, may hold values from -0.875 to 0.875
- lon_taps: float32 [6, 48, 31], P(None, 'lev'), may hold values from 0.03 to 0.12
- lat_taps: float32 [6, 48, 31], P(None, 'lev'), may hold values from 0.03 to 0.12
- innovation: float32 [6, 48, 8192], P(None, 'lev', ('lon', 'lat')), may hold values from -12 to 12
- inv_variance: float32 [6, 48], P(None, 'lev'), may hold values from 0.5 to 2
- obs_tile: int32 [8192], P(('lon', 'lat')), may hold values from 0 to 15, as said below
- obs_cell: int32 [8192], P(('lon', 'lat')), may hold values from 0 to 8191
Outputs:
- gradient: float32 [6, 48, 256, 512], P(None, 'lev', 'lat', 'lon')
Inputs may be any that keep to these rules, and one draw needn't show every extreme that they name: `obs_tile`: the rows of one source device name each tile at most 64 times, and one tile is named exactly 64 times by the rows of every source device.
All inputs are finite; a program needn't handle non-finite values.
Results may differ from a plain program's by a relative error of at most 0.00005.
Values sent between devices are 32-bit elements; how exact they have to be, the bound alone decides.
No kernel may reach another device: no remote copies, remote signals or barrier semaphores. Data moves between devices by JAX's collectives and lax.ppermute only.
A program may use at most 64 MiB of HBM per device.

v0:
```python
import jax
import jax.numpy as jnp
from jax import lax
from jax.sharding import PartitionSpec as P


def extended(value, sides, width, wrap):
    for axis, dim in sides:
        size, length = (lax.axis_size(axis), value.shape[dim])
        up = [(i, (i + 1) % size) for i in range(size if wrap else size - 1)]
        down = [(j, i) for i, j in up]
        last = lax.slice_in_dim(value, length - width, length, axis=dim)
        first = lax.slice_in_dim(value, 0, width, axis=dim)
        before = lax.ppermute(last, axis, up)
        after = lax.ppermute(first, axis, down)
        value = jnp.concatenate([before, value, after], axis=dim)
    return value


def weighted_sum(padded, coeffs, axis, extent):
    summed = coeffs[:, :, 0][:, :, None, None] * lax.slice_in_dim(padded, 0, extent, axis=axis)
    for offset in range(1, coeffs.shape[2]):
        summed = summed + coeffs[:, :, offset][:, :, None, None] * lax.slice_in_dim(
            padded, offset, offset + extent, axis=axis
        )
    return summed


def along_lon(grid_field, coeffs):
    reach = (coeffs.shape[2] - 1) // 2
    padded = extended(grid_field, (("lon", 3),), reach, True)
    return weighted_sum(padded, coeffs, 3, grid_field.shape[3])


def along_lat(grid_field, coeffs):
    reach = (coeffs.shape[2] - 1) // 2
    padded = extended(grid_field, (("lat", 2),), reach, False)
    return weighted_sum(padded, coeffs, 2, grid_field.shape[2])


def vertical_apply(grid_field, matrix):
    levels = grid_field.shape[1]
    own_rows = lax.dynamic_slice_in_dim(matrix, lax.axis_index("lev") * levels, levels, 1)
    return jnp.einsum(
        "vkl,vlyx->vkyx",
        own_rows,
        lax.all_gather(grid_field, "lev", axis=1, tiled=True),
        precision=lax.Precision.HIGHEST,
    )


def observe(grid_field, innovation, inv_variance, obs_tile, obs_cell):
    lon_count = lax.axis_size("lon")
    lat_count = lax.axis_size("lat")
    tile_count = lon_count * lat_count
    row_count = obs_tile.shape[0]
    capacity = 2 * row_count // tile_count
    slot_count = tile_count * capacity
    tile_rows = grid_field.shape[2]
    tile_cols = grid_field.shape[3]
    tile_hot = (obs_tile[:, None] == jnp.arange(tile_count, dtype=jnp.int32)[None, :]).astype(
        jnp.float32
    )
    before = jnp.cumsum(tile_hot, axis=0) - tile_hot
    position = jnp.sum(before * tile_hot, axis=1).astype(jnp.int32)
    slot_index = obs_tile * capacity + position
    slot_hot = (slot_index[:, None] == jnp.arange(slot_count, dtype=jnp.int32)[None, :]).astype(
        jnp.float32
    )
    send_values = jnp.einsum("vkr,rs->vks", innovation, slot_hot, precision=lax.Precision.HIGHEST)
    shifted_cells = (obs_cell + 1).astype(jnp.float32)
    send_cells = (jnp.dot(shifted_cells, slot_hot, precision=lax.Precision.HIGHEST) - 1.0).astype(
        jnp.int32
    )
    got_values, got_cells = (
        lax.all_to_all(send_values, ("lon", "lat"), split_axis=2, concat_axis=2, tiled=True),
        lax.all_to_all(
            send_cells.reshape(1, 1, -1), ("lon", "lat"), split_axis=2, concat_axis=2, tiled=True
        ),
    )
    cell_ids = got_cells.reshape(-1)
    present = cell_ids >= 0
    row_hot = (
        (cell_ids // tile_cols)[None, :] == jnp.arange(tile_rows, dtype=jnp.int32)[:, None]
    ).astype(jnp.float32)
    col_hot = (
        (cell_ids % tile_cols)[:, None] == jnp.arange(tile_cols, dtype=jnp.int32)[None, :]
    ).astype(jnp.float32)
    across = jnp.einsum("vkyx,rx->vkyr", grid_field, col_hot, precision=lax.Precision.HIGHEST)
    picked = jnp.sum(across * row_hot[None, None], axis=2)
    misfit = jnp.where(
        present[None, None, :], (picked - got_values) * inv_variance[:, :, None], 0.0
    )
    weighted = misfit[:, :, None, :] * row_hot[None, None]
    return jnp.einsum("vkyr,rx->vkyx", weighted, col_hot, precision=lax.Precision.HIGHEST)


def local(control, vertical, lon_taps, lat_taps, innovation, inv_variance, obs_tile, obs_cell):
    first = vertical_apply(control, vertical)
    second = along_lon(first, lon_taps)
    third = along_lat(second, lat_taps)
    placed = observe(third, innovation, inv_variance, obs_tile, obs_cell)
    back_lat = along_lat(placed, lat_taps[:, :, ::-1])
    back_lon = along_lon(back_lat, lon_taps[:, :, ::-1])
    return control + vertical_apply(back_lon, jnp.swapaxes(vertical, 1, 2))


def solution(mesh):
    return jax.shard_map(
        local,
        mesh=mesh,
        in_specs=(
            P(None, "lev", "lat", "lon"),
            P(),
            P(None, "lev", None),
            P(None, "lev", None),
            P(None, "lev", ("lon", "lat")),
            P(None, "lev"),
            P(("lon", "lat")),
            P(("lon", "lat")),
        ),
        out_specs=P(None, "lev", "lat", "lon"),
        check_vma=False,
    )
```

profile of v0, /device:TPU:1, one launch (start us, length us, event | category | flops | bytes accessed | tf_op | source)
XLA Modules:
  0.0 338.1 jit_solution(13807171272272996474)
XLA Ops:
  6.6 2.0 copy.738
  9.3 1.1 reduce-window.6
  13.6 1.0 copy.733
  14.6 7.6 %all-to-all-start = ((s32[1,1,1024]{1,0,2:T(1,128)}), s32[1,1,1024]{1,0,2:T(1,128)S(1)}, u32[]{:S(2)}, u32[]{:S(2)}) async-start(s32[1,1,1024]{1,0,2:T(1,128)} %copy.733), calls=%async_computation | async-start | bytes 1048576 | tf_op jit(solution)/shard_map/all_to_all | solution.py:77
  22.2 1.6 fusion.336
  73.9 2.0 reshape.231
  76.6 6.6 %all-to-all-start.1 = ((f32[16,1,1152]{2,1,0:T(1,128)}), f32[16,1,1152]{2,1,0:T(1,128)S(1)}, u32[]{:S(2)}, u32[]{:S(2)}) async-start(f32[16,1,1152]{2,1,0:T(1,128)} %reshape.231), calls=%async_computation.1 | async-start | bytes 147456 | tf_op jit(solution)/shard_map/all_to_all | solution.py:76
  83.5 18.6 %reduce.2 = s32[1024]{0:T(1024)S(1)} reduce(s32[1,1,1024]{1,0,2:T(1,128)S(1)} %all-to-all-done, s32[]{:T(128)} %constant.38.clone.1), dimensions={0,1}, to_apply=%all_to_all.6.reduce_sub_computation | reduce | bytes 8196 | tf_op jit(solution)/shard_map/all_to_all | solution.py:77
  102.7 13.8 %fusion.2 = f32[6,3,64,128]{3,1,2,0:T(4,128)S(1)} fusion(f32[6,48,64,128]{3,2,0,1:T(8,128)} %all-gather.3.cloned.1.call-done, f32[6,48,48]{2,1,0:T(8,128)S(1)} %copy-done, s32[]{:T(128)S(6)} %select_n.28), kind=kOutput, calls=%fused_computation.2 | convolution fusion | flops 84934656 | bytes 10039300 | tf_op jit(solution)/shard_map/vkl,vlyx->vkyx/dot_general | solution.py:44
  117.3 1.4 collective-permute-start
  119.0 1.4 collective-permute-start.1
  120.4 1.4 fusion.317
  123.4 1.3 copy.775
  124.6 28.3 %fusion.106 = f32[6,3,64,128]{3,1,2,0:T(4,128)S(1)} fusion(f32[6,3,64,128]{3,1,2,0:T(4,128)S(1)} %fusion.2, f32[6,3,64,15]{3,1,2,0:T(4,128)} %copy.775, f32[6,3,64,15]{3,1,2,0:T(4,128)S(1)} %copy.741, f32[6,3]{1,0:T(8,128)} %copy.801, f32[6,3]{1,0:T(8,128)} %copy.799, f32[6,3]{1,0:T(8,128)} %copy.797, f32[6,3]{1,0:T(8,128)} %copy.795, f32[6,3]{1,0:T(8,128)} %copy.793, ...), kind=kLoop, calls=%fused_computation.246 | loop fusion | flops 13418496 | bytes 1320120 | tf_op jit(solution)/shard_map/add | solution.py:23
  153.8 3.5 %collective-permute-start.2 = (f32[6,3,15,128]{3,1,2,0:T(4,128)}, f32[6,3,15,128]{3,1,2,0:T(4,128)}, u32[]{:S(2)}, u32[]{:S(2)}) collective-permute-start(f32[6,3,15,128]{3,1,2,0:T(4,128)} %get-tuple-element.7), channel_id=1, source_target_pairs={{0,16},{16,32},{32,48},{1,17},{17,33},{33,49},{2,18},{18,34},{34,5... | collective-permute-start | bytes 414728 | tf_op jit(solution)/shard_map/ppermute | solution.py:14
  157.3 1.5 collective-permute-start.3
  158.8 18.9 %compare_reduce_fusion = pred[1024]{0:T(1024)(128)(4,1)} fusion(s32[1,1,1024]{1,0,2:T(1,128)S(1)} %all-to-all-done), kind=kLoop, calls=%fused_computation.152 | loop fusion | flops 1024 | bytes 5120 | tf_op jit(solution)/shard_map/ge | solution.py:82
  179.0 1.2 reshape.232
  181.1 9.5 %fusion.192 = f32[6,3,64,128]{3,1,2,0:T(4,128)S(1)} fusion(f32[6,3,15,128]{3,1,2,0:T(4,128)} %collective-permute-done.3, f32[6,3,15,128]{3,1,2,0:T(4,128)} %collective-permute-done.2, f32[6,3,64,128]{3,1,2,0:T(4,128)S(1)} %fusion.106, f32[6,3]{1,0:T(8,128)} %copy.859, f32[6,3]{1,0:T(8,128)} %copy.857, f32[6,3]{1,0:T(8,128)} %copy.855, f32[6,3]{1,0:T(8,128)} %copy.853, ...), kind=kLoop, calls=%fused_computation.332 | loop fusion | flops 13418496 | bytes 1458360 | tf_op jit(solution)/shard_map/add | solution.py:23
  190.9 3.2 multiply_reduce_fusion
  195.0 2.5 fusion.4
  197.6 4.0 %collective-permute-start.4 = (f32[6,3,15,128]{3,1,2,0:T(4,128)S(1)}, f32[6,3,15,128]{3,1,2,0:T(4,128)S(1)}, u32[]{:S(2)}, u32[]{:S(2)}) collective-permute-start(f32[6,3,15,128]{3,1,2,0:T(4,128)S(1)} %copy.893), channel_id=1, source_target_pairs={{0,16},{16,32},{32,48},{1,17},{17,33},{33,49},{2,18},{18,34},{34,5... | collective-permute-start | bytes 414728 | tf_op jit(solution)/shard_map/ppermute | solution.py:14
  201.7 1.3 collective-permute-start.5
  203.0 1.1 collective-permute-done.4
  204.6 3.3 collective-permute-done.5
  208.3 5.2 %fusion.277 = f32[6,3,64,128]{3,1,2,0:T(4,128)S(1)} fusion(f32[6,3,79,128]{3,1,2,0:T(4,128)S(1)} %constant_dynamic-update-slice_fusion.1, f32[6,3,79,128]{3,1,2,0:T(4,128)S(1)} %get-tuple-element.11, f32[6,3]{1,0:T(8,128)S(1)} %copy-done.68, f32[6,3]{1,0:T(8,128)S(1)} %copy-done.67, f32[6,3]{1,0:T(8,128)S(1)} %copy-done.56, f32[6,3]{1,0:T(8,128)S(1)} %copy-done.55, ...), kind=kLoop, calls=%fused_computation.420 | loop fusion | flops 8994816 | bytes 18876600 | tf_op jit(solution)/shard_map/add | solution.py:23
  214.6 1.5 collective-permute-start.6
  216.4 1.6 collective-permute-start.7
  217.9 2.0 collective-permute-done.6
  221.3 24.6 %fusion.20 = f32[6,3,64,128]{3,1,2,0:T(4,128)S(1)} fusion(f32[6,3,64,128]{3,1,2,0:T(4,128)S(1)} %fusion.277, f32[6,3,64,15]{3,1,2,0:T(4,128)S(1)} %copy.872, f32[6,3,64,15]{3,1,2,0:T(4,128)S(1)} %copy.870, f32[6,3]{1,0:T(8,128)S(1)} %copy-done.37, f32[6,3]{1,0:T(8,128)S(1)} %copy-done.36, f32[6,3]{1,0:T(8,128)S(1)} %copy-done.25, f32[6,3]{1,0:T(8,128)S(1)} %copy-done.24, ...), kind=kLoop, calls=%fused_computation.160 | loop fusion | flops 13418496 | bytes 1320120 | tf_op jit(solution)/shard_map/add | solution.py:23
  246.9 69.5 %all-gather.5.cloned.1.call-done = f32[6,48,64,128]{3,2,0,1:T(8,128)} async-done(((f32[6,3,64,128]{3,2,0,1:T(8,128)}), f32[6,48,64,128]{3,2,0,1:T(8,128)}) %all-gather.5.cloned.1.call-update) | async-done | bytes 9437200 | tf_op jit(solution)/shard_map/all_gather | solution.py:47
  316.4 13.5 %fusion = f32[6,3,64,128]{3,1,2,0:T(4,128)S(1)} fusion(f32[6,48,64,128]{3,2,0,1:T(8,128)} %all-gather.5.cloned.1.call-done, f32[6,48,48]{2,1,0:T(8,128)S(1)} %copy-done, s32[]{:T(128)S(6)} %select_n.28), kind=kOutput, calls=%fused_computation | convolution fusion | flops 84934656 | bytes 10082308 | tf_op jit(solution)/shard_map/vkl,vlyx->vkyx/dot_general | solution.py:44
  (320 shorter events, 66.8 us)
Async XLA Ops:
  6.5 96.2 %copy-start = (f32[6,48,48]{2,1,0:T(8,128)S(1)}, f32[6,48,48]{2,1,0:T(8,128)}, u32[]{:S(2)}) copy-start(f32[6,48,48]{2,1,0:T(8,128)} %param.9) | copy-start | bytes 165892
  6.5 31.1 %copy-start.1 = (f32[6,3,31]{2,1,0:T(4,128)S(1)}, f32[6,3,31]{2,1,0:T(4,128)}, u32[]{:S(2)}) copy-start(f32[6,3,31]{2,1,0:T(4,128)} %param.10) | copy-start | bytes 6700
  6.5 40.7 %copy-start.2 = (f32[6,3,31]{2,1,0:T(4,128)S(1)}, f32[6,3,31]{2,1,0:T(4,128)}, u32[]{:S(2)}) copy-start(f32[6,3,31]{2,1,0:T(4,128)} %param.11) | copy-start | bytes 6700
  6.5 51.2 %copy-start.72 = (f32[6,3,512]{2,1,0:T(4,128)S(1)}, f32[6,3,512]{2,1,0:T(4,128)}, u32[]{:S(2)}) copy-start(f32[6,3,512]{2,1,0:T(4,128)} %param.12) | copy-start | bytes 110596
  6.5 96.2 %all-gather.3.cloned.1.call-start = ((), (), s32[]{:S(2)}) async-start(), calls=%async_computation.2 | async-start | bytes 10027008 | tf_op jit(solution)/shard_map/all_gather | solution.py:47
  14.6 62.0 %all-to-all-start = ((s32[1,1,1024]{1,0,2:T(1,128)}), s32[1,1,1024]{1,0,2:T(1,128)S(1)}, u32[]{:S(2)}, u32[]{:S(2)}) async-start(s32[1,1,1024]{1,0,2:T(1,128)} %copy.733), calls=%async_computation | async-start | bytes 1048576 | tf_op jit(solution)/shard_map/all_to_all | solution.py:77
  24.0 100.6 %copy-start.5 = (f32[6,3]{1,0:T(8,128)}, f32[6,3]{1,0:T(8,128)S(1)}, u32[]{:S(2)}) copy-start(f32[6,3]{1,0:T(8,128)S(1)} %copy.729) | copy-start | bytes 220
  24.2 100.4 %copy-start.7 = (f32[6,3]{1,0:T(8,128)}, f32[6,3]{1,0:T(8,128)S(1)}, u32[]{:S(2)}) copy-start(f32[6,3]{1,0:T(8,128)S(1)} %copy.761) | copy-start | bytes 220
  47.4 28.5 %copy-start.71 = (f32[6,3]{0,1:T(4,128)S(1)}, f32[6,3]{0,1:T(4,128)}, u32[]{:S(2)}) copy-start(f32[6,3]{0,1:T(4,128)} %param.13) | copy-start | bytes 220
  76.6 101.1 %all-to-all-start.1 = ((f32[16,1,1152]{2,1,0:T(1,128)}), f32[16,1,1152]{2,1,0:T(1,128)S(1)}, u32[]{:S(2)}, u32[]{:S(2)}) async-start(f32[16,1,1152]{2,1,0:T(1,128)} %reshape.231), calls=%async_computation.1 | async-start | bytes 147456 | tf_op jit(solution)/shard_map/all_to_all | solution.py:76
  83.2 233.1 %all-gather.5.cloned.1.call-start = ((), (), s32[]{:S(2)}) async-start(), calls=%async_computation.3 | async-start | bytes 10027008 | tf_op jit(solution)/shard_map/all_gather | solution.py:47
  117.3 5.3 %collective-permute-start = (f32[6,3,64,15]{2,3,1,0:T(8,128)S(1)}, f32[6,3,64,15]{2,3,1,0:T(8,128)S(1)}, u32[]{:S(2)}, u32[]{:S(2)}) collective-permute-start(f32[6,3,64,15]{2,3,1,0:T(8,128)S(1)} %copy.740), channel_id=1, source_target_pairs={{0,64},{64,128},{128,192},{192,0},{1,65},{65,129},{129,193},{193,1... | collective-permute-start | bytes 207368 | tf_op jit(solution)/shard_map/ppermute | solution.py:14
  119.0 4.4 %collective-permute-start.1 = (f32[6,3,64,15]{2,3,1,0:T(8,128)S(1)}, f32[6,3,64,15]{2,3,1,0:T(8,128)S(1)}, u32[]{:S(2)}, u32[]{:S(2)}) collective-permute-start(f32[6,3,64,15]{2,3,1,0:T(8,128)S(1)} %copy.774), channel_id=1, source_target_pairs={{64,0},{128,64},{192,128},{0,192},{65,1},{129,65},{193,129},{1,193... | collective-permute-start | bytes 207368 | tf_op jit(solution)/shard_map/ppermute | solution.py:15
  153.8 27.4 %collective-permute-start.2 = (f32[6,3,15,128]{3,1,2,0:T(4,128)}, f32[6,3,15,128]{3,1,2,0:T(4,128)}, u32[]{:S(2)}, u32[]{:S(2)}) collective-permute-start(f32[6,3,15,128]{3,1,2,0:T(4,128)} %get-tuple-element.7), channel_id=1, source_target_pairs={{0,16},{16,32},{32,48},{1,17},{17,33},{33,49},{2,18},{18,34},{34,5... | collective-permute-start | bytes 414728 | tf_op jit(solution)/shard_map/ppermute | solution.py:14
  157.3 23.8 %collective-permute-start.3 = (f32[6,3,15,128]{3,1,2,0:T(4,128)}, f32[6,3,15,128]{3,1,2,0:T(4,128)}, u32[]{:S(2)}, u32[]{:S(2)}) collective-permute-start(f32[6,3,15,128]{3,1,2,0:T(4,128)} %get-tuple-element.8), channel_id=1, source_target_pairs={{16,0},{32,16},{48,32},{17,1},{33,17},{49,33},{18,2},{34,18},{50,3... | collective-permute-start | bytes 414728 | tf_op jit(solution)/shard_map/ppermute | solution.py:15
  190.6 17.4 %copy-start.38 = (f32[6,3]{1,0:T(8,128)S(1)}, f32[6,3]{1,0:T(8,128)}, u32[]{:S(2)}) copy-start(f32[6,3]{1,0:T(8,128)} %copy.731) | copy-start | bytes 220
  190.6 17.4 %copy-start.39 = (f32[6,3]{1,0:T(8,128)S(1)}, f32[6,3]{1,0:T(8,128)}, u32[]{:S(2)}) copy-start(f32[6,3]{1,0:T(8,128)} %copy.821) | copy-start | bytes 220
  190.7 17.4 %copy-start.40 = (f32[6,3]{1,0:T(8,128)S(1)}, f32[6,3]{1,0:T(8,128)}, u32[]{:S(2)}) copy-start(f32[6,3]{1,0:T(8,128)} %copy.823) | copy-start | bytes 220
  190.7 17.4 %copy-start.41 = (f32[6,3]{1,0:T(8,128)S(1)}, f32[6,3]{1,0:T(8,128)}, u32[]{:S(2)}) copy-start(f32[6,3]{1,0:T(8,128)} %copy.825) | copy-start | bytes 220
  190.7 17.4 %copy-start.42 = (f32[6,3]{1,0:T(8,128)S(1)}, f32[6,3]{1,0:T(8,128)}, u32[]{:S(2)}) copy-start(f32[6,3]{1,0:T(8,128)} %copy.827) | copy-start | bytes 220
  190.7 17.4 %copy-start.43 = (f32[6,3]{1,0:T(8,128)S(1)}, f32[6,3]{1,0:T(8,128)}, u32[]{:S(2)}) copy-start(f32[6,3]{1,0:T(8,128)} %copy.829) | copy-start | bytes 220
  190.7 17.4 %copy-start.44 = (f32[6,3]{1,0:T(8,128)S(1)}, f32[6,3]{1,0:T(8,128)}, u32[]{:S(2)}) copy-start(f32[6,3]{1,0:T(8,128)} %copy.831) | copy-start | bytes 220
  190.7 17.4 %copy-start.45 = (f32[6,3]{1,0:T(8,128)S(1)}, f32[6,3]{1,0:T(8,128)}, u32[]{:S(2)}) copy-start(f32[6,3]{1,0:T(8,128)} %copy.833) | copy-start | bytes 220
  190.7 17.4 %copy-start.46 = (f32[6,3]{1,0:T(8,128)S(1)}, f32[6,3]{1,0:T(8,128)}, u32[]{:S(2)}) copy-start(f32[6,3]{1,0:T(8,128)} %copy.835) | copy-start | bytes 220
  190.7 17.4 %copy-start.47 = (f32[6,3]{1,0:T(8,128)S(1)}, f32[6,3]{1,0:T(8,128)}, u32[]{:S(2)}) copy-start(f32[6,3]{1,0:T(8,128)} %copy.837) | copy-start | bytes 220
  190.7 17.4 %copy-start.48 = (f32[6,3]{1,0:T(8,128)S(1)}, f32[6,3]{1,0:T(8,128)}, u32[]{:S(2)}) copy-start(f32[6,3]{1,0:T(8,128)} %copy.839) | copy-start | bytes 220
  190.7 17.4 %copy-start.49 = (f32[6,3]{1,0:T(8,128)S(1)}, f32[6,3]{1,0:T(8,128)}, u32[]{:S(2)}) copy-start(f32[6,3]{1,0:T(8,128)} %copy.841) | copy-start | bytes 220
  197.6 6.5 %collective-permute-start.4 = (f32[6,3,15,128]{3,1,2,0:T(4,128)S(1)}, f32[6,3,15,128]{3,1,2,0:T(4,128)S(1)}, u32[]{:S(2)}, u32[]{:S(2)}) collective-permute-start(f32[6,3,15,128]{3,1,2,0:T(4,128)S(1)} %copy.893), channel_id=1, source_target_pairs={{0,16},{16,32},{32,48},{1,17},{17,33},{33,49},{2,18},{18,34},{34,5... | collective-permute-start | bytes 414728 | tf_op jit(solution)/shard_map/ppermute | solution.py:14
  201.7 6.3 %collective-permute-start.5 = (f32[6,3,15,128]{3,1,2,0:T(4,128)S(1)}, f32[6,3,15,128]{3,1,2,0:T(4,128)S(1)}, u32[]{:S(2)}, u32[]{:S(2)}) collective-permute-start(f32[6,3,15,128]{3,1,2,0:T(4,128)S(1)} %copy.892), channel_id=1, source_target_pairs={{16,0},{32,16},{48,32},{17,1},{33,17},{49,33},{18,2},{34,18},{50,3... | collective-permute-start | bytes 414728 | tf_op jit(solution)/shard_map/ppermute | solution.py:15
  214.6 5.3 %collective-permute-start.6 = (f32[6,3,64,15]{2,3,1,0:T(8,128)S(1)}, f32[6,3,64,15]{2,3,1,0:T(8,128)S(1)}, u32[]{:S(2)}, u32[]{:S(2)}) collective-permute-start(f32[6,3,64,15]{2,3,1,0:T(8,128)S(1)} %copy.869), channel_id=1, source_target_pairs={{0,64},{64,128},{128,192},{192,0},{1,65},{65,129},{129,193},{193,1... | collective-permute-start | bytes 207368 | tf_op jit(solution)/shard_map/ppermute | solution.py:14
  216.4 4.3 %collective-permute-start.7 = (f32[6,3,64,15]{2,3,1,0:T(8,128)S(1)}, f32[6,3,64,15]{2,3,1,0:T(8,128)S(1)}, u32[]{:S(2)}, u32[]{:S(2)}) collective-permute-start(f32[6,3,64,15]{2,3,1,0:T(8,128)S(1)} %copy.871), channel_id=1, source_target_pairs={{64,0},{128,64},{192,128},{0,192},{65,1},{129,65},{193,129},{1,193... | collective-permute-start | bytes 207368 | tf_op jit(solution)/shard_map/ppermute | solution.py:15
  246.9 83.0 %copy-start.3 = (f32[6,3,64,128]{3,2,1,0:T(8,128)S(1)}, f32[6,3,64,128]{3,2,1,0:T(8,128)}, u32[]{:S(2)}) copy-start(f32[6,3,64,128]{3,2,1,0:T(8,128)} %param.8) | copy-start | bytes 1769476
  (53 other events, 613.4 us)
Sparse Core Ops, SparseCore 0:
  9.2 65.0 all-gather.2
  247.0 69.3 all-gather.4
where the time goes:
time: 344 us; the launch traced here: 338 us
  other arithmetic  114 us (33%)
  waiting for transfers between devices  77.5 us (23%)
  local copies, waits for them, and re-layouts  66.3 us (19%)
  matrix products  34.7 us (10%)
  starting transfers between devices  30.7 us (9%)
  between operations  15.2 us (4%)
    all_gather x2, waiting for transfers between devices, vertical_apply(): lax.all_gather(grid_field, 'lev', axis=1, tiled=True)  69.5 us
    add x4, other arithmetic, weighted_sum(): summed + coeffs[:, :, offset][:, :, None, None] * lax.slice_in_dim(padded...  67.7 us
    mul x58, local copies, waits for them, and re-layouts, weighted_sum(): coeffs[:, :, offset][:, :, None, None]  38.7 us
    dot_general x2, matrix products, vertical_apply(): jnp.einsum('vkl,vlyx->vkyx', own_rows, lax.all_gather(grid_field, 'lev',...  27.2 us
    ge x1, other arithmetic, observe(): present = cell_ids >= 0  18.9 us
    all_to_all x1, other arithmetic, observe(): lax.all_to_all(send_cells.reshape(1, 1, -1), ('lon', 'lat'), split_axis=2...  18.6 us
    ppermute x4, starting transfers between devices, extended(): before = lax.ppermute(last, axis, up)  10.4 us
    all_to_all x1, starting transfers between devices, observe(): lax.all_to_all(send_cells.reshape(1, 1, -1), ('lon', 'lat'), split_axis=2...  7.58 us
  transfers between devices with their start and end apart: 12, of which 7 were waited for; matrix products, arithmetic and copies ran while one was open for 44% of the time, Pallas kernels for 0%

commit v1 on v0

v1 whole, which is shorter than its diff:
```python
import functools

import jax
import jax.numpy as jnp
from jax import lax
from jax.experimental import pallas as pl
from jax.experimental.pallas import tpu as pltpu
from jax.sharding import PartitionSpec as P

F32, BF16, I32 = jnp.float32, jnp.bfloat16, jnp.int32
ROWS, COLS = 64, 128
TAPS = 31
STRIP = 16
LEVELS = 48
RINGS = 8
OWN = 6
SLOTS = 64
TILES = 16
VMEM = pl.BlockSpec(memory_space=pltpu.VMEM)
SMEM = pl.BlockSpec(memory_space=pltpu.SMEM)


def kernel_call(body, outs, ins, scratch=(), smem=(), flops=0, limit=40):
    moved = sum(a.size * a.dtype.itemsize for a in ins)
    moved += sum(o.size * o.dtype.itemsize for o in outs)
    return pl.pallas_call(
        body,
        out_shape=list(outs),
        in_specs=[SMEM if i in smem else VMEM for i in range(len(ins))],
        out_specs=[VMEM] * len(outs),
        scratch_shapes=list(scratch),
        compiler_params=pltpu.CompilerParams(vmem_limit_bytes=limit * 2**20),
        cost_estimate=pl.CostEstimate(flops=flops, bytes_accessed=moved, transcendentals=0),
    )(*ins)


def shape(*dims, dtype=F32):
    return jax.ShapeDtypeStruct(dims, dtype)


def split(value):
    high = value.astype(BF16)
    return high, (value - high.astype(F32)).astype(BF16)


def mm(a, b):
    return jnp.dot(a, b, preferred_element_type=F32)


def mm_nt(a, b):
    return lax.dot_general(a, b, (((1,), (1,)), ((), ())), preferred_element_type=F32)


def arrange_body(nv, core, control, mate, out):
    c = core[0]
    for v in range(nv):
        for l in range(3):
            out[:, v * 3 + l] = control[c * nv + v, l].reshape(RINGS, 8, COLS)
            out[:, nv * 3 + v * 3 + l] = mate[v * 3 + l].reshape(RINGS, 8, COLS)


def arrange(core, control, mate):
    nv = control.shape[0] // 2
    return kernel_call(
        functools.partial(arrange_body, nv),
        [shape(RINGS, 6 * nv, 8, COLS)],
        [core, control, mate],
        smem=(0,),
    )[0]


def rows_of(v, start, count):
    return pl.ds(v * LEVELS * 8 + start, count)


def mixed(matrix, held, v):
    at = [pl.ds(v * LEVELS * 8 + s, LEVELS, stride=8) for s in range(8)]
    columns = jnp.concatenate([held[a, :] for a in at], axis=1)
    result = jnp.dot(
        matrix[v], columns, precision=lax.Precision.HIGHEST, preferred_element_type=F32
    )
    for s in range(8):
        held[at[s], :] = result[:, s * COLS : (s + 1) * COLS]


def mix_body(nv, got, matrix, out, held):
    for v in range(nv):
        for s in range(RINGS):
            for t in range(2):
                first = t * 3 * nv + v * 3
                held[rows_of(v, (s * 2 + t) * 24, 24), :] = got[s, first : first + 3].reshape(24, COLS)
        mixed(matrix, held, v)
        for s in range(RINGS):
            out[s, v * OWN : (v + 1) * OWN] = held[rows_of(v, s * 48, 48), :].reshape(OWN, 8, COLS)


def unmix_body(nv, got, matrix, control, out, held):
    for v in range(nv):
        for s in range(RINGS):
            held[rows_of(v, s * 48, 48), :] = got[s, v * OWN : (v + 1) * OWN].reshape(48, COLS)
        mixed(matrix, held, v)
        for s in range(RINGS):
            for t in range(2):
                first = t * 3 * nv + v * 3
                part = held[rows_of(v, (s * 2 + t) * 24, 24), :].reshape(3, 8, COLS)
                out[s, first : first + 3] = part + control[s, first : first + 3]


def mix(got, matrix):
    nv = matrix.shape[0]
    return kernel_call(
        functools.partial(mix_body, nv),
        [shape(*got.shape)],
        [got, matrix],
        scratch=[pltpu.VMEM((nv * LEVELS * 8, COLS), F32)],
        flops=2 * nv * LEVELS * LEVELS * 1024 * 6,
    )[0]


def unmix(got, matrix, control):
    nv = matrix.shape[0]
    return kernel_call(
        functools.partial(unmix_body, nv),
        [shape(*got.shape)],
        [got, matrix, control],
        scratch=[pltpu.VMEM((nv * LEVELS * 8, COLS), F32)],
        flops=2 * nv * LEVELS * LEVELS * 1024 * 6,
    )[0]


def bands_body(planes, taps, lat_high, lat_low, lon_high, lon_low):
    def one(p, carry):
        for flip in range(2):
            lat = jnp.broadcast_to(taps[flip, p, :, 0:128], (ROWS, 128))
            lat = pltpu.roll(lat, 128 - 15, 1, stride=1, stride_axis=0)
            lat_high[flip, p], lat_low[flip, p] = split(lat)
            lon = jnp.broadcast_to(taps[flip, p, :, 128:384], (COLS, 256))
            lon = pltpu.roll(lon, 256 - 15, 1, stride=1, stride_axis=0)
            lon_high[flip, p], lon_low[flip, p] = split(lon)
        return carry

    lax.fori_loop(0, planes, one, 0)


def bands(lon_taps, lat_taps):
    planes = lon_taps.shape[0]
    both = []
    for lon, lat in ((lon_taps, lat_taps), (lon_taps[:, ::-1], lat_taps[:, ::-1])):
        lat = jnp.pad(lat, ((0, 0), (0, 128 - TAPS)))
        lon = jnp.pad(lon, ((0, 0), (0, 256 - TAPS)))
        both.append(jnp.concatenate([lat, lon], axis=1))
    taps = jnp.stack(both)[:, :, None, :]
    return kernel_call(
        functools.partial(bands_body, planes),
        [shape(2, planes, ROWS, 128, dtype=BF16)] * 2 + [shape(2, planes, COLS, 256, dtype=BF16)] * 2,
        [taps],
        flops=planes * 200000,
    )


def lat_filter(p, rows, before, after, high, low):
    extended = jnp.concatenate(
        [rows[:, p].reshape(ROWS, COLS), after[:, p].reshape(STRIP, COLS)]
        + [jnp.zeros((32, COLS), F32), before[:, p].reshape(STRIP, COLS)],
        axis=0,
    )
    e_high, e_low = split(extended)
    return mm(high[0, p], e_high) + (mm(high[0, p], e_low) + mm(low[0, p], e_high))


def lon_filter(p, l, field, left, right, high, low):
    lane = lax.broadcasted_iota(I32, (ROWS, COLS), 1)
    left = pltpu.roll(left, (COLS - STRIP - STRIP * l) % COLS, 1)
    right = pltpu.roll(right, (COLS - STRIP * l) % COLS, 1)
    halo = jnp.where(lane >= COLS - STRIP, left, jnp.where(lane < STRIP, right, 0.0))
    x_high, x_low = split(jnp.concatenate([field, halo], axis=1))
    return mm_nt(x_high, high[0, p]) + (mm_nt(x_low, high[0, p]) + mm_nt(x_high, low[0, p]))


def packed(fields):
    lane = lax.broadcasted_iota(I32, (ROWS, COLS), 1) // STRIP
    last = jnp.zeros((ROWS, COLS), F32)
    first = jnp.zeros((ROWS, COLS), F32)
    for l, field in enumerate(fields):
        last = jnp.where(lane == l, pltpu.roll(field, STRIP * (l + 1) % COLS, 1), last)
        first = jnp.where(lane == l, pltpu.roll(field, STRIP * l, 1) if l else field, first)
    return last, first


def lat_body(nv, rows, before, after, high, low, out, last, first):
    def one(v, carry):
        fields = [lat_filter(v * OWN + l, rows, before, after, high, low) for l in range(OWN)]
        for l in range(OWN):
            out[v * OWN + l] = fields[l]
        last[v], first[v] = packed(fields)
        return carry

    lax.fori_loop(0, nv, one, 0)


def back_lat_body(nv, rows, before, after, high, low, out):
    def one(v, carry):
        for l in range(OWN):
            p = v * OWN + l
            out[:, p] = lat_filter(p, rows, before, after, high, low).reshape(RINGS, 8, COLS)
        return carry

    lax.fori_loop(0, nv, one, 0)


def back_lon_body(nv, field, left, right, high, low, out):
    def one(v, carry):
        for l in range(OWN):
            p = v * OWN + l
            value = lon_filter(p, l, field[p], left[v], right[v], high, low)
            out[:, p] = value.reshape(RINGS, 8, COLS)
        return carry

    lax.fori_loop(0, nv, one, 0)


def observe_body(
    nv, field, left, right, high, low, values, weight, row_hot, row_hot16, col_hot, col_hot2,
    out, last, first, parts, picked, misfit_high, misfit_low,
):
    def filtered(v, carry):
        for l in range(OWN):
            p = v * OWN + l
            third = lon_filter(p, l, field[p], left[v], right[v], high, low)
            t_high, t_low = split(third)
            parts[p] = jnp.concatenate([t_high, t_low], axis=1)
        return carry

    lax.fori_loop(0, nv, filtered, 0)

    def gathered(v, carry):
        for l in range(OWN):
            p = v * OWN + l
            across = mm(parts[p], col_hot2[...])
            found = jnp.sum(across * row_hot[...], axis=0, keepdims=True)
            misfit = (found - values[p]) * weight[p]
            m_high, m_low = split(misfit)
            misfit_high[p] = m_high.astype(F32)
            misfit_low[p] = m_low.astype(F32)
        return carry

    lax.fori_loop(0, nv, gathered, 0)

    def scattered(v, carry):
        fields = []
        for l in range(OWN):
            p = v * OWN + l
            w_high = (row_hot[...] * misfit_high[p]).astype(BF16)
            w_low = (row_hot[...] * misfit_low[p]).astype(BF16)
            both = mm_nt(jnp.concatenate([w_high, w_low], axis=0), col_hot[...])
            fields.append(both[:ROWS] + both[ROWS:])
            out[p] = fields[-1]
        last[v], first[v] = packed(fields)
        return carry

    lax.fori_loop(0, nv, scattered, 0)


def route_body(innovation, tile, cell, out):
    count = tile.shape[1]
    hot = (lax.broadcasted_iota(I32, (TILES, count), 0) == tile[...]).astype(F32)
    earlier = lax.broadcasted_iota(I32, (count, count), 0) < lax.broadcasted_iota(I32, (count, count), 1)
    before = mm(hot.astype(BF16), earlier.astype(F32).astype(BF16))
    place = jnp.sum(before * hot, axis=0, keepdims=True).astype(I32)
    slot = tile[...] * SLOTS + place
    slot_hot = (lax.broadcasted_iota(I32, (TILES * SLOTS, count), 0) == slot).astype(F32).astype(BF16)
    sent = jnp.concatenate(
        [innovation[...], (cell[...] + 1).astype(F32), jnp.zeros((5, count), F32)], axis=0
    )
    high, rest = split(sent)
    remainder = sent - high.astype(F32)
    low = (remainder - rest.astype(F32)).astype(BF16)
    all_parts = mm_nt(jnp.concatenate([high, rest, low], axis=0), slot_hot)
    full = all_parts[0:24] + (all_parts[24:48] + all_parts[48:72])
    lane = lax.broadcasted_iota(I32, (8, COLS), 1)
    for e in range(TILES // 2):
        at = slice(e * COLS, (e + 1) * COLS)
        a, b, c = full[0:8, at], full[8:16, at], full[16:24, at]
        a2, b2, c2 = [pltpu.roll(x, SLOTS, 1) for x in (a, b, c)]
        out[2 * e, 0:8] = jnp.where(lane < SLOTS, a, b2)
        out[2 * e, 8:16] = jnp.where(lane < SLOTS, c, 0.0)
        out[2 * e + 1, 0:8] = jnp.where(lane < SLOTS, a2, b)
        out[2 * e + 1, 8:16] = jnp.where(lane < SLOTS, c2, 0.0)


def arrived_body(got, values, row_hot, row_hot16, col_hot, col_hot2):
    lane = lax.broadcasted_iota(I32, (8, COLS), 1)
    full = []
    for e in range(TILES // 2):
        a, b = got[2 * e, 0:8], got[2 * e + 1, 0:8]
        c, d = got[2 * e, 8:16], got[2 * e + 1, 8:16]
        low = lane < SLOTS
        full.append(
            jnp.concatenate(
                [
                    jnp.where(low, a, pltpu.roll(b, SLOTS, 1)),
                    jnp.where(low, pltpu.roll(a, SLOTS, 1), b),
                    jnp.where(low, c, pltpu.roll(d, SLOTS, 1)),
                ],
                axis=0,
            )
        )
    full = jnp.concatenate(full, axis=1)
    for p in range(18):
        values[p] = full[p : p + 1]
    cell = full[18:19].astype(I32) - 1
    count = cell.shape[1]
    rows = (lax.broadcasted_iota(I32, (ROWS, count), 0) == (cell >> 7)).astype(F32)
    row_hot[...] = rows
    row_hot16[...] = rows.astype(BF16)
    cols = (lax.broadcasted_iota(I32, (COLS, count), 0) == (cell & 127)).astype(F32).astype(BF16)
    col_hot[...] = cols
    col_hot2[...] = jnp.concatenate([cols, cols], axis=0)


def neighbours(axis, wrap):
    size = lax.axis_size(axis)
    up = [(i, (i + 1) % size) for i in range(size if wrap else size - 1)]
    return up, [(j, i) for i, j in up]


def exchanged(last, first, axis, wrap):
    up, down = neighbours(axis, wrap)
    return lax.ppermute(last, axis, up), lax.ppermute(first, axis, down)


def with_mate(value):
    pairs = [(i, i ^ 1) for i in range(lax.axis_size("lev"))]
    return lax.ppermute(value, "lev", pairs)


def over_rings(value):
    size = lax.axis_size("lev")
    groups = [list(range(0, size, 2)), list(range(1, size, 2))]
    return lax.all_to_all(value, "lev", 0, 0, tiled=True, axis_index_groups=groups)


def local(control, vertical, lon_taps, lat_taps, innovation, inv_variance, obs_tile, obs_cell):
    core = lax.axis_index("lev") % 2
    core_ref = core.astype(I32).reshape(1)
    rows = obs_tile.shape[0]

    def half(value, which):
        return lax.dynamic_slice_in_dim(value, which * 3, 3, 0)

    small = jnp.concatenate(
        [innovation, lon_taps, lat_taps, inv_variance[:, :, None]], axis=2
    )
    mate_control = with_mate(half(control, 1 - core).reshape(9, ROWS, COLS))
    columns = over_rings(arrange(core_ref, control, mate_control))

    mate_small = with_mate(half(small, 1 - core))
    kept = half(small, core)
    natural = jnp.where(
        core == 0,
        jnp.concatenate([kept, mate_small], axis=1),
        jnp.concatenate([mate_small, kept], axis=1),
    ).reshape(18, -1)
    values = natural[:, :rows]
    lon18 = natural[:, rows : rows + TAPS]
    lat18 = natural[:, rows + TAPS : rows + 2 * TAPS]
    weight = natural[:, rows + 2 * TAPS]
    lat_high, lat_low, lon_high, lon_low = bands(lon18, lat18)

    matrix = half(vertical, core).reshape(3, LEVELS, RINGS, 2, 3)
    matrix = jnp.where(core == 0, matrix, matrix[:, :, :, ::-1]).reshape(3, LEVELS, LEVELS)
    flipped = jnp.swapaxes(matrix, 1, 2)

    routed = kernel_call(
        route_body,
        [shape(TILES, 16, COLS)],
        [values, obs_tile.reshape(1, -1), obs_cell.reshape(1, -1)],
        flops=2 * 72 * 1024 * rows,
    )[0]
    got_rows = lax.all_to_all(routed, ("lon", "lat"), 0, 0, tiled=True)
    slots = TILES * SLOTS
    obs, row_hot, row_hot16, col_hot, col_hot2 = kernel_call(
        arrived_body,
        [
            shape(18, 1, slots),
            shape(ROWS, slots),
            shape(ROWS, slots, dtype=BF16),
            shape(COLS, slots, dtype=BF16),
            shape(2 * COLS, slots, dtype=BF16),
        ],
        [got_rows],
        flops=1000000,
    )

    first = over_rings(mix(columns, matrix))
    nv = 3
    planes = nv * OWN
    before, after = exchanged(first[6:8], first[0:2], "lat", False)
    field_shape = shape(planes, ROWS, COLS)
    pack_shape = shape(nv, ROWS, COLS)
    lat_flops = 2 * 3 * planes * ROWS * 128 * COLS
    field, last, lead = kernel_call(
        functools.partial(lat_body, nv),
        [field_shape, pack_shape, pack_shape],
        [first, before, after, lat_high[0:1], lat_low[0:1]],
        flops=lat_flops,
    )
    left, right = exchanged(last, lead, "lon", True)
    placed, last, lead = kernel_call(
        functools.partial(observe_body, nv),
        [field_shape, pack_shape, pack_shape],
        [field, left, right, lon_high[0:1], lon_low[0:1], obs, weight, row_hot, row_hot16, col_hot, col_hot2],
        scratch=[
            pltpu.VMEM((planes, ROWS, 2 * COLS), BF16),
            pltpu.VMEM((planes, 1, slots), F32),
            pltpu.VMEM((planes, 1, slots), F32),
            pltpu.VMEM((planes, 1, slots), F32),
        ],
        smem=(6,),
        flops=2 * planes * ROWS * slots * 256 * 2,
    )
    left, right = exchanged(last, lead, "lon", True)
    back = kernel_call(
        functools.partial(back_lon_body, nv),
        [shape(RINGS, planes, 8, COLS)],
        [placed, left, right, lon_high[1:2], lon_low[1:2]],
        flops=2 * lat_flops,
    )[0]
    before, after = exchanged(back[6:8], back[0:2], "lat", False)
    back = kernel_call(
        functools.partial(back_lat_body, nv),
        [shape(RINGS, planes, 8, COLS)],
        [back, before, after, lat_high[1:2], lat_low[1:2]],
        flops=lat_flops,
    )[0]
    result = over_rings(unmix(over_rings(back), flipped, columns))

    mine, other = result[:, :9], with_mate(result[:, 9:])
    return kernel_call(
        finish_body,
        [shape(6, 3, ROWS, COLS)],
        [core_ref, mine, other],
        smem=(0,),
    )[0]


def finish_body(core, mine, other, out):
    c = core[0]
    for v in range(3):
        for l in range(3):
            out[c * 3 + v, l] = mine[:, v * 3 + l].reshape(ROWS, COLS)
            out[(1 - c) * 3 + v, l] = other[:, v * 3 + l].reshape(ROWS, COLS)


def solution(mesh):
    return jax.shard_map(
        local,
        mesh=mesh,
        in_specs=(
            P(None, "lev", "lat", "lon"),
            P(),
            P(None, "lev", None),
            P(None, "lev", None),
            P(None, "lev", ("lon", "lat")),
            P(None, "lev"),
            P(("lon", "lat")),
            P(("lon", "lat")),
        ),
        out_specs=P(None, "lev", "lat", "lon"),
        check_vma=False,
    )
```

time: 344 us -> 154 us (0.45); the launches traced: 338 us -> 153 us
  other arithmetic: 114 us -> 0.15 us
  local copies, waits for them, and re-layouts: 66.3 us -> 13.5 us
  matrix products: 34.7 us -> 0 us
  waiting for transfers between devices: 77.5 us -> 42.9 us
  blocking collectives: 0 us -> 30.6 us
  Pallas kernels: 0 us -> 20.9 us
  between operations: 15.2 us -> 0.28 us
  starting transfers between devices: 30.7 us -> 45 us
    all_gather x2 -> x0, waiting for transfers between devices: 69.5 us -> none  [vertical_apply(): lax.all_gather(grid_field, 'lev', axis=1, tiled=True)]
    add x6 -> x0, other arithmetic: 69.2 us -> none  [the longest x4 67.7 us: weighted_sum(): summed + coeffs[:, :, offset][:, :, None, None] * lax.slice_in_dim(padded...]
    mul x62 -> x0, local copies, waits for them, and re-layouts: 40.9 us -> none  [the longest x58 38.7 us: weighted_sum(): coeffs[:, :, offset][:, :, None, None]]
    dot_general x6 -> x0, matrix products: 34.7 us -> none  [the longest x2 27.2 us: vertical_apply(): jnp.einsum('vkl,vlyx->vkyx', own_rows, lax.all_gather(grid_field, 'lev',...]
    all_to_all x0 -> x2, blocking collectives: none -> 30.6 us  [over_rings(): lax.all_to_all(value, 'lev', 0, 0, tiled=True, axis_index_groups=groups)]
    all_to_all x2 -> x3, waiting for transfers between devices: 0.01 us -> 29.7 us  [the longest x2 29.7 us: over_rings(): lax.all_to_all(value, 'lev', 0, 0, tiled=True, axis_index_groups=groups)]
    pallas_call x0 -> x11, Pallas kernels: none -> 20.9 us  [kernel_call(): pl.pallas_call(body, out_shape=list(outs), in_specs=[SMEM if i in smem el...]
    all_to_all x2 -> x0, other arithmetic: 19.4 us -> none  [the longest x1 18.6 us: observe(): lax.all_to_all(send_cells.reshape(1, 1, -1), ('lon', 'lat'), split_axis=2...]
  transfers between devices with their start and end apart: 12 -> 14, of which waited for: 7 -> 10; matrix products, arithmetic and copies ran while one was open for 44% -> 5% of each run, Pallas kernels for 0% -> 5%
where the time goes in v1:
time: 154 us; the launch traced here: 153 us
  starting transfers between devices  45 us (29%)
  waiting for transfers between devices  42.9 us (28%)
  blocking collectives  30.6 us (20%)
  Pallas kernels  20.9 us (14%)
  local copies, waits for them, and re-layouts  13.5 us (9%)
    all_to_all x2, blocking collectives, over_rings(): lax.all_to_all(value, 'lev', 0, 0, tiled=True, axis_index_groups=groups)  30.6 us
    all_to_all x2, waiting for transfers between devices, over_rings(): lax.all_to_all(value, 'lev', 0, 0, tiled=True, axis_index_groups=groups)  29.7 us
    pallas_call x11, Pallas kernels, kernel_call(): pl.pallas_call(body, out_shape=list(outs), in_specs=[SMEM if i in smem el...  20.9 us
    ppermute x8, starting transfers between devices, exchanged(): return (lax.ppermute(last, axis, up), lax.ppermute(first, axis, down))  14.4 us
    ppermute x3, starting transfers between devices, with_mate(): return lax.ppermute(value, 'lev', pairs)  13 us
    all_to_all x2, starting transfers between devices, over_rings(): lax.all_to_all(value, 'lev', 0, 0, tiled=True, axis_index_groups=groups)  10.8 us
    ppermute x8, waiting for transfers between devices, exchanged(): return (lax.ppermute(last, axis, up), lax.ppermute(first, axis, down))  10.3 us
    all_to_all x1, starting transfers between devices, local(): got_rows = lax.all_to_all(routed, ('lon', 'lat'), 0, 0, tiled=True)  6.81 us
  transfers between devices with their start and end apart: 14, of which 10 were waited for; matrix products, arithmetic and copies ran while one was open for 5% of the time, Pallas kernels for 5%

profile of v1, /device:TPU:1, one launch (start us, length us, event | category | flops | bytes accessed | tf_op | source)
XLA Modules:
  0.0 153.3 jit_solution(7501874328858010218)
XLA Ops:
  1.0 3.3 %collective-permute-start = (f32[9,64,128]{2,1,0:T(8,128)S(1)}, f32[9,64,128]{2,1,0:T(8,128)S(1)}, u32[]{:S(2)}, u32[]{:S(2)}) collective-permute-start(f32[9,64,128]{2,1,0:T(8,128)S(1)} %bitcast.19), channel_id=1, source_target_pairs={{0,1},{1,0},{2,3},{3,2},{4,5},{5,4},{6,7},{7,6},{8,9},{9,8},{10,11... | collective-permute-start | bytes 884744 | tf_op jit(solution)/shard_map/ppermute | solution.py:334
  4.4 1.2 collective-permute-done.mate
  7.5 6.5 %all-to-all-start = ((f32[8,18,8,128]{3,2,1,0:T(8,128)}), f32[8,18,8,128]{3,2,1,0:T(8,128)S(1)}, u32[]{:S(2)}, u32[]{:S(2)}) async-start(f32[8,18,8,128]{3,2,1,0:T(8,128)} %shard_map.82), calls=%async_computation | async-start | bytes 1179648 | tf_op jit(solution)/shard_map/all_to_all | solution.py:340
  16.0 17.3 %all-to-all-done.got.control = f32[8,18,8,128]{3,2,1,0:T(8,128)S(1)} async-done(((f32[8,18,8,128]{3,2,1,0:T(8,128)}), f32[8,18,8,128]{3,2,1,0:T(8,128)S(1)}, u32[]{:S(2)}, u32[]{:S(2)}) %all-to-all-start) | async-done | bytes 589856 | tf_op jit(solution)/shard_map/all_to_all | solution.py:340
  33.3 1.5 shard_map.83
  34.8 4.3 %all-to-all-start.1 = ((f32[8,18,8,128]{3,2,1,0:T(8,128)}), f32[8,18,8,128]{3,2,1,0:T(8,128)}, u32[]{:S(2)}, u32[]{:S(2)}) async-start(f32[8,18,8,128]{3,2,1,0:T(8,128)} %shard_map.83), calls=%async_computation.1 | async-start | bytes 1179648 | tf_op jit(solution)/shard_map/all_to_all | solution.py:340
  39.3 2.8 %shard_map.84 = (bf16[2,18,64,128]{3,2,1,0:T(8,128)(2,1)S(1)}, bf16[2,18,64,128]{3,2,1,0:T(8,128)(2,1)S(1)}, bf16[2,18,128,256]{3,2,1,0:T(8,128)(2,1)S(1)}, bf16[2,18,128,256]{3,2,1,0:T(8,128)(2,1)S(1)}) custom-call(f32[2,18,1,384]{3,2,1,0:T(1,128)S(1)} %copy.15.taps), custom_call_target="tpu_custom_call" | custom-call | flops 3600000 | bytes 5953536 | tf_op jit(solution)/shard_map/pallas_call | solution.py:26
  43.7 1.2 fusion.2
  44.9 1.2 fusion.3
  46.1 12.4 %all-to-all-done.1.rows = f32[8,18,8,128]{3,2,1,0:T(8,128)} async-done(((f32[8,18,8,128]{3,2,1,0:T(8,128)}), f32[8,18,8,128]{3,2,1,0:T(8,128)}, u32[]{:S(2)}, u32[]{:S(2)}) %all-to-all-start.1) | async-done | bytes 589856 | tf_op jit(solution)/shard_map/all_to_all | solution.py:340
  58.6 6.8 %all-to-all-start.2 = ((f32[16,16,128]{2,1,0:T(8,128)}), f32[16,16,128]{2,1,0:T(8,128)}, u32[]{:S(2)}, u32[]{:S(2)}) async-start(f32[16,16,128]{2,1,0:T(8,128)} %copy-done.7), calls=%async_computation.2 | async-start | bytes 262144 | tf_op jit(solution)/shard_map/all_to_all | solution.py:380
  66.4 3.2 %collective-permute-start.1 = (f32[2,18,8,128]{3,2,1,0:T(8,128)S(1)}, f32[2,18,8,128]{3,2,1,0:T(8,128)S(1)}, u32[]{:S(2)}, u32[]{:S(2)}) collective-permute-start(f32[2,18,8,128]{3,2,1,0:T(8,128)S(1)} %get-tuple-element.48), channel_id=1, source_target_pairs={{0,16},{16,32},{32,48},{1,17},{17,33},{33,49},{2,18},{18,34},{34,5... | collective-permute-start | bytes 442376 | tf_op jit(solution)/shard_map/ppermute | solution.py:329
  69.7 1.3 collective-permute-start.2
  71.0 1.8 %fusion.6 = (bf16[1,18,64,128]{3,2,1,0:T(8,128)(2,1)}, bf16[1,18,64,128]{3,2,1,0:T(8,128)(2,1)S(1)}) fusion(bf16[2,18,64,128]{3,2,1,0:T(8,128)(2,1)} %copy-done.6), kind=kLoop, calls=%fused_computation.19 | loop fusion | bytes 1179648 | tf_op jit(solution)/shard_map/slice | solution.py:433
  72.8 2.8 %collective-permute-done.2.after = f32[2,18,8,128]{3,2,1,0:T(8,128)S(1)} collective-permute-done((f32[2,18,8,128]{3,2,1,0:T(8,128)S(1)}, f32[2,18,8,128]{3,2,1,0:T(8,128)S(1)}, u32[]{:S(2)}, u32[]{:S(2)}) %collective-permute-start.2) | collective-permute-done | bytes 147488 | tf_op jit(solution)/shard_map/ppermute | solution.py:329
  75.5 2.9 %shard_map.85 = (f32[18,64,128]{2,1,0:T(8,128)S(1)}, f32[3,64,128]{2,1,0:T(8,128)}, f32[3,64,128]{2,1,0:T(8,128)}) custom-call(f32[8,18,8,128]{3,2,1,0:T(8,128)} %all-to-all-done.1.rows, f32[2,18,8,128]{3,2,1,0:T(8,128)S(1)} %collective-permute-done.1.before, f32[2,18,8,128]{3,2,1,0:T(8,128)S(1)} %collective-permute-done.2.after, ...), custom_call_target="tpu_custom_call" | custom-call | flops 113246208 | bytes 2260992 | tf_op jit(solution)/shard_map/pallas_call | solution.py:26
  79.3 1.2 collective-permute-start.4
  80.4 1.5 collective-permute-start.5
  84.3 1.3 copy-done.2
  85.5 1.3 copy-done.3
  87.9 6.7 %shard_map.88 = (f32[18,64,128]{2,1,0:T(8,128)S(1)}, f32[3,64,128]{2,1,0:T(8,128)S(1)}, f32[3,64,128]{2,1,0:T(8,128)S(1)}) custom-call(f32[18,64,128]{2,1,0:T(8,128)S(1)} %copy-done.9, f32[3,64,128]{2,1,0:T(8,128)} %collective-permute-done.4.left, f32[3,64,128]{2,1,0:T(8,128)} %collective-permute-done.5.right, bf16[1,18,128,256]{3,2,1,0:T(8,128)(2,1)S(1)} %copy-done.3, ...), custom_call_target="tpu_custom_call" | custom-call | flops 1207959552 | bytes 5185608 | tf_op jit(solution)/shard_map/pallas_call | solution.py:26
  94.6 1.2 collective-permute-start.6
  95.8 1.6 %collective-permute-start.7 = (f32[3,64,128]{2,1,0:T(8,128)S(1)}, f32[3,64,128]{2,1,0:T(8,128)S(1)}, u32[]{:S(2)}, u32[]{:S(2)}) collective-permute-start(f32[3,64,128]{2,1,0:T(8,128)S(1)} %get-tuple-element.34), channel_id=1, source_target_pairs={{64,0},{128,64},{192,128},{0,192},{65,1},{129,65},{193,129},{1,193... | collective-permute-start | bytes 294920 | tf_op jit(solution)/shard_map/ppermute | solution.py:329
  97.5 1.9 %collective-permute-done.6.left = f32[3,64,128]{2,1,0:T(8,128)S(1)} collective-permute-done((f32[3,64,128]{2,1,0:T(8,128)S(1)}, f32[3,64,128]{2,1,0:T(8,128)S(1)}, u32[]{:S(2)}, u32[]{:S(2)}) %collective-permute-start.6) | collective-permute-done | bytes 98336 | tf_op jit(solution)/shard_map/ppermute | solution.py:329
  99.4 1.7 %shard_map.89.rows = f32[8,18,8,128]{3,2,1,0:T(8,128)S(1)} custom-call(f32[18,64,128]{2,1,0:T(8,128)S(1)} %get-tuple-element.32.field, f32[3,64,128]{2,1,0:T(8,128)S(1)} %collective-permute-done.6.left, f32[3,64,128]{2,1,0:T(8,128)S(1)} %collective-permute-done.7.right, bf16[1,18,128,256]{3,2,1,0:T(8,128)(2,1)S(1)} %get-tuple-element.37.high, ...), custom_call_target="tpu_custom_call" | custom-call | flops 226492416 | bytes 3735552 | tf_op jit(solution)/shard_map/pallas_call | solution.py:26
  101.1 3.1 %collective-permute-start.8 = (f32[2,18,8,128]{3,2,1,0:T(8,128)S(1)}, f32[2,18,8,128]{3,2,1,0:T(8,128)S(1)}, u32[]{:S(2)}, u32[]{:S(2)}) collective-permute-start(f32[2,18,8,128]{3,2,1,0:T(8,128)S(1)} %get-tuple-element.46), channel_id=1, source_target_pairs={{0,16},{16,32},{32,48},{1,17},{17,33},{33,49},{2,18},{18,34},{34,5... | collective-permute-start | bytes 442376 | tf_op jit(solution)/shard_map/ppermute | solution.py:329
  104.2 1.3 collective-permute-start.9
  106.3 3.8 %collective-permute-done.9.after = f32[2,18,8,128]{3,2,1,0:T(8,128)S(1)} collective-permute-done((f32[2,18,8,128]{3,2,1,0:T(8,128)S(1)}, f32[2,18,8,128]{3,2,1,0:T(8,128)S(1)}, u32[]{:S(2)}, u32[]{:S(2)}) %collective-permute-start.9) | collective-permute-done | bytes 147488 | tf_op jit(solution)/shard_map/ppermute | solution.py:329
  111.0 15.3 %all_to_all.25.got = f32[8,18,8,128]{3,2,1,0:T(8,128)S(1)} all-to-all(f32[8,18,8,128]{3,2,1,0:T(8,128)S(1)} %shard_map.90), channel_id=1, replica_groups={{0,2,4,6,8,10,12,14},{1,3,5,7,9,11,13,15},{16,18,20,22,24,26,28,30},{17..., dimensions={0} | all-to-all | bytes 1179648 | tf_op jit(solution)/shard_map/all_to_all | solution.py:340
  127.0 15.2 %all_to_all.26 = f32[8,18,8,128]{3,2,1,0:T(8,128)S(1)} all-to-all(f32[8,18,8,128]{3,2,1,0:T(8,128)S(1)} %shard_map.91), channel_id=1, replica_groups={{0,2,4,6,8,10,12,14},{1,3,5,7,9,11,13,15},{16,18,20,22,24,26,28,30},{17..., dimensions={0} | all-to-all | bytes 1179648 | tf_op jit(solution)/shard_map/all_to_all | solution.py:340
  142.3 9.0 %collective-permute-start.10 = (f32[8,9,8,128]{3,2,1,0:T(8,128)S(1)}, f32[8,9,8,128]{3,2,1,0:T(8,128)S(1)}, u32[]{:S(2)}, u32[]{:S(2)}) collective-permute-start(f32[8,9,8,128]{3,2,1,0:T(8,128)S(1)} %get-tuple-element.39), channel_id=1, source_target_pairs={{0,1},{1,0},{2,3},{3,2},{4,5},{5,4},{6,7},{7,6},{8,9},{9,8},{10,11... | collective-permute-start | bytes 884744 | tf_op jit(solution)/shard_map/ppermute | solution.py:334
  151.3 1.2 collective-permute-done.10.other
  (68 shorter events, 15.1 us)
Async XLA Ops:
  0.0 14.9 %copy-start = (f32[6,48,48]{2,1,0:T(8,128)S(1)}, f32[6,48,48]{2,1,0:T(8,128)}, u32[]{:S(2)}) copy-start(f32[6,48,48]{2,1,0:T(8,128)} %param.9) | copy-start | bytes 165892
  1.0 4.5 %collective-permute-start = (f32[9,64,128]{2,1,0:T(8,128)S(1)}, f32[9,64,128]{2,1,0:T(8,128)S(1)}, u32[]{:S(2)}, u32[]{:S(2)}) collective-permute-start(f32[9,64,128]{2,1,0:T(8,128)S(1)} %bitcast.19), channel_id=1, source_target_pairs={{0,1},{1,0},{2,3},{3,2},{4,5},{5,4},{6,7},{7,6},{8,9},{9,8},{10,11... | collective-permute-start | bytes 884744 | tf_op jit(solution)/shard_map/ppermute | solution.py:334
  5.6 1.1 copy-start.1
  6.6 7.3 %copy-start.15 = (f32[6,3]{0,1:T(4,128)S(1)}, f32[6,3]{0,1:T(4,128)}, u32[]{:S(2)}) copy-start(f32[6,3]{0,1:T(4,128)} %param.13) | copy-start | bytes 220
  6.6 7.4 %copy-start.12 = (f32[6,3,512]{2,1,0:T(4,128)S(1)}, f32[6,3,512]{2,1,0:T(4,128)}, u32[]{:S(2)}) copy-start(f32[6,3,512]{2,1,0:T(4,128)} %param.12) | copy-start | bytes 110596
  6.6 7.4 %copy-start.13 = (f32[6,3,31]{2,1,0:T(4,128)S(1)}, f32[6,3,31]{2,1,0:T(4,128)}, u32[]{:S(2)}) copy-start(f32[6,3,31]{2,1,0:T(4,128)} %param.11) | copy-start | bytes 6700
  6.6 7.4 %copy-start.14 = (f32[6,3,31]{2,1,0:T(4,128)S(1)}, f32[6,3,31]{2,1,0:T(4,128)}, u32[]{:S(2)}) copy-start(f32[6,3,31]{2,1,0:T(4,128)} %param.10) | copy-start | bytes 6700
  7.5 25.8 %all-to-all-start = ((f32[8,18,8,128]{3,2,1,0:T(8,128)}), f32[8,18,8,128]{3,2,1,0:T(8,128)S(1)}, u32[]{:S(2)}, u32[]{:S(2)}) async-start(f32[8,18,8,128]{3,2,1,0:T(8,128)} %shard_map.82), calls=%async_computation | async-start | bytes 1179648 | tf_op jit(solution)/shard_map/all_to_all | solution.py:340
  14.2 1.6 %collective-permute-start.3 = (f32[3,3,575]{2,1,0:T(4,128)S(1)}, f32[3,3,575]{2,1,0:T(4,128)S(1)}, u32[]{:S(2)}, u32[]{:S(2)}) collective-permute-start(f32[3,3,575]{2,1,0:T(4,128)S(1)} %get-tuple-element.52), channel_id=1, source_target_pairs={{0,1},{1,0},{2,3},{3,2},{4,5},{5,4},{6,7},{7,6},{8,9},{9,8},{10,11... | collective-permute-start | bytes 62108 | tf_op jit(solution)/shard_map/ppermute | solution.py:334
  34.8 7.3 %copy-start.10 = (s32[512]{0:T(512)S(1)}, s32[512]{0:T(512)}, u32[]{:S(2)}) copy-start(s32[512]{0:T(512)} %param.14) | copy-start | bytes 6148
  34.8 7.3 %copy-start.11 = (s32[512]{0:T(512)S(1)}, s32[512]{0:T(512)}, u32[]{:S(2)}) copy-start(s32[512]{0:T(512)} %param.15) | copy-start | bytes 6148
  34.8 23.7 %all-to-all-start.1 = ((f32[8,18,8,128]{3,2,1,0:T(8,128)}), f32[8,18,8,128]{3,2,1,0:T(8,128)}, u32[]{:S(2)}, u32[]{:S(2)}) async-start(f32[8,18,8,128]{3,2,1,0:T(8,128)} %shard_map.83), calls=%async_computation.1 | async-start | bytes 1179648 | tf_op jit(solution)/shard_map/all_to_all | solution.py:340
  42.1 2.8 %copy-start.6 = (bf16[2,18,64,128]{3,2,1,0:T(8,128)(2,1)}, bf16[2,18,64,128]{3,2,1,0:T(8,128)(2,1)S(1)}, u32[]{:S(2)}) copy-start(bf16[2,18,64,128]{3,2,1,0:T(8,128)(2,1)S(1)} %get-tuple-element.20) | copy-start | bytes 1769476
  42.9 2.0 %copy-start.7 = (f32[16,16,128]{2,1,0:T(8,128)}, f32[16,16,128]{2,1,0:T(8,128)S(1)}, u32[]{:S(2)}) copy-start(f32[16,16,128]{2,1,0:T(8,128)S(1)} %shard_map.86) | copy-start | bytes 393220
  58.6 23.6 %all-to-all-start.2 = ((f32[16,16,128]{2,1,0:T(8,128)}), f32[16,16,128]{2,1,0:T(8,128)}, u32[]{:S(2)}, u32[]{:S(2)}) async-start(f32[16,16,128]{2,1,0:T(8,128)} %copy-done.7), calls=%async_computation.2 | async-start | bytes 262144 | tf_op jit(solution)/shard_map/all_to_all | solution.py:380
  65.4 10.2 %copy-start.5 = (bf16[1,18,64,128]{3,2,1,0:T(8,128)(2,1)S(1)}, bf16[1,18,64,128]{3,2,1,0:T(8,128)(2,1)}, u32[]{:S(2)}) copy-start(bf16[1,18,64,128]{3,2,1,0:T(8,128)(2,1)} %get-tuple-element.42.low) | copy-start | bytes 884740
  66.4 6.3 %collective-permute-start.1 = (f32[2,18,8,128]{3,2,1,0:T(8,128)S(1)}, f32[2,18,8,128]{3,2,1,0:T(8,128)S(1)}, u32[]{:S(2)}, u32[]{:S(2)}) collective-permute-start(f32[2,18,8,128]{3,2,1,0:T(8,128)S(1)} %get-tuple-element.48), channel_id=1, source_target_pairs={{0,16},{16,32},{32,48},{1,17},{17,33},{33,49},{2,18},{18,34},{34,5... | collective-permute-start | bytes 442376 | tf_op jit(solution)/shard_map/ppermute | solution.py:329
  69.7 5.9 %collective-permute-start.2 = (f32[2,18,8,128]{3,2,1,0:T(8,128)S(1)}, f32[2,18,8,128]{3,2,1,0:T(8,128)S(1)}, u32[]{:S(2)}, u32[]{:S(2)}) collective-permute-start(f32[2,18,8,128]{3,2,1,0:T(8,128)S(1)} %get-tuple-element.47), channel_id=1, source_target_pairs={{16,0},{32,16},{48,32},{17,1},{33,17},{49,33},{18,2},{34,18},{50,3... | collective-permute-start | bytes 442376 | tf_op jit(solution)/shard_map/ppermute | solution.py:329
  78.4 0.8 copy-start.8
  79.3 5.0 %collective-permute-start.4 = (f32[3,64,128]{2,1,0:T(8,128)}, f32[3,64,128]{2,1,0:T(8,128)}, u32[]{:S(2)}, u32[]{:S(2)}) collective-permute-start(f32[3,64,128]{2,1,0:T(8,128)} %get-tuple-element.23), channel_id=1, source_target_pairs={{0,64},{64,128},{128,192},{192,0},{1,65},{65,129},{129,193},{193,1... | collective-permute-start | bytes 294920 | tf_op jit(solution)/shard_map/ppermute | solution.py:329
  80.4 3.8 %collective-permute-start.5 = (f32[3,64,128]{2,1,0:T(8,128)}, f32[3,64,128]{2,1,0:T(8,128)}, u32[]{:S(2)}, u32[]{:S(2)}) collective-permute-start(f32[3,64,128]{2,1,0:T(8,128)} %get-tuple-element.24), channel_id=1, source_target_pairs={{64,0},{128,64},{192,128},{0,192},{65,1},{129,65},{193,129},{1,193... | collective-permute-start | bytes 294920 | tf_op jit(solution)/shard_map/ppermute | solution.py:329
  84.3 1.3 copy-start.2
  85.5 1.3 copy-start.3
  86.8 1.1 copy-start.9
  94.6 4.8 %collective-permute-start.6 = (f32[3,64,128]{2,1,0:T(8,128)S(1)}, f32[3,64,128]{2,1,0:T(8,128)S(1)}, u32[]{:S(2)}, u32[]{:S(2)}) collective-permute-start(f32[3,64,128]{2,1,0:T(8,128)S(1)} %get-tuple-element.33), channel_id=1, source_target_pairs={{0,64},{64,128},{128,192},{192,0},{1,65},{65,129},{129,193},{193,1... | collective-permute-start | bytes 294920 | tf_op jit(solution)/shard_map/ppermute | solution.py:329
  95.8 3.5 %collective-permute-start.7 = (f32[3,64,128]{2,1,0:T(8,128)S(1)}, f32[3,64,128]{2,1,0:T(8,128)S(1)}, u32[]{:S(2)}, u32[]{:S(2)}) collective-permute-start(f32[3,64,128]{2,1,0:T(8,128)S(1)} %get-tuple-element.34), channel_id=1, source_target_pairs={{64,0},{128,64},{192,128},{0,192},{65,1},{129,65},{193,129},{1,193... | collective-permute-start | bytes 294920 | tf_op jit(solution)/shard_map/ppermute | solution.py:329
  99.4 10.8 %copy-start.4 = (bf16[1,18,64,128]{3,2,1,0:T(8,128)(2,1)S(1)}, bf16[1,18,64,128]{3,2,1,0:T(8,128)(2,1)}, u32[]{:S(2)}) copy-start(bf16[1,18,64,128]{3,2,1,0:T(8,128)(2,1)} %get-tuple-element.43.high) | copy-start | bytes 884740
  101.1 5.2 %collective-permute-start.8 = (f32[2,18,8,128]{3,2,1,0:T(8,128)S(1)}, f32[2,18,8,128]{3,2,1,0:T(8,128)S(1)}, u32[]{:S(2)}, u32[]{:S(2)}) collective-permute-start(f32[2,18,8,128]{3,2,1,0:T(8,128)S(1)} %get-tuple-element.46), channel_id=1, source_target_pairs={{0,16},{16,32},{32,48},{1,17},{17,33},{33,49},{2,18},{18,34},{34,5... | collective-permute-start | bytes 442376 | tf_op jit(solution)/shard_map/ppermute | solution.py:329
  104.2 5.9 %collective-permute-start.9 = (f32[2,18,8,128]{3,2,1,0:T(8,128)S(1)}, f32[2,18,8,128]{3,2,1,0:T(8,128)S(1)}, u32[]{:S(2)}, u32[]{:S(2)}) collective-permute-start(f32[2,18,8,128]{3,2,1,0:T(8,128)S(1)} %get-tuple-element.45), channel_id=1, source_target_pairs={{16,0},{32,16},{48,32},{17,1},{33,17},{49,33},{18,2},{34,18},{50,3... | collective-permute-start | bytes 442376 | tf_op jit(solution)/shard_map/ppermute | solution.py:329
  142.3 10.2 %collective-permute-start.10 = (f32[8,9,8,128]{3,2,1,0:T(8,128)S(1)}, f32[8,9,8,128]{3,2,1,0:T(8,128)S(1)}, u32[]{:S(2)}, u32[]{:S(2)}) collective-permute-start(f32[8,9,8,128]{3,2,1,0:T(8,128)S(1)} %get-tuple-element.39), channel_id=1, source_target_pairs={{0,1},{1,0},{2,3},{3,2},{4,5},{5,4},{6,7},{7,6},{8,9},{9,8},{10,11... | collective-permute-start | bytes 884744 | tf_op jit(solution)/shard_map/ppermute | solution.py:334

commit v2 on v1

v2 whole, which is shorter than its diff:
```python
import functools

import jax
import jax.numpy as jnp
from jax import lax
from jax.experimental import pallas as pl
from jax.experimental.pallas import tpu as pltpu
from jax.sharding import PartitionSpec as P

F32, BF16, I32 = jnp.float32, jnp.bfloat16, jnp.int32
ROWS, COLS = 64, 128
TAPS = 31
STRIP = 16
LEVELS = 48
RINGS = 8
OWN = 6
SLOTS = 64
TILES = 16
OBS = 512
LON_AT, LAT_AT, WEIGHT_AT, SMALL = OBS, OBS + 128, OBS + 256, OBS + 384
PIECE = 16
VMEM = pl.BlockSpec(memory_space=pltpu.VMEM)
SMEM = pl.BlockSpec(memory_space=pltpu.SMEM)


def kernel_call(body, outs, ins, scratch=(), smem=(), flops=0, limit=16, after=()):
    moved = sum(a.size * a.dtype.itemsize for a in ins)
    moved += sum(o.size * o.dtype.itemsize for o in outs)
    count = len(after)
    return pl.pallas_call(
        lambda *refs: body(*refs[count:]),
        out_shape=list(outs),
        in_specs=[pl.BlockSpec(memory_space=pl.ANY)] * count
        + [SMEM if i in smem else VMEM for i in range(len(ins))],
        out_specs=[VMEM] * len(outs),
        scratch_shapes=list(scratch),
        compiler_params=pltpu.CompilerParams(vmem_limit_bytes=limit * 2**20),
        cost_estimate=pl.CostEstimate(flops=flops, bytes_accessed=moved, transcendentals=0),
    )(*after, *ins)


def shape(*dims, dtype=F32):
    return jax.ShapeDtypeStruct(dims, dtype)


def split(value):
    high = value.astype(BF16)
    return high, (value - high.astype(F32)).astype(BF16)


def mm(a, b):
    return jnp.dot(a, b, preferred_element_type=F32)


def mm_nt(a, b):
    return lax.dot_general(a, b, (((1,), (1,)), ((), ())), preferred_element_type=F32)


def begin_body(core, control, innovation, lon_taps, lat_taps, weight, kept, sent, kept_small, sent_small):
    c = core[0]
    kept_small[...] = jnp.zeros(kept_small.shape, F32)
    sent_small[...] = jnp.zeros(sent_small.shape, F32)
    for which, big, little in ((c, kept, kept_small), (1 - c, sent, sent_small)):
        for v in range(3):
            lon, lat, seen = [a[which * 3 + v] for a in (lon_taps, lat_taps, innovation)]
            for l in range(3):
                p = v * 3 + l
                big[p] = control[which * 3 + v, l]
                little[p, :, 0:OBS] = seen[l : l + 1]
                little[p, :, LON_AT : LON_AT + TAPS] = lon[l : l + 1]
                little[p, :, LAT_AT : LAT_AT + TAPS] = lat[l : l + 1]
                little[p, :, WEIGHT_AT:] = jnp.full((1, 128), weight[l, which * 3 + v], F32)


def arrange_body(control, mate, out):
    for p in range(9):
        out[:, p] = control[p].reshape(RINGS, 8, COLS)
        out[:, 9 + p] = mate[p].reshape(RINGS, 8, COLS)


def rows_of(v, start, count):
    return pl.ds(v * LEVELS * 8 + start, count)


def mixed(matrix, held, v, side):
    at = [pl.ds(v * LEVELS * 8 + s, LEVELS, stride=8) for s in range(8)]
    columns = jnp.concatenate([held[a, :] for a in at], axis=1)
    result = lax.dot_general(
        matrix, columns, (((side,), (0,)), ((), ())),
        precision=lax.Precision.HIGHEST, preferred_element_type=F32,
    )
    for s in range(8):
        held[at[s], :] = result[:, s * COLS : (s + 1) * COLS]


def levels_of(c, s, t, v):
    own = c if t == 0 else 1 - c
    return pl.ds(pl.multiple_of(v * LEVELS * 8 + s * 48 + own * 24, 8), 24)


def mix_body(core, got, matrix, out, held):
    c = core[0]
    for v in range(3):
        for s in range(RINGS):
            for t in range(2):
                first = t * 9 + v * 3
                held[levels_of(c, s, t, v), :] = got[s, first : first + 3].reshape(24, COLS)
        mixed(matrix[c * 3 + v], held, v, 1)
        for s in range(RINGS):
            out[s, v * OWN : (v + 1) * OWN] = held[rows_of(v, s * 48, 48), :].reshape(OWN, 8, COLS)


def unmix_body(core, got, matrix, control, out, held):
    c = core[0]
    for v in range(3):
        for s in range(RINGS):
            held[rows_of(v, s * 48, 48), :] = got[s, v * OWN : (v + 1) * OWN].reshape(48, COLS)
        mixed(matrix[c * 3 + v], held, v, 0)
        for s in range(RINGS):
            for t in range(2):
                first = t * 9 + v * 3
                part = held[levels_of(c, s, t, v), :].reshape(3, 8, COLS)
                out[s, first : first + 3] = part + control[s, first : first + 3]


def column_call(body, *ins):
    return kernel_call(
        body,
        [shape(*ins[1].shape)],
        ins,
        scratch=[pltpu.VMEM((3 * LEVELS * 8, COLS), F32)],
        smem=(0,),
        flops=2 * 3 * LEVELS * LEVELS * 1024 * 6,
    )[0]


def bands_body(core, kept, mate, high, low, back_high, back_low, lon_high, lon_low, weight):
    c = core[0]

    def toeplitz(row, height):
        full = jnp.broadcast_to(row, (height, row.shape[1]))
        return pltpu.roll(full, row.shape[1] - 15, 1, stride=1, stride_axis=0)

    def one(v, carry):
        for l in range(3):
            mine, other = kept[v * 3 + l], mate[v * 3 + l]
            for part in range(2):
                row = jnp.where(c == part, mine, other)
                p = v * OWN + part * 3 + l
                lat = toeplitz(row[:, LAT_AT : LAT_AT + 128], COLS)
                high[p], low[p] = split(lat[:ROWS])
                back_high[p], back_low[p] = split(lat.T[:ROWS])
                lon = jnp.concatenate([row[:, LON_AT : LON_AT + 128], jnp.zeros((1, 128), F32)], axis=1)
                lon_high[p], lon_low[p] = split(toeplitz(lon, COLS))
                weight[p] = row[:, WEIGHT_AT:]
        return carry

    lax.fori_loop(0, 3, one, 0)


def lat_filter(p, rows, before, after, high, low):
    extended = jnp.concatenate(
        [rows[:, p].reshape(ROWS, COLS), after, jnp.zeros((32, COLS), F32), before], axis=0
    )
    e_high, e_low = split(extended)
    return mm(high[p], e_high) + (mm(high[p], e_low) + mm(low[p], e_high))


def with_halo(l, field, left, right):
    lane = lax.broadcasted_iota(I32, (ROWS, COLS), 1)
    left = pltpu.roll(left, (COLS - STRIP - STRIP * l) % COLS, 1)
    right = pltpu.roll(right, (COLS - STRIP * l) % COLS, 1)
    halo = jnp.where(lane >= COLS - STRIP, left, jnp.where(lane < STRIP, right, 0.0))
    return split(jnp.concatenate([field, halo], axis=1))


def lon_filter(p, l, field, left, right, high, low):
    x_high, x_low = with_halo(l, field, left, right)
    return mm_nt(x_high, high[p]) + (mm_nt(x_low, high[p]) + mm_nt(x_high, low[p]))


def back_lon_filter(p, l, field, left, right, high, low):
    x_high, x_low = with_halo(l, field, left, right)
    b_high = jnp.concatenate([high[p, :, :COLS], high[p, :, COLS:]], axis=0)
    b_low = jnp.concatenate([low[p, :, :COLS], low[p, :, COLS:]], axis=0)
    return mm(x_high, b_high) + (mm(x_low, b_high) + mm(x_high, b_low))


def packed(fields):
    lane = lax.broadcasted_iota(I32, (ROWS, COLS), 1) // STRIP
    last = jnp.zeros((ROWS, COLS), F32)
    first = jnp.zeros((ROWS, COLS), F32)
    for l, field in enumerate(fields):
        last = jnp.where(lane == l, pltpu.roll(field, STRIP * (l + 1) % COLS, 1), last)
        first = jnp.where(lane == l, pltpu.roll(field, STRIP * l, 1) if l else field, first)
    return last, first


def lat_body(
    nv, latitude, rows, before, after, near, far, high, low, out, last, lead, own_rows, far_rows
):
    y = latitude[0]
    planes = nv * OWN

    def strip(at, p, there):
        both = jnp.concatenate([at[p], at[planes + p]], axis=0)
        return jnp.where(there, both, 0.0)

    def one(v, carry):
        fields = []
        for l in range(OWN):
            p = v * OWN + l
            ends = strip(before, p, y > 0), strip(after, p, y < 3)
            fields.append(lat_filter(p, rows, *ends, high, low))
        for l in range(OWN):
            out[v * OWN + l] = fields[l]
        last[v], lead[v] = packed(fields)
        return carry

    lax.fori_loop(0, nv, one, 0)
    for d, (target, block) in enumerate(((own_rows, None), (last, nv), (far_rows, None), (lead, nv))):
        first = 2 * planes + 2 * d
        came = jnp.concatenate(
            [near[d], before[first : first + 2].reshape(PIECE, COLS)]
            + [far[d], after[first : first + 2].reshape(PIECE, COLS)],
            axis=0,
        )
        if block is None:
            target[...] = came
        else:
            target[block] = came


def back_lat_body(nv, rows, before, after, high, low, out):
    def one(v, carry):
        for l in range(OWN):
            p = v * OWN + l
            ends = before[:, p].reshape(STRIP, COLS), after[:, p].reshape(STRIP, COLS)
            out[:, p] = lat_filter(p, rows, *ends, high, low).reshape(RINGS, 8, COLS)
        return carry

    lax.fori_loop(0, nv, one, 0)


def back_lon_body(nv, field, left, right, high, low, out):
    def one(v, carry):
        for l in range(OWN):
            p = v * OWN + l
            value = back_lon_filter(p, l, field[p], left[v], right[v], high, low)
            out[:, p] = value.reshape(RINGS, 8, COLS)
        return carry

    lax.fori_loop(0, nv, one, 0)


def observe_body(
    nv, field, left, right, own_rows, far_rows, high, low, weight,
    out, last, first, parts, values, misfit_high, misfit_low, row_hot, col_hot, col_hot2,
):
    arrived([own_rows[...], left[nv], far_rows[...], right[nv]], values, row_hot, col_hot, col_hot2)

    def filtered(v, carry):
        for l in range(OWN):
            p = v * OWN + l
            third = lon_filter(p, l, field[p], left[v], right[v], high, low)
            t_high, t_low = split(third)
            parts[p] = jnp.concatenate([t_high, t_low], axis=1)
        return carry

    lax.fori_loop(0, nv, filtered, 0)

    def gathered(v, carry):
        for l in range(OWN):
            p = v * OWN + l
            across = mm(parts[p], col_hot2[...])
            found = jnp.sum(across * row_hot[...], axis=0, keepdims=True)
            misfit = (found - values[p]) * jnp.concatenate([weight[p]] * 8, axis=1)
            m_high, m_low = split(misfit)
            misfit_high[p] = m_high.astype(F32)
            misfit_low[p] = m_low.astype(F32)
        return carry

    lax.fori_loop(0, nv, gathered, 0)

    def scattered(v, carry):
        fields = []
        for l in range(OWN):
            p = v * OWN + l
            w_high = (row_hot[...] * misfit_high[p]).astype(BF16)
            w_low = (row_hot[...] * misfit_low[p]).astype(BF16)
            both = mm_nt(jnp.concatenate([w_high, w_low], axis=0), col_hot[...])
            fields.append(both[:ROWS] + both[ROWS:])
            out[p] = fields[-1]
        last[v], first[v] = packed(fields)
        return carry

    lax.fori_loop(0, nv, scattered, 0)


def route_body(core, longitude, latitude, kept, mate, tile, cell, *outs):
    c = core[0]
    count = tile.shape[1]
    east = ((tile[...] >> 2) - longitude[0]) & 3
    north = ((tile[...] & 3) - latitude[0]) & 3
    away = north * 4 + east
    hot = (lax.broadcasted_iota(I32, (TILES, count), 0) == away).astype(F32)
    earlier = lax.broadcasted_iota(I32, (count, count), 0) < lax.broadcasted_iota(I32, (count, count), 1)
    before = mm(hot.astype(BF16), earlier.astype(F32).astype(BF16))
    place = jnp.sum(before * hot, axis=0, keepdims=True).astype(I32)
    slot = away * SLOTS + place
    slot_hot = (lax.broadcasted_iota(I32, (TILES * SLOTS, count), 0) == slot).astype(F32).astype(BF16)
    observed = []
    for v in range(3):
        for part in range(2):
            for l in range(3):
                p = v * 3 + l
                observed.append(jnp.where(c == part, kept[p, :, 0:OBS], mate[p, :, 0:OBS]))
    sent = jnp.concatenate(
        observed + [(cell[...] + 1).astype(F32), jnp.zeros((5, count), F32)], axis=0
    )
    high, rest = split(sent)
    remainder = sent - high.astype(F32)
    low = (remainder - rest.astype(F32)).astype(BF16)
    all_parts = mm_nt(jnp.concatenate([high, rest, low], axis=0), slot_hot)
    full = all_parts[0:24] + (all_parts[24:48] + all_parts[48:72])
    lane = lax.broadcasted_iota(I32, (8, COLS), 1)
    for e in range(TILES // 2):
        at = slice(e * COLS, (e + 1) * COLS)
        a, b, c = full[0:8, at], full[8:16, at], full[16:24, at]
        a2, b2, c2 = [pltpu.roll(x, SLOTS, 1) for x in (a, b, c)]
        out, d = outs[e // 2], e % 2 * 2
        out[d, 0:8] = jnp.where(lane < SLOTS, a, b2)
        out[d, 8:16] = jnp.where(lane < SLOTS, c, 0.0)
        out[d + 1, 0:8] = jnp.where(lane < SLOTS, a2, b)
        out[d + 1, 8:16] = jnp.where(lane < SLOTS, c2, 0.0)


def arrived(blocks, values, row_hot, col_hot, col_hot2):
    low = lax.broadcasted_iota(I32, (8, COLS), 1) < SLOTS
    full = []
    for block in blocks:
        for first in (0, 2 * PIECE):
            a, c, b, d = [block[first + 8 * i : first + 8 * i + 8] for i in range(4)]
            full.append(
                jnp.concatenate(
                    [
                        jnp.where(low, a, pltpu.roll(b, SLOTS, 1)),
                        jnp.where(low, pltpu.roll(a, SLOTS, 1), b),
                        jnp.where(low, c, pltpu.roll(d, SLOTS, 1)),
                    ],
                    axis=0,
                )
            )
    full = jnp.concatenate(full, axis=1)
    for p in range(18):
        values[p] = full[p : p + 1]
    cell = full[18:19].astype(I32) - 1
    count = cell.shape[1]
    row_hot[...] = (lax.broadcasted_iota(I32, (ROWS, count), 0) == (cell >> 7)).astype(F32)
    cols = (lax.broadcasted_iota(I32, (COLS, count), 0) == (cell & 127)).astype(F32).astype(BF16)
    col_hot[...] = cols
    col_hot2[0:COLS] = cols
    col_hot2[COLS : 2 * COLS] = cols


def neighbours(axis, wrap):
    size = lax.axis_size(axis)
    up = [(i, (i + 1) % size) for i in range(size if wrap else size - 1)]
    return up, [(j, i) for i, j in up]


def exchanged(last, first, axis, wrap):
    up, down = neighbours(axis, wrap)
    return lax.ppermute(last, axis, up), lax.ppermute(first, axis, down)


def across(value, axis):
    size = lax.axis_size(axis)
    return lax.ppermute(value, axis, [(i, (i + 2) % size) for i in range(size)])


def with_mate(value):
    pairs = [(i, i ^ 1) for i in range(lax.axis_size("lev"))]
    return lax.ppermute(value, "lev", pairs)


def over_rings(value):
    size = lax.axis_size("lev")
    groups = [list(range(0, size, 2)), list(range(1, size, 2))]
    return lax.all_to_all(value, "lev", 0, 0, tiled=True, axis_index_groups=groups)


def local(control, vertical, lon_taps, lat_taps, innovation, inv_variance, obs_tile, obs_cell):
    def index(axis):
        return lax.axis_index(axis).astype(I32).reshape(1)

    core, longitude, latitude = index("lev") % 2, index("lon"), index("lat")
    nv = 3
    planes = nv * OWN
    slots = TILES * SLOTS

    block, small_block = shape(9, ROWS, COLS), shape(9, 1, SMALL)
    kept, sent, kept_small, sent_small = kernel_call(
        begin_body,
        [block, block, small_block, small_block],
        [core, control, innovation, lon_taps, lat_taps, jnp.swapaxes(inv_variance, 0, 1)],
        smem=(0, 5),
    )
    mate_small = with_mate(sent_small)
    mate_control = with_mate(sent)
    piece = shape(4, PIECE, COLS)
    near, north, far, south = kernel_call(
        route_body,
        [piece] * 4,
        [core, longitude, latitude, kept_small, mate_small, obs_tile.reshape(1, -1), obs_cell.reshape(1, -1)],
        smem=(0, 1, 2),
        flops=2 * 72 * slots * obs_tile.shape[0],
    )
    arranged = kernel_call(
        arrange_body,
        [shape(RINGS, planes, 8, COLS)],
        [kept, mate_control],
        after=(near,),
    )[0]
    columns = over_rings(arranged)
    first = over_rings(column_call(mix_body, core, columns, vertical))

    def with_rows(strips, rows):
        return jnp.concatenate([strips.reshape(-1, 8, COLS), rows.reshape(-1, 8, COLS)], axis=0)

    before, after = exchanged(with_rows(first[6:8], north), with_rows(first[0:2], south), "lat", True)
    far = across(far, "lat")
    high, low, back_high, back_low, lon_high, lon_low, weight = kernel_call(
        bands_body,
        [shape(planes, ROWS, 128, dtype=BF16)] * 4
        + [shape(planes, COLS, 256, dtype=BF16)] * 2
        + [shape(planes, 1, 128)],
        [core, kept_small, mate_small],
        smem=(0,),
        flops=planes * 200000,
        after=(first,),
    )
    field_shape = shape(planes, ROWS, COLS)
    lat_flops = 2 * 3 * planes * ROWS * 128 * COLS
    row_block = shape(4 * PIECE, COLS)
    field, last, lead, own_rows, far_rows = kernel_call(
        functools.partial(lat_body, nv),
        [field_shape] + [shape(nv + 1, ROWS, COLS)] * 2 + [row_block] * 2,
        [latitude, first, before, after, near, far, high, low],
        smem=(0,),
        flops=lat_flops,
    )
    left, right = exchanged(last, lead, "lon", True)
    far_rows = across(far_rows, "lon")
    pack_shape = shape(nv, ROWS, COLS)
    placed, last, lead = kernel_call(
        functools.partial(observe_body, nv),
        [field_shape, pack_shape, pack_shape],
        [field, left, right, own_rows, far_rows, lon_high, lon_low, weight],
        scratch=[
            pltpu.VMEM((planes, ROWS, 2 * COLS), BF16),
            pltpu.VMEM((planes, 1, slots), F32),
            pltpu.VMEM((planes, 1, slots), F32),
            pltpu.VMEM((planes, 1, slots), F32),
            pltpu.VMEM((ROWS, slots), F32),
            pltpu.VMEM((COLS, slots), BF16),
            pltpu.VMEM((2 * COLS, slots), BF16),
        ],
        flops=2 * planes * ROWS * slots * 256 * 2,
    )
    left, right = exchanged(last, lead, "lon", True)
    back = kernel_call(
        functools.partial(back_lon_body, nv),
        [shape(RINGS, planes, 8, COLS)],
        [placed, left, right, lon_high, lon_low],
        flops=2 * lat_flops,
    )[0]
    before, after = exchanged(back[6:8], back[0:2], "lat", False)
    back = kernel_call(
        functools.partial(back_lat_body, nv),
        [shape(RINGS, planes, 8, COLS)],
        [back, before, after, back_high, back_low],
        flops=lat_flops,
    )[0]
    result = over_rings(column_call(unmix_body, core, over_rings(back), vertical, columns))

    mine, other = result[:, :9], with_mate(result[:, 9:])
    return kernel_call(
        finish_body,
        [shape(6, 3, ROWS, COLS)],
        [core, mine, other],
        smem=(0,),
    )[0]


def finish_body(core, mine, other, out):
    c = core[0]
    for v in range(3):
        for l in range(3):
            out[c * 3 + v, l] = mine[:, v * 3 + l].reshape(ROWS, COLS)
            out[(1 - c) * 3 + v, l] = other[:, v * 3 + l].reshape(ROWS, COLS)


def solution(mesh):
    return jax.shard_map(
        local,
        mesh=mesh,
        in_specs=(
            P(None, "lev", "lat", "lon"),
            P(),
            P(None, "lev", None),
            P(None, "lev", None),
            P(None, "lev", ("lon", "lat")),
            P(None, "lev"),
            P(("lon", "lat")),
            P(("lon", "lat")),
        ),
        out_specs=P(None, "lev", "lat", "lon"),
        check_vma=False,
    )
```

time: 154 us -> 138 us (0.90)
  blocking collectives: 30.6 us -> 76.1 us
  waiting for transfers between devices: 42.9 us -> 10.5 us
  starting transfers between devices: 45 us -> 29.6 us
  local copies, waits for them, and re-layouts: 13.5 us -> 5.4 us
  Pallas kernels: 20.9 us -> 15 us
    all_to_all x2 -> x4, blocking collectives: 30.6 us -> 76.1 us  [over_rings(): lax.all_to_all(value, 'lev', 0, 0, tiled=True, axis_index_groups=groups)]
    all_to_all x3 -> x0, waiting for transfers between devices: 29.7 us -> none  [the longest x2 29.7 us: over_rings(): lax.all_to_all(value, 'lev', 0, 0, tiled=True, axis_index_groups=groups)]
    all_to_all x3 -> x0, starting transfers between devices: 17.6 us -> none  [the longest x2 10.8 us: over_rings(): lax.all_to_all(value, 'lev', 0, 0, tiled=True, axis_index_groups=groups)]
    slice x8 -> x1, local copies, waits for them, and re-layouts: 6.32 us -> 0.02 us  [local(): first[0:2]]
    ppermute x8, waiting for transfers between devices: 10.3 us -> 4.09 us  [exchanged(): return (lax.ppermute(last, axis, up), lax.ppermute(first, axis, down))]
    pallas_call x11, Pallas kernels: 20.9 us -> 15 us  [kernel_call(): pl.pallas_call(lambda *refs: body(*refs[count:]), out_shape=list(outs), i...]
    ppermute x0 -> x2, waiting for transfers between devices: none -> 4.08 us  [across(): return lax.ppermute(value, axis, [(i, (i + 2) % size) for i in range(size)])]
    ppermute x0 -> x2, starting transfers between devices: none -> 3.16 us  [across(): return lax.ppermute(value, axis, [(i, (i + 2) % size) for i in range(size)])]
  transfers between devices with their start and end apart: 14 -> 13, of which waited for: 10 -> 7; matrix products, arithmetic and copies ran while one was open for 5% -> 0% of each run, Pallas kernels for 5% -> 2%
where the time goes in v2:
time: 138 us; the launch traced here: 137 us
  blocking collectives  76.1 us (55%)
  starting transfers between devices  29.6 us (21%)
  Pallas kernels  15 us (11%)
  waiting for transfers between devices  10.5 us (8%)
  local copies, waits for them, and re-layouts  5.4 us (4%)
    all_to_all x4, blocking collectives, over_rings(): lax.all_to_all(value, 'lev', 0, 0, tiled=True, axis_index_groups=groups)  76.1 us
    pallas_call x11, Pallas kernels, kernel_call(): pl.pallas_call(lambda *refs: body(*refs[count:]), out_shape=list(outs), i...  15 us
    ppermute x8, starting transfers between devices, exchanged(): return (lax.ppermute(last, axis, up), lax.ppermute(first, axis, down))  13.7 us
    ppermute x3, starting transfers between devices, with_mate(): return lax.ppermute(value, 'lev', pairs)  12.8 us
    unnamed x16, local copies, waits for them, and re-layouts  5.32 us
    ppermute x8, waiting for transfers between devices, exchanged(): return (lax.ppermute(last, axis, up), lax.ppermute(first, axis, down))  4.09 us
    ppermute x2, waiting for transfers between devices, across(): return lax.ppermute(value, axis, [(i, (i + 2) % size) for i in range(size)])  4.08 us
    ppermute x2, starting transfers between devices, across(): return lax.ppermute(value, axis, [(i, (i + 2) % size) for i in range(size)])  3.16 us
  transfers between devices with their start and end apart: 13, of which 7 were waited for; matrix products, arithmetic and copies ran while one was open for 0% of the time, Pallas kernels for 2%

profile of v2, /device:TPU:1, one launch (start us, length us, event | category | flops | bytes accessed | tf_op | source)
XLA Modules:
  0.0 136.8 jit_solution(3433354374194806885)
XLA Ops:
  0.0 1.1 copy-done.1
  1.1 0.8 copy-done.2
  4.6 3.3 %collective-permute-start.1 = (f32[9,64,128]{2,1,0:T(8,128)S(1)}, f32[9,64,128]{2,1,0:T(8,128)S(1)}, u32[]{:S(2)}, u32[]{:S(2)}) collective-permute-start(f32[9,64,128]{2,1,0:T(8,128)S(1)} %get-tuple-element.32), channel_id=1, source_target_pairs={{0,1},{1,0},{2,3},{3,2},{4,5},{5,4},{6,7},{7,6},{8,9},{9,8},{10,11... | collective-permute-start | bytes 884744 | tf_op jit(solution)/shard_map/ppermute | solution.py:384
  8.0 1.2 collective-permute-done.refs_4_.refs_3_
  10.5 0.7 shard_map.83
  11.4 24.8 %all_to_all.20.refs_1_.refs_3_ = f32[8,18,8,128]{3,2,1,0:T(8,128)S(1)} all-to-all(f32[8,18,8,128]{3,2,1,0:T(8,128)S(1)} %shard_map.84), channel_id=1, replica_groups={{0,2,4,6,8,10,12,14},{1,3,5,7,9,11,13,15},{16,18,20,22,24,26,28,30},{17..., dimensions={0} | all-to-all | bytes 1179648 | tf_op jit(solution)/shard_map/all_to_all | solution.py:390
  36.1 1.0 shard_map.85
  37.2 19.3 %all_to_all.21.refs_0_.refs_1_ = f32[8,18,8,128]{3,2,1,0:T(8,128)S(1)} all-to-all(f32[8,18,8,128]{3,2,1,0:T(8,128)S(1)} %shard_map.85), channel_id=1, replica_groups={{0,2,4,6,8,10,12,14},{1,3,5,7,9,11,13,15},{16,18,20,22,24,26,28,30},{17..., dimensions={0} | all-to-all | bytes 1179648 | tf_op jit(solution)/shard_map/all_to_all | solution.py:390
  56.6 1.4 collective-permute-start.2
  58.0 1.5 %collective-permute-start.3 = (f32[44,8,128]{2,1,0:T(8,128)S(1)}, f32[44,8,128]{2,1,0:T(8,128)S(1)}, u32[]{:S(2)}, u32[]{:S(2)}) collective-permute-start(f32[44,8,128]{2,1,0:T(8,128)S(1)} %pad_maximum_fusion.1), channel_id=1, source_target_pairs={{16,0},{32,16},{48,32},{0,48},{17,1},{33,17},{49,33},{1,49},{18,2}... | collective-permute-start | bytes 540680 | tf_op jit(solution)/shard_map/ppermute | solution.py:374
  59.5 1.6 %collective-permute-start.4 = (f32[4,16,128]{2,1,0:T(8,128)S(1)}, f32[4,16,128]{2,1,0:T(8,128)S(1)}, u32[]{:S(2)}, u32[]{:S(2)}) collective-permute-start(f32[4,16,128]{2,1,0:T(8,128)S(1)} %get-tuple-element.35), channel_id=1, source_target_pairs={{0,32},{16,48},{32,0},{48,16},{1,33},{17,49},{33,1},{49,17},{2,34}... | collective-permute-start | bytes 98312 | tf_op jit(solution)/shard_map/ppermute | solution.py:379
  61.1 1.3 shard_map.86
  62.5 1.3 collective-permute-done.4.refs_5_
  63.8 1.2 shard_map.87
  65.0 1.3 collective-permute-start.5
  66.3 1.4 %collective-permute-start.6 = (f32[4,64,128]{2,1,0:T(8,128)S(1)}, f32[4,64,128]{2,1,0:T(8,128)S(1)}, u32[]{:S(2)}, u32[]{:S(2)}) collective-permute-start(f32[4,64,128]{2,1,0:T(8,128)S(1)} %get-tuple-element.40), channel_id=1, source_target_pairs={{64,0},{128,64},{192,128},{0,192},{65,1},{129,65},{193,129},{1,193... | collective-permute-start | bytes 393224 | tf_op jit(solution)/shard_map/ppermute | solution.py:374
  67.7 1.5 %collective-permute-start.7 = (f32[64,128]{1,0:T(8,128)S(1)}, f32[64,128]{1,0:T(8,128)S(1)}, u32[]{:S(2)}, u32[]{:S(2)}) collective-permute-start(f32[64,128]{1,0:T(8,128)S(1)} %get-tuple-element.42), channel_id=1, source_target_pairs={{0,128},{64,192},{128,0},{192,64},{1,129},{65,193},{129,1},{193,65... | collective-permute-start | bytes 98312 | tf_op jit(solution)/shard_map/ppermute | solution.py:379
  69.3 2.7 %collective-permute-done.7.refs_4_ = f32[64,128]{1,0:T(8,128)S(1)} collective-permute-done((f32[64,128]{1,0:T(8,128)S(1)}, f32[64,128]{1,0:T(8,128)S(1)}, u32[]{:S(2)}, u32[]{:S(2)}) %collective-permute-start.7) | collective-permute-done | bytes 32800 | tf_op jit(solution)/shard_map/ppermute | solution.py:379
  72.0 6.1 %shard_map.88 = (f32[18,64,128]{2,1,0:T(8,128)S(1)}, f32[3,64,128]{2,1,0:T(8,128)S(1)}, f32[3,64,128]{2,1,0:T(8,128)S(1)}) custom-call(f32[18,64,128]{2,1,0:T(8,128)S(1)} %get-tuple-element.38.refs_0_, f32[4,64,128]{2,1,0:T(8,128)S(1)} %collective-permute-done.5.refs_1_, f32[4,64,128]{2,1,0:T(8,128)S(1)} %collective-permute-done.6.refs_2_, ...), custom_call_target="tpu_custom_call" | custom-call | flops 1207959552 | bytes 4072448 | tf_op jit(solution)/shard_map/pallas_call | solution.py:30
  78.4 2.4 %collective-permute-start.9 = (f32[3,64,128]{2,1,0:T(8,128)S(1)}, f32[3,64,128]{2,1,0:T(8,128)S(1)}, u32[]{:S(2)}, u32[]{:S(2)}) collective-permute-start(f32[3,64,128]{2,1,0:T(8,128)S(1)} %get-tuple-element.48), channel_id=1, source_target_pairs={{64,0},{128,64},{192,128},{0,192},{65,1},{129,65},{193,129},{1,193... | collective-permute-start | bytes 294920 | tf_op jit(solution)/shard_map/ppermute | solution.py:374
  80.9 2.0 %collective-permute-done.8.refs_1_ = f32[3,64,128]{2,1,0:T(8,128)S(1)} collective-permute-done((f32[3,64,128]{2,1,0:T(8,128)S(1)}, f32[3,64,128]{2,1,0:T(8,128)S(1)}, u32[]{:S(2)}, u32[]{:S(2)}) %collective-permute-start.8) | collective-permute-done | bytes 98336 | tf_op jit(solution)/shard_map/ppermute | solution.py:374
  82.9 1.1 shard_map.89.refs_0_
  84.0 1.3 collective-permute-start.11
  85.3 4.0 %collective-permute-start.10 = (f32[2,18,8,128]{3,2,1,0:T(8,128)S(1)}, f32[2,18,8,128]{3,2,1,0:T(8,128)S(1)}, u32[]{:S(2)}, u32[]{:S(2)}) collective-permute-start(f32[2,18,8,128]{3,2,1,0:T(8,128)S(1)} %get-tuple-element.54), channel_id=1, source_target_pairs={{0,16},{16,32},{32,48},{1,17},{17,33},{33,49},{2,18},{18,34},{34,5... | collective-permute-start | bytes 442376 | tf_op jit(solution)/shard_map/ppermute | solution.py:374
  89.9 1.5 %collective-permute-done.10.refs_1_ = f32[2,18,8,128]{3,2,1,0:T(8,128)S(1)} collective-permute-done((f32[2,18,8,128]{3,2,1,0:T(8,128)S(1)}, f32[2,18,8,128]{3,2,1,0:T(8,128)S(1)}, u32[]{:S(2)}, u32[]{:S(2)}) %collective-permute-start.10) | collective-permute-done | bytes 147488 | tf_op jit(solution)/shard_map/ppermute | solution.py:374
  91.4 0.9 shard_map.90
  92.3 16.8 %all_to_all.22.refs_1_ = f32[8,18,8,128]{3,2,1,0:T(8,128)S(1)} all-to-all(f32[8,18,8,128]{3,2,1,0:T(8,128)S(1)} %shard_map.90), channel_id=1, replica_groups={{0,2,4,6,8,10,12,14},{1,3,5,7,9,11,13,15},{16,18,20,22,24,26,28,30},{17..., dimensions={0} | all-to-all | bytes 1179648 | tf_op jit(solution)/shard_map/all_to_all | solution.py:390
  109.0 1.1 shard_map.91
  110.1 15.2 %all_to_all.23 = f32[8,18,8,128]{3,2,1,0:T(8,128)S(1)} all-to-all(f32[8,18,8,128]{3,2,1,0:T(8,128)S(1)} %shard_map.91), channel_id=1, replica_groups={{0,2,4,6,8,10,12,14},{1,3,5,7,9,11,13,15},{16,18,20,22,24,26,28,30},{17..., dimensions={0} | all-to-all | bytes 1179648 | tf_op jit(solution)/shard_map/all_to_all | solution.py:390
  125.4 9.3 %collective-permute-start.12 = (f32[8,9,8,128]{3,2,1,0:T(8,128)S(1)}, f32[8,9,8,128]{3,2,1,0:T(8,128)S(1)}, u32[]{:S(2)}, u32[]{:S(2)}) collective-permute-start(f32[8,9,8,128]{3,2,1,0:T(8,128)S(1)} %get-tuple-element.51), channel_id=1, source_target_pairs={{0,1},{1,0},{2,3},{3,2},{4,5},{5,4},{6,7},{7,6},{8,9},{9,8},{10,11... | collective-permute-start | bytes 884744 | tf_op jit(solution)/shard_map/ppermute | solution.py:384
  134.7 1.2 collective-permute-done.12.refs_2_
  136.0 0.9 shard_map.92
  (30 shorter events, 5.3 us)
Async XLA Ops:
  0.0 1.1 copy-start.1
  1.1 0.8 copy-start.2
  1.9 0.7 copy-start.3
  2.6 0.7 copy-start.4
  3.3 0.7 copy-start.5
  4.6 6.7 %collective-permute-start.1 = (f32[9,64,128]{2,1,0:T(8,128)S(1)}, f32[9,64,128]{2,1,0:T(8,128)S(1)}, u32[]{:S(2)}, u32[]{:S(2)}) collective-permute-start(f32[9,64,128]{2,1,0:T(8,128)S(1)} %get-tuple-element.32), channel_id=1, source_target_pairs={{0,1},{1,0},{2,3},{3,2},{4,5},{5,4},{6,7},{7,6},{8,9},{9,8},{10,11... | collective-permute-start | bytes 884744 | tf_op jit(solution)/shard_map/ppermute | solution.py:384
  7.9 1.3 collective-permute-start
  9.2 0.7 copy-start.6
  9.9 0.7 copy-start.7
  11.3 24.8 %copy-start = (f32[6,48,48]{2,1,0:T(8,128)S(1)}, f32[6,48,48]{2,1,0:T(8,128)}, u32[]{:S(2)}) copy-start(f32[6,48,48]{2,1,0:T(8,128)} %refs_2_.5) | copy-start | bytes 165892
  56.6 7.2 %collective-permute-start.2 = (f32[44,8,128]{2,1,0:T(8,128)S(1)}, f32[44,8,128]{2,1,0:T(8,128)S(1)}, u32[]{:S(2)}, u32[]{:S(2)}) collective-permute-start(f32[44,8,128]{2,1,0:T(8,128)S(1)} %pad_maximum_fusion), channel_id=1, source_target_pairs={{0,16},{16,32},{32,48},{48,0},{1,17},{17,33},{33,49},{49,1},{2,18}... | collective-permute-start | bytes 540680 | tf_op jit(solution)/shard_map/ppermute | solution.py:374
  58.0 5.9 %collective-permute-start.3 = (f32[44,8,128]{2,1,0:T(8,128)S(1)}, f32[44,8,128]{2,1,0:T(8,128)S(1)}, u32[]{:S(2)}, u32[]{:S(2)}) collective-permute-start(f32[44,8,128]{2,1,0:T(8,128)S(1)} %pad_maximum_fusion.1), channel_id=1, source_target_pairs={{16,0},{32,16},{48,32},{0,48},{17,1},{33,17},{49,33},{1,49},{18,2}... | collective-permute-start | bytes 540680 | tf_op jit(solution)/shard_map/ppermute | solution.py:374
  59.5 4.3 %collective-permute-start.4 = (f32[4,16,128]{2,1,0:T(8,128)S(1)}, f32[4,16,128]{2,1,0:T(8,128)S(1)}, u32[]{:S(2)}, u32[]{:S(2)}) collective-permute-start(f32[4,16,128]{2,1,0:T(8,128)S(1)} %get-tuple-element.35), channel_id=1, source_target_pairs={{0,32},{16,48},{32,0},{48,16},{1,33},{17,49},{33,1},{49,17},{2,34}... | collective-permute-start | bytes 98312 | tf_op jit(solution)/shard_map/ppermute | solution.py:379
  65.0 7.0 %collective-permute-start.5 = (f32[4,64,128]{2,1,0:T(8,128)S(1)}, f32[4,64,128]{2,1,0:T(8,128)S(1)}, u32[]{:S(2)}, u32[]{:S(2)}) collective-permute-start(f32[4,64,128]{2,1,0:T(8,128)S(1)} %get-tuple-element.39), channel_id=1, source_target_pairs={{0,64},{64,128},{128,192},{192,0},{1,65},{65,129},{129,193},{193,1... | collective-permute-start | bytes 393224 | tf_op jit(solution)/shard_map/ppermute | solution.py:374
  66.3 5.7 %collective-permute-start.6 = (f32[4,64,128]{2,1,0:T(8,128)S(1)}, f32[4,64,128]{2,1,0:T(8,128)S(1)}, u32[]{:S(2)}, u32[]{:S(2)}) collective-permute-start(f32[4,64,128]{2,1,0:T(8,128)S(1)} %get-tuple-element.40), channel_id=1, source_target_pairs={{64,0},{128,64},{192,128},{0,192},{65,1},{129,65},{193,129},{1,193... | collective-permute-start | bytes 393224 | tf_op jit(solution)/shard_map/ppermute | solution.py:374
  67.7 4.3 %collective-permute-start.7 = (f32[64,128]{1,0:T(8,128)S(1)}, f32[64,128]{1,0:T(8,128)S(1)}, u32[]{:S(2)}, u32[]{:S(2)}) collective-permute-start(f32[64,128]{1,0:T(8,128)S(1)} %get-tuple-element.42), channel_id=1, source_target_pairs={{0,128},{64,192},{128,0},{192,64},{1,129},{65,193},{129,1},{193,65... | collective-permute-start | bytes 98312 | tf_op jit(solution)/shard_map/ppermute | solution.py:379
  78.1 4.8 %collective-permute-start.8 = (f32[3,64,128]{2,1,0:T(8,128)S(1)}, f32[3,64,128]{2,1,0:T(8,128)S(1)}, u32[]{:S(2)}, u32[]{:S(2)}) collective-permute-start(f32[3,64,128]{2,1,0:T(8,128)S(1)} %get-tuple-element.47), channel_id=1, source_target_pairs={{0,64},{64,128},{128,192},{192,0},{1,65},{65,129},{129,193},{193,1... | collective-permute-start | bytes 294920 | tf_op jit(solution)/shard_map/ppermute | solution.py:374
  78.4 4.4 %collective-permute-start.9 = (f32[3,64,128]{2,1,0:T(8,128)S(1)}, f32[3,64,128]{2,1,0:T(8,128)S(1)}, u32[]{:S(2)}, u32[]{:S(2)}) collective-permute-start(f32[3,64,128]{2,1,0:T(8,128)S(1)} %get-tuple-element.48), channel_id=1, source_target_pairs={{64,0},{128,64},{192,128},{0,192},{65,1},{129,65},{193,129},{1,193... | collective-permute-start | bytes 294920 | tf_op jit(solution)/shard_map/ppermute | solution.py:374
  84.0 5.9 %collective-permute-start.11 = (f32[2,18,8,128]{3,2,1,0:T(8,128)S(1)}, f32[2,18,8,128]{3,2,1,0:T(8,128)S(1)}, u32[]{:S(2)}, u32[]{:S(2)}) collective-permute-start(f32[2,18,8,128]{3,2,1,0:T(8,128)S(1)} %get-tuple-element.53), channel_id=1, source_target_pairs={{16,0},{32,16},{48,32},{17,1},{33,17},{49,33},{18,2},{34,18},{50,3... | collective-permute-start | bytes 442376 | tf_op jit(solution)/shard_map/ppermute | solution.py:374
  85.3 6.1 %collective-permute-start.10 = (f32[2,18,8,128]{3,2,1,0:T(8,128)S(1)}, f32[2,18,8,128]{3,2,1,0:T(8,128)S(1)}, u32[]{:S(2)}, u32[]{:S(2)}) collective-permute-start(f32[2,18,8,128]{3,2,1,0:T(8,128)S(1)} %get-tuple-element.54), channel_id=1, source_target_pairs={{0,16},{16,32},{32,48},{1,17},{17,33},{33,49},{2,18},{18,34},{34,5... | collective-permute-start | bytes 442376 | tf_op jit(solution)/shard_map/ppermute | solution.py:374
  125.4 10.5 %collective-permute-start.12 = (f32[8,9,8,128]{3,2,1,0:T(8,128)S(1)}, f32[8,9,8,128]{3,2,1,0:T(8,128)S(1)}, u32[]{:S(2)}, u32[]{:S(2)}) collective-permute-start(f32[8,9,8,128]{3,2,1,0:T(8,128)S(1)} %get-tuple-element.51), channel_id=1, source_target_pairs={{0,1},{1,0},{2,3},{3,2},{4,5},{5,4},{6,7},{7,6},{8,9},{9,8},{10,11... | collective-permute-start | bytes 884744 | tf_op jit(solution)/shard_map/ppermute | solution.py:384

commit v3 on v2

--- a/solution.py
+++ b/solution.py
@@ -56,16 +56,23 @@
     return lax.dot_general(a, b, (((1,), (1,)), ((), ())), preferred_element_type=F32)
 
 
-def begin_body(core, control, innovation, lon_taps, lat_taps, weight, kept, sent, kept_small, sent_small):
-    c = core[0]
-    kept_small[...] = jnp.zeros(kept_small.shape, F32)
-    sent_small[...] = jnp.zeros(sent_small.shape, F32)
-    for which, big, little in ((c, kept, kept_small), (1 - c, sent, sent_small)):
+def begin_body(core, control, kept, sent):
+    c = core[0]
+    for which, big in ((c, kept), (1 - c, sent)):
+        for v in range(3):
+            for l in range(3):
+                big[v * 3 + l] = control[which * 3 + v, l]
+
+
+def small_body(core, innovation, lon_taps, lat_taps, weight, kept, sent):
+    c = core[0]
+    kept[...] = jnp.zeros(kept.shape, F32)
+    sent[...] = jnp.zeros(sent.shape, F32)
+    for which, little in ((c, kept), (1 - c, sent)):
         for v in range(3):
             lon, lat, seen = [a[which * 3 + v] for a in (lon_taps, lat_taps, innovation)]
             for l in range(3):
                 p = v * 3 + l
-                big[p] = control[which * 3 + v, l]
                 little[p, :, 0:OBS] = seen[l : l + 1]
                 little[p, :, LON_AT : LON_AT + TAPS] = lon[l : l + 1]
                 little[p, :, LAT_AT : LAT_AT + TAPS] = lat[l : l + 1]
@@ -123,7 +130,7 @@
                 out[s, first : first + 3] = part + control[s, first : first + 3]
 
 
-def column_call(body, *ins):
+def column_call(body, *ins, after=()):
     return kernel_call(
         body,
         [shape(*ins[1].shape)],
@@ -131,6 +138,7 @@
         scratch=[pltpu.VMEM((3 * LEVELS * 8, COLS), F32)],
         smem=(0,),
         flops=2 * 3 * LEVELS * LEVELS * 1024 * 6,
+        after=after,
     )[0]
 
 
@@ -218,7 +226,7 @@
         return carry
 
     lax.fori_loop(0, nv, one, 0)
-    for d, (target, block) in enumerate(((own_rows, None), (last, nv), (far_rows, None), (lead, nv))):
+    for d, (target, block) in enumerate(((own_rows, None), (last, nv), (lead, nv), (far_rows, None))):
         first = 2 * planes + 2 * d
         came = jnp.concatenate(
             [near[d], before[first : first + 2].reshape(PIECE, COLS)]
@@ -231,11 +239,16 @@
             target[block] = came
 
 
-def back_lat_body(nv, rows, before, after, high, low, out):
+def back_lat_body(nv, latitude, rows, before, after, high, low, out):
+    y = latitude[0]
+
     def one(v, carry):
         for l in range(OWN):
             p = v * OWN + l
-            ends = before[:, p].reshape(STRIP, COLS), after[:, p].reshape(STRIP, COLS)
+            ends = (
+                jnp.where(y > 0, before[:, p].reshape(STRIP, COLS), 0.0),
+                jnp.where(y < 3, after[:, p].reshape(STRIP, COLS), 0.0),
+            )
             out[:, p] = lat_filter(p, rows, *ends, high, low).reshape(RINGS, 8, COLS)
         return carry
 
@@ -270,10 +283,11 @@
     lax.fori_loop(0, nv, filtered, 0)
 
     def gathered(v, carry):
+        block = parts[pl.ds(v * OWN, OWN)].reshape(OWN * ROWS, 2 * COLS)
+        across = mm(block, col_hot2[...])
         for l in range(OWN):
             p = v * OWN + l
-            across = mm(parts[p], col_hot2[...])
-            found = jnp.sum(across * row_hot[...], axis=0, keepdims=True)
+            found = jnp.sum(across[l * ROWS : (l + 1) * ROWS] * row_hot[...], axis=0, keepdims=True)
             misfit = (found - values[p]) * jnp.concatenate([weight[p]] * 8, axis=1)
             m_high, m_low = split(misfit)
             misfit_high[p] = m_high.astype(F32)
@@ -283,21 +297,24 @@
     lax.fori_loop(0, nv, gathered, 0)
 
     def scattered(v, carry):
+        placed = []
+        for l in range(OWN):
+            p = v * OWN + l
+            placed.append((row_hot[...] * misfit_high[p]).astype(BF16))
+            placed.append((row_hot[...] * misfit_low[p]).astype(BF16))
+        both = mm_nt(jnp.concatenate(placed, axis=0), col_hot[...])
         fields = []
         for l in range(OWN):
-            p = v * OWN + l
-            w_high = (row_hot[...] * misfit_high[p]).astype(BF16)
-            w_low = (row_hot[...] * misfit_low[p]).astype(BF16)
-            both = mm_nt(jnp.concatenate([w_high, w_low], axis=0), col_hot[...])
-            fields.append(both[:ROWS] + both[ROWS:])
-            out[p] = fields[-1]
+            at = 2 * l * ROWS
+            fields.append(both[at : at + ROWS] + both[at + ROWS : at + 2 * ROWS])
+            out[v * OWN + l] = fields[-1]
         last[v], first[v] = packed(fields)
         return carry
 
     lax.fori_loop(0, nv, scattered, 0)
 
 
-def route_body(core, longitude, latitude, kept, mate, tile, cell, *outs):
+def route_body(core, longitude, latitude, kept, mate, tile, cell, out, half_way):
     c = core[0]
     count = tile.shape[1]
     east = ((tile[...] >> 2) - longitude[0]) & 3
@@ -328,11 +345,13 @@
         at = slice(e * COLS, (e + 1) * COLS)
         a, b, c = full[0:8, at], full[8:16, at], full[16:24, at]
         a2, b2, c2 = [pltpu.roll(x, SLOTS, 1) for x in (a, b, c)]
-        out, d = outs[e // 2], e % 2 * 2
-        out[d, 0:8] = jnp.where(lane < SLOTS, a, b2)
-        out[d, 8:16] = jnp.where(lane < SLOTS, c, 0.0)
-        out[d + 1, 0:8] = jnp.where(lane < SLOTS, a2, b)
-        out[d + 1, 8:16] = jnp.where(lane < SLOTS, c2, 0.0)
+        pair = (
+            (jnp.where(lane < SLOTS, a, b2), jnp.where(lane < SLOTS, c, 0.0)),
+            (jnp.where(lane < SLOTS, a2, b), jnp.where(lane < SLOTS, c2, 0.0)),
+        )
+        for i in range(2):
+            target, at = (out, (e // 2, i)) if e % 2 == 0 else ((half_way, (e // 2,)), (out, (e // 2, 2)))[i]
+            target[(*at, slice(0, 8))], target[(*at, slice(8, 16))] = pair[i]
 
 
 def arrived(blocks, values, row_hot, col_hot, col_hot2):
@@ -363,14 +382,10 @@
     col_hot2[COLS : 2 * COLS] = cols
 
 
-def neighbours(axis, wrap):
+def exchanged(last, first, axis):
     size = lax.axis_size(axis)
-    up = [(i, (i + 1) % size) for i in range(size if wrap else size - 1)]
-    return up, [(j, i) for i, j in up]
-
-
-def exchanged(last, first, axis, wrap):
-    up, down = neighbours(axis, wrap)
+    up = [(i, (i + 1) % size) for i in range(size)]
+    down = [(j, i) for i, j in up]
     return lax.ppermute(last, axis, up), lax.ppermute(first, axis, down)
 
 
@@ -400,36 +415,29 @@
     slots = TILES * SLOTS
 
     block, small_block = shape(9, ROWS, COLS), shape(9, 1, SMALL)
-    kept, sent, kept_small, sent_small = kernel_call(
-        begin_body,
-        [block, block, small_block, small_block],
-        [core, control, innovation, lon_taps, lat_taps, jnp.swapaxes(inv_variance, 0, 1)],
-        smem=(0, 5),
+    kept, sent = kernel_call(begin_body, [block, block], [core, control], smem=(0,))
+    arranged = kernel_call(
+        arrange_body, [shape(RINGS, planes, 8, COLS)], [kept, with_mate(sent)]
+    )[0]
+    columns = over_rings(arranged)
+
+    kept_small, sent_small = kernel_call(
+        small_body,
+        [small_block, small_block],
+        [core, innovation, lon_taps, lat_taps, jnp.swapaxes(inv_variance, 0, 1)],
+        smem=(0, 4),
+        after=(arranged,),
     )
     mate_small = with_mate(sent_small)
-    mate_control = with_mate(sent)
-    piece = shape(4, PIECE, COLS)
-    near, north, far, south = kernel_call(
+    routed, half_way = kernel_call(
         route_body,
-        [piece] * 4,
+        [shape(4, 3, PIECE, COLS), shape(4, PIECE, COLS)],
         [core, longitude, latitude, kept_small, mate_small, obs_tile.reshape(1, -1), obs_cell.reshape(1, -1)],
         smem=(0, 1, 2),
         flops=2 * 72 * slots * obs_tile.shape[0],
     )
-    arranged = kernel_call(
-        arrange_body,
-        [shape(RINGS, planes, 8, COLS)],
-        [kept, mate_control],
-        after=(near,),
-    )[0]
-    columns = over_rings(arranged)
-    first = over_rings(column_call(mix_body, core, columns, vertical))
-
-    def with_rows(strips, rows):
-        return jnp.concatenate([strips.reshape(-1, 8, COLS), rows.reshape(-1, 8, COLS)], axis=0)
-
-    before, after = exchanged(with_rows(first[6:8], north), with_rows(first[0:2], south), "lat", True)
-    far = across(far, "lat")
+    pieces = jnp.concatenate([routed, across(half_way, "lon")[:, None]], axis=1)
+    far = across(pieces[2], "lat")
     high, low, back_high, back_low, lon_high, lon_low, weight = kernel_call(
         bands_body,
         [shape(planes, ROWS, 128, dtype=BF16)] * 4
@@ -438,7 +446,14 @@
         [core, kept_small, mate_small],
         smem=(0,),
         flops=planes * 200000,
-        after=(first,),
+    )
+    first = over_rings(column_call(mix_body, core, columns, vertical, after=(far, weight)))
+
+    def with_rows(strips, rows):
+        return jnp.concatenate([strips.reshape(-1, 8, COLS), rows.reshape(-1, 8, COLS)], axis=0)
+
+    before, after = exchanged(
+        with_rows(first[6:8], pieces[1]), with_rows(first[0:2], pieces[3]), "lat"
     )
     field_shape = shape(planes, ROWS, COLS)
     lat_flops = 2 * 3 * planes * ROWS * 128 * COLS
@@ -446,12 +461,11 @@
     field, last, lead, own_rows, far_rows = kernel_call(
         functools.partial(lat_body, nv),
         [field_shape] + [shape(nv + 1, ROWS, COLS)] * 2 + [row_block] * 2,
-        [latitude, first, before, after, near, far, high, low],
+        [latitude, first, before, after, pieces[0], far, high, low],
         smem=(0,),
         flops=lat_flops,
     )
-    left, right = exchanged(last, lead, "lon", True)
-    far_rows = across(far_rows, "lon")
+    left, right = exchanged(last, lead, "lon")
     pack_shape = shape(nv, ROWS, COLS)
     placed, last, lead = kernel_call(
         functools.partial(observe_body, nv),
@@ -468,18 +482,19 @@
         ],
         flops=2 * planes * ROWS * slots * 256 * 2,
     )
-    left, right = exchanged(last, lead, "lon", True)
+    left, right = exchanged(last, lead, "lon")
     back = kernel_call(
         functools.partial(back_lon_body, nv),
         [shape(RINGS, planes, 8, COLS)],
         [placed, left, right, lon_high, lon_low],
         flops=2 * lat_flops,
     )[0]
-    before, after = exchanged(back[6:8], back[0:2], "lat", False)
+    before, after = exchanged(back[6:8], back[0:2], "lat")
     back = kernel_call(
         functools.partial(back_lat_body, nv),
         [shape(RINGS, planes, 8, COLS)],
-        [back, before, after, back_high, back_low],
+        [latitude, back, before, after, back_high, back_low],
+        smem=(0,),
         flops=lat_flops,
     )[0]
     result = over_rings(column_call(unmix_body, core, over_rings(back), vertical, columns))

time: 138 us -> 130 us (0.942)
  blocking collectives: 76.1 us -> 50.2 us
  waiting for transfers between devices: 10.5 us -> 22.9 us
  starting transfers between devices: 29.6 us -> 37.7 us
  local copies, waits for them, and re-layouts: 5.4 us -> 3.34 us
    all_to_all x4 -> x3, blocking collectives: 76.1 us -> 50.2 us  [over_rings(): lax.all_to_all(value, 'lev', 0, 0, tiled=True, axis_index_groups=groups)]
    ppermute x8, waiting for transfers between devices: 4.09 us -> 13.1 us  [exchanged(): return (lax.ppermute(last, axis, up), lax.ppermute(first, axis, down))]
    all_to_all x0 -> x1, starting transfers between devices: none -> 6.58 us  [over_rings(): lax.all_to_all(value, 'lev', 0, 0, tiled=True, axis_index_groups=groups)]
    all_to_all x0 -> x1, waiting for transfers between devices: none -> 4.67 us  [over_rings(): lax.all_to_all(value, 'lev', 0, 0, tiled=True, axis_index_groups=groups)]
    ppermute x2, starting transfers between devices: 3.16 us -> 5.74 us  [across(): return lax.ppermute(value, axis, [(i, (i + 2) % size) for i in range(size)])]
    ppermute x2, waiting for transfers between devices: 4.08 us -> 1.82 us  [across(): return lax.ppermute(value, axis, [(i, (i + 2) % size) for i in range(size)])]
    unnamed x16 -> x32, local copies, waits for them, and re-layouts: 5.32 us -> 3.26 us
    pallas_call x11 -> x12, Pallas kernels: 15 us -> 14.8 us  [kernel_call(): pl.pallas_call(lambda *refs: body(*refs[count:]), out_shape=list(outs), i...]
  transfers between devices with their start and end apart: 13 -> 14, of which waited for: 7 -> 11; matrix products, arithmetic and copies ran while one was open for 0% -> 0% of each run, Pallas kernels for 2% -> 2%
where the time goes in v3:
time: 130 us
  blocking collectives  50.2 us (39%)
  starting transfers between devices  37.7 us (29%)
  waiting for transfers between devices  22.9 us (18%)
  Pallas kernels  14.8 us (11%)
  local copies, waits for them, and re-layouts  3.34 us (3%)
    all_to_all x3, blocking collectives, over_rings(): lax.all_to_all(value, 'lev', 0, 0, tiled=True, axis_index_groups=groups)  50.2 us
    pallas_call x12, Pallas kernels, kernel_call(): pl.pallas_call(lambda *refs: body(*refs[count:]), out_shape=list(outs), i...  14.8 us
    ppermute x8, waiting for transfers between devices, exchanged(): return (lax.ppermute(last, axis, up), lax.ppermute(first, axis, down))  13.1 us
    ppermute x3, starting transfers between devices, with_mate(): return lax.ppermute(value, 'lev', pairs)  12.7 us
    ppermute x8, starting transfers between devices, exchanged(): return (lax.ppermute(last, axis, up), lax.ppermute(first, axis, down))  12.6 us
    all_to_all x1, starting transfers between devices, over_rings(): lax.all_to_all(value, 'lev', 0, 0, tiled=True, axis_index_groups=groups)  6.58 us
    ppermute x2, starting transfers between devices, across(): return lax.ppermute(value, axis, [(i, (i + 2) % size) for i in range(size)])  5.74 us
    all_to_all x1, waiting for transfers between devices, over_rings(): lax.all_to_all(value, 'lev', 0, 0, tiled=True, axis_index_groups=groups)  4.67 us
  transfers between devices with their start and end apart: 14, of which 11 were waited for; matrix products, arithmetic and copies ran while one was open for 0% of the time, Pallas kernels for 2%

profile of v3, /device:TPU:1, one launch (start us, length us, event | category | flops | bytes accessed | tf_op | source)
XLA Modules:
  0.0 129.7 jit_solution(3019714347671153900)
XLA Ops:
  0.0 1.1 copy-done.1
  1.1 3.3 %collective-permute-start = (f32[9,64,128]{2,1,0:T(8,128)S(1)}, f32[9,64,128]{2,1,0:T(8,128)S(1)}, u32[]{:S(2)}, u32[]{:S(2)}) collective-permute-start(f32[9,64,128]{2,1,0:T(8,128)S(1)} %get-tuple-element.27), channel_id=1, source_target_pairs={{0,1},{1,0},{2,3},{3,2},{4,5},{5,4},{6,7},{7,6},{8,9},{9,8},{10,11... | collective-permute-start | bytes 884744 | tf_op jit(solution)/shard_map/ppermute | solution.py:399
  4.4 1.2 collective-permute-done.refs_1_
  6.5 6.6 %all-to-all-start = ((f32[8,18,8,128]{3,2,1,0:T(8,128)}), f32[8,18,8,128]{3,2,1,0:T(8,128)S(1)}, u32[]{:S(2)}, u32[]{:S(2)}) async-start(f32[8,18,8,128]{3,2,1,0:T(8,128)} %shard_map.83.refs_0_), calls=%async_computation | async-start | bytes 1179648 | tf_op jit(solution)/shard_map/all_to_all | solution.py:405
  16.1 2.8 %collective-permute-start.2 = (f32[4,16,128]{2,1,0:T(8,128)S(1)}, f32[4,16,128]{2,1,0:T(8,128)S(1)}, u32[]{:S(2)}, u32[]{:S(2)}) collective-permute-start(f32[4,16,128]{2,1,0:T(8,128)S(1)} %get-tuple-element.31), channel_id=1, source_target_pairs={{0,128},{64,192},{128,0},{192,64},{1,129},{65,193},{129,1},{193,65... | collective-permute-start | bytes 98312 | tf_op jit(solution)/shard_map/ppermute | solution.py:394
  18.9 1.8 %collective-permute-done.2 = f32[4,16,128]{2,1,0:T(8,128)S(1)} collective-permute-done((f32[4,16,128]{2,1,0:T(8,128)S(1)}, f32[4,16,128]{2,1,0:T(8,128)S(1)}, u32[]{:S(2)}, u32[]{:S(2)}) %collective-permute-start.2) | collective-permute-done | bytes 32800 | tf_op jit(solution)/shard_map/ppermute | solution.py:394
  21.4 2.9 %collective-permute-start.3 = (f32[4,16,128]{2,1,0:T(8,128)S(1)}, f32[4,16,128]{2,1,0:T(8,128)S(1)}, u32[]{:S(2)}, u32[]{:S(2)}) collective-permute-start(f32[4,16,128]{2,1,0:T(8,128)S(1)} %get-tuple-element.54), channel_id=1, source_target_pairs={{0,32},{16,48},{32,0},{48,16},{1,33},{17,49},{33,1},{49,17},{2,34}... | collective-permute-start | bytes 98312 | tf_op jit(solution)/shard_map/ppermute | solution.py:394
  24.3 1.3 %shard_map.86 = (bf16[18,64,128]{2,1,0:T(8,128)(2,1)S(1)}, bf16[18,64,128]{2,1,0:T(8,128)(2,1)S(1)}, bf16[18,64,128]{2,1,0:T(8,128)(2,1)S(1)}, bf16[18,64,128]{2...) custom-call(s32[1]{0:T(128)S(6)} %select_n.7.refs_0_.refs_1_.refs_2_, ...), custom_call_target="tpu_custom_call" | custom-call | flops 3600000 | bytes 3612676 | tf_op jit(solution)/shard_map/pallas_call | solution.py:30
  27.8 4.7 %all-to-all-done.refs_3_ = f32[8,18,8,128]{3,2,1,0:T(8,128)S(1)} async-done(((f32[8,18,8,128]{3,2,1,0:T(8,128)}), f32[8,18,8,128]{3,2,1,0:T(8,128)S(1)}, u32[]{:S(2)}, u32[]{:S(2)}) %all-to-all-start) | async-done | bytes 589856 | tf_op jit(solution)/shard_map/all_to_all | solution.py:405
  32.5 1.0 shard_map.87
  33.6 19.5 %all_to_all.20.refs_1_ = f32[8,18,8,128]{3,2,1,0:T(8,128)S(1)} all-to-all(f32[8,18,8,128]{3,2,1,0:T(8,128)S(1)} %shard_map.87), channel_id=1, replica_groups={{0,2,4,6,8,10,12,14},{1,3,5,7,9,11,13,15},{16,18,20,22,24,26,28,30},{17..., dimensions={0} | all-to-all | bytes 1179648 | tf_op jit(solution)/shard_map/all_to_all | solution.py:405
  53.1 2.8 %collective-permute-start.4 = (f32[44,8,128]{2,1,0:T(8,128)S(1)}, f32[44,8,128]{2,1,0:T(8,128)S(1)}, u32[]{:S(2)}, u32[]{:S(2)}) collective-permute-start(f32[44,8,128]{2,1,0:T(8,128)S(1)} %pad_maximum_fusion), channel_id=1, source_target_pairs={{0,16},{16,32},{32,48},{48,0},{1,17},{17,33},{33,49},{49,1},{2,18}... | collective-permute-start | bytes 540680 | tf_op jit(solution)/shard_map/ppermute | solution.py:389
  55.9 1.9 %collective-permute-start.5 = (f32[44,8,128]{2,1,0:T(8,128)S(1)}, f32[44,8,128]{2,1,0:T(8,128)S(1)}, u32[]{:S(2)}, u32[]{:S(2)}) collective-permute-start(f32[44,8,128]{2,1,0:T(8,128)S(1)} %pad_maximum_fusion.1), channel_id=1, source_target_pairs={{16,0},{32,16},{48,32},{0,48},{17,1},{33,17},{49,33},{1,49},{18,2}... | collective-permute-start | bytes 540680 | tf_op jit(solution)/shard_map/ppermute | solution.py:389
  57.8 3.4 %collective-permute-done.4.refs_2_ = f32[44,8,128]{2,1,0:T(8,128)S(1)} collective-permute-done((f32[44,8,128]{2,1,0:T(8,128)S(1)}, f32[44,8,128]{2,1,0:T(8,128)S(1)}, u32[]{:S(2)}, u32[]{:S(2)}) %collective-permute-start.4) | collective-permute-done | bytes 180256 | tf_op jit(solution)/shard_map/ppermute | solution.py:389
  61.2 1.2 shard_map.88
  62.3 1.2 collective-permute-start.6
  63.6 1.5 %collective-permute-start.7 = (f32[4,64,128]{2,1,0:T(8,128)S(1)}, f32[4,64,128]{2,1,0:T(8,128)S(1)}, u32[]{:S(2)}, u32[]{:S(2)}) collective-permute-start(f32[4,64,128]{2,1,0:T(8,128)S(1)} %get-tuple-element.37), channel_id=1, source_target_pairs={{64,0},{128,64},{192,128},{0,192},{65,1},{129,65},{193,129},{1,193... | collective-permute-start | bytes 393224 | tf_op jit(solution)/shard_map/ppermute | solution.py:389
  65.1 2.4 %collective-permute-done.6.refs_1_ = f32[4,64,128]{2,1,0:T(8,128)S(1)} collective-permute-done((f32[4,64,128]{2,1,0:T(8,128)S(1)}, f32[4,64,128]{2,1,0:T(8,128)S(1)}, u32[]{:S(2)}, u32[]{:S(2)}) %collective-permute-start.6) | collective-permute-done | bytes 131104 | tf_op jit(solution)/shard_map/ppermute | solution.py:389
  67.4 5.1 %shard_map.89 = (f32[18,64,128]{2,1,0:T(8,128)S(1)}, f32[3,64,128]{2,1,0:T(8,128)S(1)}, f32[3,64,128]{2,1,0:T(8,128)S(1)}) custom-call(f32[18,64,128]{2,1,0:T(8,128)S(1)} %get-tuple-element.35.refs_0_, f32[4,64,128]{2,1,0:T(8,128)S(1)} %collective-permute-done.6.refs_1_, f32[4,64,128]{2,1,0:T(8,128)S(1)} %collective-permute-done.7.refs_2_, ...), custom_call_target="tpu_custom_call" | custom-call | flops 1207959552 | bytes 4072448 | tf_op jit(solution)/shard_map/pallas_call | solution.py:30
  72.5 1.5 %collective-permute-start.8 = (f32[3,64,128]{2,1,0:T(8,128)S(1)}, f32[3,64,128]{2,1,0:T(8,128)S(1)}, u32[]{:S(2)}, u32[]{:S(2)}) collective-permute-start(f32[3,64,128]{2,1,0:T(8,128)S(1)} %get-tuple-element.43), channel_id=1, source_target_pairs={{0,64},{64,128},{128,192},{192,0},{1,65},{65,129},{129,193},{193,1... | collective-permute-start | bytes 294920 | tf_op jit(solution)/shard_map/ppermute | solution.py:389
  74.1 1.3 %collective-permute-start.9 = (f32[3,64,128]{2,1,0:T(8,128)S(1)}, f32[3,64,128]{2,1,0:T(8,128)S(1)}, u32[]{:S(2)}, u32[]{:S(2)}) collective-permute-start(f32[3,64,128]{2,1,0:T(8,128)S(1)} %get-tuple-element.44), channel_id=1, source_target_pairs={{64,0},{128,64},{192,128},{0,192},{65,1},{129,65},{193,129},{1,193... | collective-permute-start | bytes 294920 | tf_op jit(solution)/shard_map/ppermute | solution.py:389
  75.4 1.9 %collective-permute-done.8.refs_1_ = f32[3,64,128]{2,1,0:T(8,128)S(1)} collective-permute-done((f32[3,64,128]{2,1,0:T(8,128)S(1)}, f32[3,64,128]{2,1,0:T(8,128)S(1)}, u32[]{:S(2)}, u32[]{:S(2)}) %collective-permute-start.8) | collective-permute-done | bytes 98336 | tf_op jit(solution)/shard_map/ppermute | solution.py:389
  77.5 1.1 shard_map.90.refs_1_
  78.7 2.4 %collective-permute-start.11 = (f32[2,18,8,128]{3,2,1,0:T(8,128)S(1)}, f32[2,18,8,128]{3,2,1,0:T(8,128)S(1)}, u32[]{:S(2)}, u32[]{:S(2)}) collective-permute-start(f32[2,18,8,128]{3,2,1,0:T(8,128)S(1)} %get-tuple-element.49), channel_id=1, source_target_pairs={{16,0},{32,16},{48,32},{0,48},{17,1},{33,17},{49,33},{1,49},{18,2}... | collective-permute-start | bytes 442376 | tf_op jit(solution)/shard_map/ppermute | solution.py:389
  81.1 2.1 %collective-permute-done.11.refs_3_ = f32[2,18,8,128]{3,2,1,0:T(8,128)S(1)} collective-permute-done((f32[2,18,8,128]{3,2,1,0:T(8,128)S(1)}, f32[2,18,8,128]{3,2,1,0:T(8,128)S(1)}, u32[]{:S(2)}, u32[]{:S(2)}) %collective-permute-start.11) | collective-permute-done | bytes 147488 | tf_op jit(solution)/shard_map/ppermute | solution.py:389
  83.2 3.1 %collective-permute-done.10.refs_2_ = f32[2,18,8,128]{3,2,1,0:T(8,128)S(1)} collective-permute-done((f32[2,18,8,128]{3,2,1,0:T(8,128)S(1)}, f32[2,18,8,128]{3,2,1,0:T(8,128)S(1)}, u32[]{:S(2)}, u32[]{:S(2)}) %collective-permute-start.10) | collective-permute-done | bytes 147488 | tf_op jit(solution)/shard_map/ppermute | solution.py:389
  86.3 0.9 shard_map.91
  87.1 15.3 %all_to_all.21.refs_1_ = f32[8,18,8,128]{3,2,1,0:T(8,128)S(1)} all-to-all(f32[8,18,8,128]{3,2,1,0:T(8,128)S(1)} %shard_map.91), channel_id=1, replica_groups={{0,2,4,6,8,10,12,14},{1,3,5,7,9,11,13,15},{16,18,20,22,24,26,28,30},{17..., dimensions={0} | all-to-all | bytes 1179648 | tf_op jit(solution)/shard_map/all_to_all | solution.py:405
  102.5 1.1 shard_map.92
  103.6 15.3 %all_to_all.22 = f32[8,18,8,128]{3,2,1,0:T(8,128)S(1)} all-to-all(f32[8,18,8,128]{3,2,1,0:T(8,128)S(1)} %shard_map.92), channel_id=1, replica_groups={{0,2,4,6,8,10,12,14},{1,3,5,7,9,11,13,15},{16,18,20,22,24,26,28,30},{17..., dimensions={0} | all-to-all | bytes 1179648 | tf_op jit(solution)/shard_map/all_to_all | solution.py:405
  119.0 8.7 %collective-permute-start.12 = (f32[8,9,8,128]{3,2,1,0:T(8,128)S(1)}, f32[8,9,8,128]{3,2,1,0:T(8,128)S(1)}, u32[]{:S(2)}, u32[]{:S(2)}) collective-permute-start(f32[8,9,8,128]{3,2,1,0:T(8,128)S(1)} %get-tuple-element.47), channel_id=1, source_target_pairs={{0,1},{1,0},{2,3},{3,2},{4,5},{5,4},{6,7},{7,6},{8,9},{9,8},{10,11... | collective-permute-start | bytes 884744 | tf_op jit(solution)/shard_map/ppermute | solution.py:399
  127.6 1.2 collective-permute-done.12.refs_2_
  (49 shorter events, 7.9 us)
Async XLA Ops:
  0.0 1.1 copy-start.1
  1.1 4.5 %collective-permute-start = (f32[9,64,128]{2,1,0:T(8,128)S(1)}, f32[9,64,128]{2,1,0:T(8,128)S(1)}, u32[]{:S(2)}, u32[]{:S(2)}) collective-permute-start(f32[9,64,128]{2,1,0:T(8,128)S(1)} %get-tuple-element.27), channel_id=1, source_target_pairs={{0,1},{1,0},{2,3},{3,2},{4,5},{5,4},{6,7},{7,6},{8,9},{9,8},{10,11... | collective-permute-start | bytes 884744 | tf_op jit(solution)/shard_map/ppermute | solution.py:399
  5.6 7.5 %copy-start.8 = (f32[6,3,512]{2,1,0:T(4,128)S(1)}, f32[6,3,512]{2,1,0:T(4,128)}, u32[]{:S(2)}) copy-start(f32[6,3,512]{2,1,0:T(4,128)} %refs_2_.2) | copy-start | bytes 110596
  5.6 7.5 %copy-start.9 = (f32[6,3,31]{2,1,0:T(4,128)S(1)}, f32[6,3,31]{2,1,0:T(4,128)}, u32[]{:S(2)}) copy-start(f32[6,3,31]{2,1,0:T(4,128)} %refs_3_.1) | copy-start | bytes 6700
  5.6 7.5 %copy-start.10 = (f32[6,3,31]{2,1,0:T(4,128)S(1)}, f32[6,3,31]{2,1,0:T(4,128)}, u32[]{:S(2)}) copy-start(f32[6,3,31]{2,1,0:T(4,128)} %refs_4_.2) | copy-start | bytes 6700
  5.7 7.5 %copy-start.11 = (f32[6,3]{0,1:T(4,128)S(1)}, f32[6,3]{0,1:T(4,128)}, u32[]{:S(2)}) copy-start(f32[6,3]{0,1:T(4,128)} %param.13) | copy-start | bytes 220
  6.5 8.8 %copy-start.12 = (s32[512]{0:T(512)S(1)}, s32[512]{0:T(512)}, u32[]{:S(2)}) copy-start(s32[512]{0:T(512)} %param.14) | copy-start | bytes 6148
  6.5 8.8 %copy-start.13 = (s32[512]{0:T(512)S(1)}, s32[512]{0:T(512)}, u32[]{:S(2)}) copy-start(s32[512]{0:T(512)} %param.15) | copy-start | bytes 6148
  6.5 25.9 %copy-start = (f32[6,48,48]{2,1,0:T(8,128)S(1)}, f32[6,48,48]{2,1,0:T(8,128)}, u32[]{:S(2)}) copy-start(f32[6,48,48]{2,1,0:T(8,128)} %refs_2_.3) | copy-start | bytes 165892
  6.5 25.9 %all-to-all-start = ((f32[8,18,8,128]{3,2,1,0:T(8,128)}), f32[8,18,8,128]{3,2,1,0:T(8,128)S(1)}, u32[]{:S(2)}, u32[]{:S(2)}) async-start(f32[8,18,8,128]{3,2,1,0:T(8,128)} %shard_map.83.refs_0_), calls=%async_computation | async-start | bytes 1179648 | tf_op jit(solution)/shard_map/all_to_all | solution.py:405
  13.7 1.6 %collective-permute-start.1 = (f32[9,1,896]{2,1,0:T(1,128)S(1)}, f32[9,1,896]{2,1,0:T(1,128)S(1)}, u32[]{:S(2)}, u32[]{:S(2)}) collective-permute-start(f32[9,1,896]{2,1,0:T(1,128)S(1)} %get-tuple-element.29), channel_id=1, source_target_pairs={{0,1},{1,0},{2,3},{3,2},{4,5},{5,4},{6,7},{7,6},{8,9},{9,8},{10,11... | collective-permute-start | bytes 96776 | tf_op jit(solution)/shard_map/ppermute | solution.py:399
  16.1 4.7 %collective-permute-start.2 = (f32[4,16,128]{2,1,0:T(8,128)S(1)}, f32[4,16,128]{2,1,0:T(8,128)S(1)}, u32[]{:S(2)}, u32[]{:S(2)}) collective-permute-start(f32[4,16,128]{2,1,0:T(8,128)S(1)} %get-tuple-element.31), channel_id=1, source_target_pairs={{0,128},{64,192},{128,0},{192,64},{1,129},{65,193},{129,1},{193,65... | collective-permute-start | bytes 98312 | tf_op jit(solution)/shard_map/ppermute | solution.py:394
  21.4 6.4 %collective-permute-start.3 = (f32[4,16,128]{2,1,0:T(8,128)S(1)}, f32[4,16,128]{2,1,0:T(8,128)S(1)}, u32[]{:S(2)}, u32[]{:S(2)}) collective-permute-start(f32[4,16,128]{2,1,0:T(8,128)S(1)} %get-tuple-element.54), channel_id=1, source_target_pairs={{0,32},{16,48},{32,0},{48,16},{1,33},{17,49},{33,1},{49,17},{2,34}... | collective-permute-start | bytes 98312 | tf_op jit(solution)/shard_map/ppermute | solution.py:394
  25.6 0.7 copy-start.2
  26.3 0.7 copy-start.4
  27.1 0.7 copy-start.6
  33.5 19.5 %copy-start.15 = (f32[1,4,16,128]{3,2,1,0:T(8,128)S(1)}, f32[1,4,16,128]{3,2,1,0:T(8,128)}, u32[]{:S(2)}) copy-start(f32[1,4,16,128]{3,2,1,0:T(8,128)} %get-tuple-element.55) | copy-start | bytes 98308
  33.5 22.4 %copy-start.14 = (f32[1,4,16,128]{3,2,1,0:T(8,128)S(1)}, f32[1,4,16,128]{3,2,1,0:T(8,128)}, u32[]{:S(2)}) copy-start(f32[1,4,16,128]{3,2,1,0:T(8,128)} %get-tuple-element.56) | copy-start | bytes 98308
  33.5 27.6 %copy-start.5 = (bf16[18,64,128]{2,1,0:T(8,128)(2,1)S(1)}, bf16[18,64,128]{2,1,0:T(8,128)(2,1)}, u32[]{:S(2)}) copy-start(bf16[18,64,128]{2,1,0:T(8,128)(2,1)} %copy-done.4) | copy-start | bytes 884740
  33.5 27.6 %copy-start.7 = (bf16[18,64,128]{2,1,0:T(8,128)(2,1)S(1)}, bf16[18,64,128]{2,1,0:T(8,128)(2,1)}, u32[]{:S(2)}) copy-start(bf16[18,64,128]{2,1,0:T(8,128)(2,1)} %copy-done.6) | copy-start | bytes 884740
  53.1 8.1 %collective-permute-start.4 = (f32[44,8,128]{2,1,0:T(8,128)S(1)}, f32[44,8,128]{2,1,0:T(8,128)S(1)}, u32[]{:S(2)}, u32[]{:S(2)}) collective-permute-start(f32[44,8,128]{2,1,0:T(8,128)S(1)} %pad_maximum_fusion), channel_id=1, source_target_pairs={{0,16},{16,32},{32,48},{48,0},{1,17},{17,33},{33,49},{49,1},{2,18}... | collective-permute-start | bytes 540680 | tf_op jit(solution)/shard_map/ppermute | solution.py:389
  55.9 5.3 %collective-permute-start.5 = (f32[44,8,128]{2,1,0:T(8,128)S(1)}, f32[44,8,128]{2,1,0:T(8,128)S(1)}, u32[]{:S(2)}, u32[]{:S(2)}) collective-permute-start(f32[44,8,128]{2,1,0:T(8,128)S(1)} %pad_maximum_fusion.1), channel_id=1, source_target_pairs={{16,0},{32,16},{48,32},{0,48},{17,1},{33,17},{49,33},{1,49},{18,2}... | collective-permute-start | bytes 540680 | tf_op jit(solution)/shard_map/ppermute | solution.py:389
  62.3 5.1 %collective-permute-start.6 = (f32[4,64,128]{2,1,0:T(8,128)S(1)}, f32[4,64,128]{2,1,0:T(8,128)S(1)}, u32[]{:S(2)}, u32[]{:S(2)}) collective-permute-start(f32[4,64,128]{2,1,0:T(8,128)S(1)} %get-tuple-element.36), channel_id=1, source_target_pairs={{0,64},{64,128},{128,192},{192,0},{1,65},{65,129},{129,193},{193,1... | collective-permute-start | bytes 393224 | tf_op jit(solution)/shard_map/ppermute | solution.py:389
  63.6 3.9 %collective-permute-start.7 = (f32[4,64,128]{2,1,0:T(8,128)S(1)}, f32[4,64,128]{2,1,0:T(8,128)S(1)}, u32[]{:S(2)}, u32[]{:S(2)}) collective-permute-start(f32[4,64,128]{2,1,0:T(8,128)S(1)} %get-tuple-element.37), channel_id=1, source_target_pairs={{64,0},{128,64},{192,128},{0,192},{65,1},{129,65},{193,129},{1,193... | collective-permute-start | bytes 393224 | tf_op jit(solution)/shard_map/ppermute | solution.py:389
  72.5 4.8 %collective-permute-start.8 = (f32[3,64,128]{2,1,0:T(8,128)S(1)}, f32[3,64,128]{2,1,0:T(8,128)S(1)}, u32[]{:S(2)}, u32[]{:S(2)}) collective-permute-start(f32[3,64,128]{2,1,0:T(8,128)S(1)} %get-tuple-element.43), channel_id=1, source_target_pairs={{0,64},{64,128},{128,192},{192,0},{1,65},{65,129},{129,193},{193,1... | collective-permute-start | bytes 294920 | tf_op jit(solution)/shard_map/ppermute | solution.py:389
  74.1 3.5 %collective-permute-start.9 = (f32[3,64,128]{2,1,0:T(8,128)S(1)}, f32[3,64,128]{2,1,0:T(8,128)S(1)}, u32[]{:S(2)}, u32[]{:S(2)}) collective-permute-start(f32[3,64,128]{2,1,0:T(8,128)S(1)} %get-tuple-element.44), channel_id=1, source_target_pairs={{64,0},{128,64},{192,128},{0,192},{65,1},{129,65},{193,129},{1,193... | collective-permute-start | bytes 294920 | tf_op jit(solution)/shard_map/ppermute | solution.py:389
  77.5 8.7 %copy-start.3 = (bf16[18,64,128]{2,1,0:T(8,128)(2,1)S(1)}, bf16[18,64,128]{2,1,0:T(8,128)(2,1)}, u32[]{:S(2)}) copy-start(bf16[18,64,128]{2,1,0:T(8,128)(2,1)} %copy-done.2) | copy-start | bytes 884740
  78.7 4.5 %collective-permute-start.11 = (f32[2,18,8,128]{3,2,1,0:T(8,128)S(1)}, f32[2,18,8,128]{3,2,1,0:T(8,128)S(1)}, u32[]{:S(2)}, u32[]{:S(2)}) collective-permute-start(f32[2,18,8,128]{3,2,1,0:T(8,128)S(1)} %get-tuple-element.49), channel_id=1, source_target_pairs={{16,0},{32,16},{48,32},{0,48},{17,1},{33,17},{49,33},{1,49},{18,2}... | collective-permute-start | bytes 442376 | tf_op jit(solution)/shard_map/ppermute | solution.py:389
  81.0 5.2 %collective-permute-start.10 = (f32[2,18,8,128]{3,2,1,0:T(8,128)S(1)}, f32[2,18,8,128]{3,2,1,0:T(8,128)S(1)}, u32[]{:S(2)}, u32[]{:S(2)}) collective-permute-start(f32[2,18,8,128]{3,2,1,0:T(8,128)S(1)} %get-tuple-element.50), channel_id=1, source_target_pairs={{0,16},{16,32},{32,48},{48,0},{1,17},{17,33},{33,49},{49,1},{2,18}... | collective-permute-start | bytes 442376 | tf_op jit(solution)/shard_map/ppermute | solution.py:389
  119.0 9.9 %collective-permute-start.12 = (f32[8,9,8,128]{3,2,1,0:T(8,128)S(1)}, f32[8,9,8,128]{3,2,1,0:T(8,128)S(1)}, u32[]{:S(2)}, u32[]{:S(2)}) collective-permute-start(f32[8,9,8,128]{3,2,1,0:T(8,128)S(1)} %get-tuple-element.47), channel_id=1, source_target_pairs={{0,1},{1,0},{2,3},{3,2},{4,5},{5,4},{6,7},{7,6},{8,9},{9,8},{10,11... | collective-permute-start | bytes 884744 | tf_op jit(solution)/shard_map/ppermute | solution.py:399

commit v4 on v3

--- a/solution.py
+++ b/solution.py
@@ -100,18 +100,18 @@
         held[at[s], :] = result[:, s * COLS : (s + 1) * COLS]
 
 
-def levels_of(c, s, t, v):
-    own = c if t == 0 else 1 - c
-    return pl.ds(pl.multiple_of(v * LEVELS * 8 + s * 48 + own * 24, 8), 24)
+def chip_order(c, part, own, mate):
+    return jnp.where(c == part, own, mate)
 
 
 def mix_body(core, got, matrix, out, held):
     c = core[0]
     for v in range(3):
         for s in range(RINGS):
-            for t in range(2):
-                first = t * 9 + v * 3
-                held[levels_of(c, s, t, v), :] = got[s, first : first + 3].reshape(24, COLS)
+            own, mate = got[s, v * 3 : v * 3 + 3], got[s, 9 + v * 3 : 12 + v * 3]
+            for part in range(2):
+                value = chip_order(c, part, own, mate)
+                held[rows_of(v, s * 48 + part * 24, 24), :] = value.reshape(24, COLS)
         mixed(matrix[c * 3 + v], held, v, 1)
         for s in range(RINGS):
             out[s, v * OWN : (v + 1) * OWN] = held[rows_of(v, s * 48, 48), :].reshape(OWN, 8, COLS)
@@ -124,9 +124,10 @@
             held[rows_of(v, s * 48, 48), :] = got[s, v * OWN : (v + 1) * OWN].reshape(48, COLS)
         mixed(matrix[c * 3 + v], held, v, 0)
         for s in range(RINGS):
+            lower, upper = [held[rows_of(v, s * 48 + h * 24, 24), :].reshape(3, 8, COLS) for h in range(2)]
             for t in range(2):
                 first = t * 9 + v * 3
-                part = held[levels_of(c, s, t, v), :].reshape(3, 8, COLS)
+                part = chip_order(c, t, lower, upper)
                 out[s, first : first + 3] = part + control[s, first : first + 3]
 
 
@@ -174,10 +175,23 @@
     return mm(high[p], e_high) + (mm(high[p], e_low) + mm(low[p], e_high))
 
 
+PACKED = 48
+
+
+def unpacked(pack, l, base):
+    block = pack[l // 2 * STRIP : (l // 2 + 1) * STRIP]
+    return jnp.concatenate(
+        [
+            pltpu.roll(pack, (base - STRIP * l) % COLS, 1) if (base - STRIP * l) % COLS else pack,
+            pltpu.roll(block, (base - STRIP * (OWN + l % 2)) % COLS, 1),
+        ],
+        axis=0,
+    )
+
+
 def with_halo(l, field, left, right):
     lane = lax.broadcasted_iota(I32, (ROWS, COLS), 1)
-    left = pltpu.roll(left, (COLS - STRIP - STRIP * l) % COLS, 1)
-    right = pltpu.roll(right, (COLS - STRIP * l) % COLS, 1)
+    left, right = unpacked(left, l, COLS - STRIP), unpacked(right, l, 0)
     halo = jnp.where(lane >= COLS - STRIP, left, jnp.where(lane < STRIP, right, 0.0))
     return split(jnp.concatenate([field, halo], axis=1))
 
@@ -195,13 +209,29 @@
 
 
 def packed(fields):
-    lane = lax.broadcasted_iota(I32, (ROWS, COLS), 1) // STRIP
-    last = jnp.zeros((ROWS, COLS), F32)
-    first = jnp.zeros((ROWS, COLS), F32)
-    for l, field in enumerate(fields):
-        last = jnp.where(lane == l, pltpu.roll(field, STRIP * (l + 1) % COLS, 1), last)
-        first = jnp.where(lane == l, pltpu.roll(field, STRIP * l, 1) if l else field, first)
-    return last, first
+    group = lax.broadcasted_iota(I32, (STRIP, COLS), 1) // STRIP
+
+    def rolled(value, shift):
+        return pltpu.roll(value, shift % COLS, 1) if shift % COLS else value
+
+    packs = []
+    for base in (COLS - STRIP, 0):
+        tops = [rolled(field[:PACKED], STRIP * l - base) for l, field in enumerate(fields)]
+        blocks = []
+        for i in range(PACKED // STRIP):
+            block = tops[0][i * STRIP : (i + 1) * STRIP]
+            for l in range(1, OWN):
+                block = jnp.where(group == l, tops[l][i * STRIP : (i + 1) * STRIP], block)
+            for q in range(2):
+                tail = rolled(fields[2 * i + q][PACKED:], STRIP * (OWN + q) - base)
+                block = jnp.where(group == OWN + q, tail, block)
+            blocks.append(block)
+        packs.append(jnp.concatenate(blocks, axis=0))
+    return packs
+
+
+def rows_at(v):
+    return pl.ds(pl.multiple_of(v * PACKED, 8), PACKED)
 
 
 def lat_body(
@@ -222,7 +252,7 @@
             fields.append(lat_filter(p, rows, *ends, high, low))
         for l in range(OWN):
             out[v * OWN + l] = fields[l]
-        last[v], lead[v] = packed(fields)
+        last[rows_at(v), :], lead[rows_at(v), :] = packed(fields)
         return carry
 
     lax.fori_loop(0, nv, one, 0)
@@ -236,7 +266,7 @@
         if block is None:
             target[...] = came
         else:
-            target[block] = came
+            target[nv * PACKED :, :] = came
 
 
 def back_lat_body(nv, latitude, rows, before, after, high, low, out):
@@ -259,7 +289,7 @@
     def one(v, carry):
         for l in range(OWN):
             p = v * OWN + l
-            value = back_lon_filter(p, l, field[p], left[v], right[v], high, low)
+            value = back_lon_filter(p, l, field[p], left[rows_at(v), :], right[rows_at(v), :], high, low)
             out[:, p] = value.reshape(RINGS, 8, COLS)
         return carry
 
@@ -270,12 +300,14 @@
     nv, field, left, right, own_rows, far_rows, high, low, weight,
     out, last, first, parts, values, misfit_high, misfit_low, row_hot, col_hot, col_hot2,
 ):
-    arrived([own_rows[...], left[nv], far_rows[...], right[nv]], values, row_hot, col_hot, col_hot2)
+    came = pl.ds(nv * PACKED, 4 * PIECE)
+    blocks = [own_rows[...], left[came, :], far_rows[...], right[came, :]]
+    arrived(blocks, values, row_hot, col_hot, col_hot2)
 
     def filtered(v, carry):
         for l in range(OWN):
             p = v * OWN + l
-            third = lon_filter(p, l, field[p], left[v], right[v], high, low)
+            third = lon_filter(p, l, field[p], left[rows_at(v), :], right[rows_at(v), :], high, low)
             t_high, t_low = split(third)
             parts[p] = jnp.concatenate([t_high, t_low], axis=1)
         return carry
@@ -308,13 +340,13 @@
             at = 2 * l * ROWS
             fields.append(both[at : at + ROWS] + both[at + ROWS : at + 2 * ROWS])
             out[v * OWN + l] = fields[-1]
-        last[v], first[v] = packed(fields)
+        last[rows_at(v), :], first[rows_at(v), :] = packed(fields)
         return carry
 
     lax.fori_loop(0, nv, scattered, 0)
 
 
-def route_body(core, longitude, latitude, kept, mate, tile, cell, out, half_way):
+def route_body(core, longitude, latitude, kept, mate, tile, cell, out, by_lon, by_lat, by_both):
     c = core[0]
     count = tile.shape[1]
     east = ((tile[...] >> 2) - longitude[0]) & 3
@@ -350,8 +382,13 @@
             (jnp.where(lane < SLOTS, a2, b), jnp.where(lane < SLOTS, c2, 0.0)),
         )
         for i in range(2):
-            target, at = (out, (e // 2, i)) if e % 2 == 0 else ((half_way, (e // 2,)), (out, (e // 2, 2)))[i]
-            target[(*at, slice(0, 8))], target[(*at, slice(8, 16))] = pair[i]
+            north, east = e // 2, e % 2 * 2 + i
+            y, x = (0, 1, None, 2)[north], (0, 1, None, 2)[east]
+            if x is None:
+                target = by_both if y is None else by_lon.at[y]
+            else:
+                target = by_lat.at[x] if y is None else out.at[y, x]
+            target[0:8], target[8:16] = pair[i]
 
 
 def arrived(blocks, values, row_hot, col_hot, col_hot2):
@@ -389,9 +426,9 @@
     return lax.ppermute(last, axis, up), lax.ppermute(first, axis, down)
 
 
-def across(value, axis):
+def shifted(value, axis, by):
     size = lax.axis_size(axis)
-    return lax.ppermute(value, axis, [(i, (i + 2) % size) for i in range(size)])
+    return lax.ppermute(value, axis, [(i, (i + by) % size) for i in range(size)])
 
 
 def with_mate(value):
@@ -429,15 +466,31 @@
         after=(arranged,),
     )
     mate_small = with_mate(sent_small)
-    routed, half_way = kernel_call(
+    routed, by_lon, by_lat, by_both = kernel_call(
         route_body,
-        [shape(4, 3, PIECE, COLS), shape(4, PIECE, COLS)],
+        [shape(3, 3, PIECE, COLS), shape(3, PIECE, COLS), shape(3, PIECE, COLS), shape(PIECE, COLS)],
         [core, longitude, latitude, kept_small, mate_small, obs_tile.reshape(1, -1), obs_cell.reshape(1, -1)],
         smem=(0, 1, 2),
         flops=2 * 72 * slots * obs_tile.shape[0],
     )
-    pieces = jnp.concatenate([routed, across(half_way, "lon")[:, None]], axis=1)
-    far = across(pieces[2], "lat")
+    n_lon, n_lat = lax.axis_size("lon"), lax.axis_size("lat")
+    opposite = [
+        (x * n_lat + y, (x + 2) % n_lon * n_lat + (y + 2) % n_lat)
+        for x in range(n_lon)
+        for y in range(n_lat)
+    ]
+    by_lon, by_lat = shifted(by_lon, "lon", 2), shifted(by_lat, "lat", 2)
+    by_both = lax.ppermute(by_both, ("lon", "lat"), opposite)
+    near, up, down = [jnp.concatenate([routed[i], by_lon[i : i + 1]], axis=0) for i in range(3)]
+    far = jnp.concatenate([by_lat, by_both[None]], axis=0)
+    first = over_rings(column_call(mix_body, core, columns, vertical, after=(far, near, up, down)))
+
+    def with_rows(strips, rows):
+        return jnp.concatenate([strips.reshape(-1, 8, COLS), rows.reshape(-1, 8, COLS)], axis=0)
+
+    before, after = exchanged(
+        with_rows(first[6:8], up), with_rows(first[0:2], down), "lat"
+    )
     high, low, back_high, back_low, lon_high, lon_low, weight = kernel_call(
         bands_body,
         [shape(planes, ROWS, 128, dtype=BF16)] * 4
@@ -446,27 +499,21 @@
         [core, kept_small, mate_small],
         smem=(0,),
         flops=planes * 200000,
-    )
-    first = over_rings(column_call(mix_body, core, columns, vertical, after=(far, weight)))
-
-    def with_rows(strips, rows):
-        return jnp.concatenate([strips.reshape(-1, 8, COLS), rows.reshape(-1, 8, COLS)], axis=0)
-
-    before, after = exchanged(
-        with_rows(first[6:8], pieces[1]), with_rows(first[0:2], pieces[3]), "lat"
+        after=(first,),
     )
     field_shape = shape(planes, ROWS, COLS)
     lat_flops = 2 * 3 * planes * ROWS * 128 * COLS
     row_block = shape(4 * PIECE, COLS)
+    pack_rows = shape(nv * PACKED + 4 * PIECE, COLS)
     field, last, lead, own_rows, far_rows = kernel_call(
         functools.partial(lat_body, nv),
-        [field_shape] + [shape(nv + 1, ROWS, COLS)] * 2 + [row_block] * 2,
-        [latitude, first, before, after, pieces[0], far, high, low],
+        [field_shape, pack_rows, pack_rows, row_block, row_block],
+        [latitude, first, before, after, near, far, high, low],
         smem=(0,),
         flops=lat_flops,
     )
     left, right = exchanged(last, lead, "lon")
-    pack_shape = shape(nv, ROWS, COLS)
+    pack_shape = shape(nv * PACKED, COLS)
     placed, last, lead = kernel_call(
         functools.partial(observe_body, nv),
         [field_shape, pack_shape, pack_shape],

time: 130 us -> 129 us (level)
  local copies, waits for them, and re-layouts: 3.34 us -> 1.18 us
  waiting for transfers between devices: 22.9 us -> 24.7 us
  blocking collectives: 50.2 us -> 51.8 us
  starting transfers between devices: 37.7 us -> 36.3 us
    ppermute x2 -> x3, waiting for transfers between devices: 1.82 us -> 4.14 us  [the longest x2 4.14 us: shifted(): lax.ppermute(value, axis, [(i, (i + by) % size) for i in range(size)])]
    unnamed x32 -> x16, local copies, waits for them, and re-layouts: 3.26 us -> 1.09 us
    ppermute x8, waiting for transfers between devices: 13.1 us -> 11 us  [exchanged(): return (lax.ppermute(last, axis, up), lax.ppermute(first, axis, down))]
    all_to_all x1, waiting for transfers between devices: 4.67 us -> 6.31 us  [over_rings(): lax.all_to_all(value, 'lev', 0, 0, tiled=True, axis_index_groups=groups)]
    all_to_all x3, blocking collectives: 50.2 us -> 51.8 us  [over_rings(): lax.all_to_all(value, 'lev', 0, 0, tiled=True, axis_index_groups=groups)]
    ppermute x8, starting transfers between devices: 12.6 us -> 11.1 us  [exchanged(): return (lax.ppermute(last, axis, up), lax.ppermute(first, axis, down))]
    ppermute x2 -> x3, starting transfers between devices: 5.74 us -> 5.85 us  [the longest x1 5.46 us: local(): by_both = lax.ppermute(by_both, ('lon', 'lat'), opposite)]
  transfers between devices with their start and end apart: 14 -> 15, of which waited for: 11 -> 10; matrix products, arithmetic and copies ran while one was open for 0% -> 0% of each run, Pallas kernels for 2% -> 2%
where the time goes in v4:
time: 129 us; the launch traced here: 128 us
  blocking collectives  51.8 us (40%)
  starting transfers between devices  36.3 us (28%)
  waiting for transfers between devices  24.7 us (19%)
  Pallas kernels  14.1 us (11%)
    all_to_all x3, blocking collectives, over_rings(): lax.all_to_all(value, 'lev', 0, 0, tiled=True, axis_index_groups=groups)  51.8 us
    pallas_call x12, Pallas kernels, kernel_call(): pl.pallas_call(lambda *refs: body(*refs[count:]), out_shape=list(outs), i...  14.1 us
    ppermute x3, starting transfers between devices, with_mate(): return lax.ppermute(value, 'lev', pairs)  12.7 us
    ppermute x8, starting transfers between devices, exchanged(): return (lax.ppermute(last, axis, up), lax.ppermute(first, axis, down))  11.1 us
    ppermute x8, waiting for transfers between devices, exchanged(): return (lax.ppermute(last, axis, up), lax.ppermute(first, axis, down))  11 us
    all_to_all x1, starting transfers between devices, over_rings(): lax.all_to_all(value, 'lev', 0, 0, tiled=True, axis_index_groups=groups)  6.58 us
    all_to_all x1, waiting for transfers between devices, over_rings(): lax.all_to_all(value, 'lev', 0, 0, tiled=True, axis_index_groups=groups)  6.31 us
    ppermute x1, starting transfers between devices, local(): by_both = lax.ppermute(by_both, ('lon', 'lat'), opposite)  5.46 us
  transfers between devices with their start and end apart: 15, of which 10 were waited for; matrix products, arithmetic and copies ran while one was open for 0% of the time, Pallas kernels for 2%

profile of v4, /device:TPU:1, one launch (start us, length us, event | category | flops | bytes accessed | tf_op | source)
XLA Modules:
  0.0 128.3 jit_solution(11605644394785754981)
XLA Ops:
  0.0 1.1 copy-done.1
  1.1 3.3 %collective-permute-start = (f32[9,64,128]{2,1,0:T(8,128)S(1)}, f32[9,64,128]{2,1,0:T(8,128)S(1)}, u32[]{:S(2)}, u32[]{:S(2)}) collective-permute-start(f32[9,64,128]{2,1,0:T(8,128)S(1)} %get-tuple-element.29), channel_id=1, source_target_pairs={{0,1},{1,0},{2,3},{3,2},{4,5},{5,4},{6,7},{7,6},{8,9},{9,8},{10,11... | collective-permute-start | bytes 884744 | tf_op jit(solution)/shard_map/ppermute | solution.py:436
  4.4 1.2 collective-permute-done.refs_1_
  5.7 0.9 shard_map.83.refs_0_
  6.5 6.6 %all-to-all-start = ((f32[8,18,8,128]{3,2,1,0:T(8,128)}), f32[8,18,8,128]{3,2,1,0:T(8,128)S(1)}, u32[]{:S(2)}, u32[]{:S(2)}) async-start(f32[8,18,8,128]{3,2,1,0:T(8,128)} %shard_map.83.refs_0_), calls=%async_computation | async-start | bytes 1179648 | tf_op jit(solution)/shard_map/all_to_all | solution.py:442
  14.5 0.9 collective-permute-done.1.refs_4_.refs_3_
  16.1 5.5 %collective-permute-start.3 = (f32[16,128]{1,0:T(8,128)S(1)}, f32[16,128]{1,0:T(8,128)S(1)}, u32[]{:S(2)}, u32[]{:S(2)}) collective-permute-start(f32[16,128]{1,0:T(8,128)S(1)} %get-tuple-element.33), channel_id=1, source_target_pairs={{0,160},{16,176},{32,128},{48,144},{64,224},{80,240},{96,192},{112... | collective-permute-start | bytes 24584 | tf_op jit(solution)/shard_map/ppermute | solution.py:483
  22.0 4.1 %collective-permute-done.4 = f32[3,16,128]{2,1,0:T(8,128)S(1)} collective-permute-done((f32[3,16,128]{2,1,0:T(8,128)S(1)}, f32[3,16,128]{2,1,0:T(8,128)S(1)}, u32[]{:S(2)}, u32[]{:S(2)}) %collective-permute-start.4) | collective-permute-done | bytes 24608 | tf_op jit(solution)/shard_map/ppermute | solution.py:431
  26.1 6.3 %all-to-all-done.refs_5_.refs_3_ = f32[8,18,8,128]{3,2,1,0:T(8,128)S(1)} async-done(((f32[8,18,8,128]{3,2,1,0:T(8,128)}), f32[8,18,8,128]{3,2,1,0:T(8,128)S(1)}, u32[]{:S(2)}, u32[]{:S(2)}) %all-to-all-start) | async-done | bytes 589856 | tf_op jit(solution)/shard_map/all_to_all | solution.py:442
  33.2 21.1 %all_to_all.20.refs_0_.refs_1_ = f32[8,18,8,128]{3,2,1,0:T(8,128)S(1)} all-to-all(f32[8,18,8,128]{3,2,1,0:T(8,128)S(1)} %shard_map.86), channel_id=1, replica_groups={{0,2,4,6,8,10,12,14},{1,3,5,7,9,11,13,15},{16,18,20,22,24,26,28,30},{17..., dimensions={0} | all-to-all | bytes 1179648 | tf_op jit(solution)/shard_map/all_to_all | solution.py:442
  54.3 1.4 %collective-permute-start.5 = (f32[44,8,128]{2,1,0:T(8,128)S(1)}, f32[44,8,128]{2,1,0:T(8,128)S(1)}, u32[]{:S(2)}, u32[]{:S(2)}) collective-permute-start(f32[44,8,128]{2,1,0:T(8,128)S(1)} %pad_maximum_fusion), channel_id=1, source_target_pairs={{0,16},{16,32},{32,48},{48,0},{1,17},{17,33},{33,49},{49,1},{2,18}... | collective-permute-start | bytes 540680 | tf_op jit(solution)/shard_map/ppermute | solution.py:426
  55.7 1.5 %collective-permute-start.6 = (f32[44,8,128]{2,1,0:T(8,128)S(1)}, f32[44,8,128]{2,1,0:T(8,128)S(1)}, u32[]{:S(2)}, u32[]{:S(2)}) collective-permute-start(f32[44,8,128]{2,1,0:T(8,128)S(1)} %pad_maximum_fusion.1), channel_id=1, source_target_pairs={{16,0},{32,16},{48,32},{0,48},{17,1},{33,17},{49,33},{1,49},{18,2}... | collective-permute-start | bytes 540680 | tf_op jit(solution)/shard_map/ppermute | solution.py:426
  57.2 1.3 %shard_map.87 = (bf16[18,64,128]{2,1,0:T(8,128)(2,1)S(1)}, bf16[18,64,128]{2,1,0:T(8,128)(2,1)S(1)}, bf16[18,64,128]{2,1,0:T(8,128)(2,1)S(1)}, bf16[18,64,128]{2...) custom-call(f32[8,18,8,128]{3,2,1,0:T(8,128)S(1)} %all_to_all.20.ref, ...), custom_call_target="tpu_custom_call" | custom-call | flops 3600000 | bytes 3612676 | tf_op jit(solution)/shard_map/pallas_call | solution.py:30
  58.6 2.0 %collective-permute-done.5.refs_2_ = f32[44,8,128]{2,1,0:T(8,128)S(1)} collective-permute-done((f32[44,8,128]{2,1,0:T(8,128)S(1)}, f32[44,8,128]{2,1,0:T(8,128)S(1)}, u32[]{:S(2)}, u32[]{:S(2)}) %collective-permute-start.5) | collective-permute-done | bytes 180256 | tf_op jit(solution)/shard_map/ppermute | solution.py:426
  60.6 1.2 shard_map.88
  61.8 1.3 %collective-permute-start.7 = (f32[208,128]{1,0:T(8,128)S(1)}, f32[208,128]{1,0:T(8,128)S(1)}, u32[]{:S(2)}, u32[]{:S(2)}) collective-permute-start(f32[208,128]{1,0:T(8,128)S(1)} %get-tuple-element.39), channel_id=1, source_target_pairs={{0,64},{64,128},{128,192},{192,0},{1,65},{65,129},{129,193},{193,1... | collective-permute-start | bytes 319496 | tf_op jit(solution)/shard_map/ppermute | solution.py:426
  63.1 1.5 %collective-permute-start.8 = (f32[208,128]{1,0:T(8,128)S(1)}, f32[208,128]{1,0:T(8,128)S(1)}, u32[]{:S(2)}, u32[]{:S(2)}) collective-permute-start(f32[208,128]{1,0:T(8,128)S(1)} %get-tuple-element.40), channel_id=1, source_target_pairs={{64,0},{128,64},{192,128},{0,192},{65,1},{129,65},{193,129},{1,193... | collective-permute-start | bytes 319496 | tf_op jit(solution)/shard_map/ppermute | solution.py:426
  64.5 2.1 %collective-permute-done.7.refs_1_ = f32[208,128]{1,0:T(8,128)S(1)} collective-permute-done((f32[208,128]{1,0:T(8,128)S(1)}, f32[208,128]{1,0:T(8,128)S(1)}, u32[]{:S(2)}, u32[]{:S(2)}) %collective-permute-start.7) | collective-permute-done | bytes 106528 | tf_op jit(solution)/shard_map/ppermute | solution.py:426
  66.6 5.1 %shard_map.89 = (f32[18,64,128]{2,1,0:T(8,128)S(1)}, f32[144,128]{1,0:T(8,128)S(1)}, f32[144,128]{1,0:T(8,128)S(1)}) custom-call(f32[18,64,128]{2,1,0:T(8,128)S(1)} %get-tuple-element.38.refs_0_, f32[208,128]{1,0:T(8,128)S(1)} %collective-permute-done.7.refs_1_, f32[208,128]{1,0:T(8,128)S(1)} %collective-permute-done.8.refs_2_, ...), custom_call_target="tpu_custom_call" | custom-call | flops 1207959552 | bytes 3974144 | tf_op jit(solution)/shard_map/pallas_call | solution.py:30
  71.7 1.3 collective-permute-start.9
  73.0 1.6 %collective-permute-start.10 = (f32[144,128]{1,0:T(8,128)S(1)}, f32[144,128]{1,0:T(8,128)S(1)}, u32[]{:S(2)}, u32[]{:S(2)}) collective-permute-start(f32[144,128]{1,0:T(8,128)S(1)} %get-tuple-element.48), channel_id=1, source_target_pairs={{64,0},{128,64},{192,128},{0,192},{65,1},{129,65},{193,129},{1,193... | collective-permute-start | bytes 221192 | tf_op jit(solution)/shard_map/ppermute | solution.py:426
  74.6 1.7 %collective-permute-done.9.refs_1_ = f32[144,128]{1,0:T(8,128)S(1)} collective-permute-done((f32[144,128]{1,0:T(8,128)S(1)}, f32[144,128]{1,0:T(8,128)S(1)}, u32[]{:S(2)}, u32[]{:S(2)}) %collective-permute-start.9) | collective-permute-done | bytes 73760 | tf_op jit(solution)/shard_map/ppermute | solution.py:426
  76.2 1.1 shard_map.90.refs_1_
  77.4 2.6 %collective-permute-start.12 = (f32[2,18,8,128]{3,2,1,0:T(8,128)S(1)}, f32[2,18,8,128]{3,2,1,0:T(8,128)S(1)}, u32[]{:S(2)}, u32[]{:S(2)}) collective-permute-start(f32[2,18,8,128]{3,2,1,0:T(8,128)S(1)} %get-tuple-element.53), channel_id=1, source_target_pairs={{16,0},{32,16},{48,32},{0,48},{17,1},{33,17},{49,33},{1,49},{18,2}... | collective-permute-start | bytes 442376 | tf_op jit(solution)/shard_map/ppermute | solution.py:426
  80.0 2.1 %collective-permute-done.12.refs_3_ = f32[2,18,8,128]{3,2,1,0:T(8,128)S(1)} collective-permute-done((f32[2,18,8,128]{3,2,1,0:T(8,128)S(1)}, f32[2,18,8,128]{3,2,1,0:T(8,128)S(1)}, u32[]{:S(2)}, u32[]{:S(2)}) %collective-permute-start.12) | collective-permute-done | bytes 147488 | tf_op jit(solution)/shard_map/ppermute | solution.py:426
  82.1 3.1 %collective-permute-done.11.refs_2_ = f32[2,18,8,128]{3,2,1,0:T(8,128)S(1)} collective-permute-done((f32[2,18,8,128]{3,2,1,0:T(8,128)S(1)}, f32[2,18,8,128]{3,2,1,0:T(8,128)S(1)}, u32[]{:S(2)}, u32[]{:S(2)}) %collective-permute-start.11) | collective-permute-done | bytes 147488 | tf_op jit(solution)/shard_map/ppermute | solution.py:426
  85.2 0.9 shard_map.91
  86.1 15.3 %all_to_all.21.refs_1_ = f32[8,18,8,128]{3,2,1,0:T(8,128)S(1)} all-to-all(f32[8,18,8,128]{3,2,1,0:T(8,128)S(1)} %shard_map.91), channel_id=1, replica_groups={{0,2,4,6,8,10,12,14},{1,3,5,7,9,11,13,15},{16,18,20,22,24,26,28,30},{17..., dimensions={0} | all-to-all | bytes 1179648 | tf_op jit(solution)/shard_map/all_to_all | solution.py:442
  102.2 15.3 %all_to_all.22 = f32[8,18,8,128]{3,2,1,0:T(8,128)S(1)} all-to-all(f32[8,18,8,128]{3,2,1,0:T(8,128)S(1)} %shard_map.92), channel_id=1, replica_groups={{0,2,4,6,8,10,12,14},{1,3,5,7,9,11,13,15},{16,18,20,22,24,26,28,30},{17..., dimensions={0} | all-to-all | bytes 1179648 | tf_op jit(solution)/shard_map/all_to_all | solution.py:442
  117.5 8.7 %collective-permute-start.13 = (f32[8,9,8,128]{3,2,1,0:T(8,128)S(1)}, f32[8,9,8,128]{3,2,1,0:T(8,128)S(1)}, u32[]{:S(2)}, u32[]{:S(2)}) collective-permute-start(f32[8,9,8,128]{3,2,1,0:T(8,128)S(1)} %get-tuple-element.51), channel_id=1, source_target_pairs={{0,1},{1,0},{2,3},{3,2},{4,5},{5,4},{6,7},{7,6},{8,9},{9,8},{10,11... | collective-permute-start | bytes 884744 | tf_op jit(solution)/shard_map/ppermute | solution.py:436
  126.2 1.2 collective-permute-done.13.refs_2_
  127.4 0.9 shard_map.93
  (39 shorter events, 4.1 us)
Async XLA Ops:
  0.0 1.1 copy-start.1
  1.1 4.5 %collective-permute-start = (f32[9,64,128]{2,1,0:T(8,128)S(1)}, f32[9,64,128]{2,1,0:T(8,128)S(1)}, u32[]{:S(2)}, u32[]{:S(2)}) collective-permute-start(f32[9,64,128]{2,1,0:T(8,128)S(1)} %get-tuple-element.29), channel_id=1, source_target_pairs={{0,1},{1,0},{2,3},{3,2},{4,5},{5,4},{6,7},{7,6},{8,9},{9,8},{10,11... | collective-permute-start | bytes 884744 | tf_op jit(solution)/shard_map/ppermute | solution.py:436
  5.6 7.5 %copy-start.2 = (f32[6,3,512]{2,1,0:T(4,128)S(1)}, f32[6,3,512]{2,1,0:T(4,128)}, u32[]{:S(2)}) copy-start(f32[6,3,512]{2,1,0:T(4,128)} %refs_2_.2) | copy-start | bytes 110596
  5.6 7.5 %copy-start.3 = (f32[6,3,31]{2,1,0:T(4,128)S(1)}, f32[6,3,31]{2,1,0:T(4,128)}, u32[]{:S(2)}) copy-start(f32[6,3,31]{2,1,0:T(4,128)} %refs_3_.1) | copy-start | bytes 6700
  5.6 7.5 %copy-start.4 = (f32[6,3,31]{2,1,0:T(4,128)S(1)}, f32[6,3,31]{2,1,0:T(4,128)}, u32[]{:S(2)}) copy-start(f32[6,3,31]{2,1,0:T(4,128)} %refs_4_.1) | copy-start | bytes 6700
  5.7 7.5 %copy-start.5 = (f32[6,3]{0,1:T(4,128)S(1)}, f32[6,3]{0,1:T(4,128)}, u32[]{:S(2)}) copy-start(f32[6,3]{0,1:T(4,128)} %param.13) | copy-start | bytes 220
  6.5 8.8 %copy-start.6 = (s32[512]{0:T(512)S(1)}, s32[512]{0:T(512)}, u32[]{:S(2)}) copy-start(s32[512]{0:T(512)} %param.14) | copy-start | bytes 6148
  6.5 8.8 %copy-start.7 = (s32[512]{0:T(512)S(1)}, s32[512]{0:T(512)}, u32[]{:S(2)}) copy-start(s32[512]{0:T(512)} %param.15) | copy-start | bytes 6148
  6.5 25.9 %copy-start = (f32[6,48,48]{2,1,0:T(8,128)S(1)}, f32[6,48,48]{2,1,0:T(8,128)}, u32[]{:S(2)}) copy-start(f32[6,48,48]{2,1,0:T(8,128)} %refs_2_.3) | copy-start | bytes 165892
  6.5 25.9 %all-to-all-start = ((f32[8,18,8,128]{3,2,1,0:T(8,128)}), f32[8,18,8,128]{3,2,1,0:T(8,128)S(1)}, u32[]{:S(2)}, u32[]{:S(2)}) async-start(f32[8,18,8,128]{3,2,1,0:T(8,128)} %shard_map.83.refs_0_), calls=%async_computation | async-start | bytes 1179648 | tf_op jit(solution)/shard_map/all_to_all | solution.py:442
  13.7 1.6 %collective-permute-start.1 = (f32[9,1,896]{2,1,0:T(1,128)S(1)}, f32[9,1,896]{2,1,0:T(1,128)S(1)}, u32[]{:S(2)}, u32[]{:S(2)}) collective-permute-start(f32[9,1,896]{2,1,0:T(1,128)S(1)} %get-tuple-element.31), channel_id=1, source_target_pairs={{0,1},{1,0},{2,3},{3,2},{4,5},{5,4},{6,7},{7,6},{8,9},{9,8},{10,11... | collective-permute-start | bytes 96776 | tf_op jit(solution)/shard_map/ppermute | solution.py:436
  16.1 10.0 %collective-permute-start.3 = (f32[16,128]{1,0:T(8,128)S(1)}, f32[16,128]{1,0:T(8,128)S(1)}, u32[]{:S(2)}, u32[]{:S(2)}) collective-permute-start(f32[16,128]{1,0:T(8,128)S(1)} %get-tuple-element.33), channel_id=1, source_target_pairs={{0,160},{16,176},{32,128},{48,144},{64,224},{80,240},{96,192},{112... | collective-permute-start | bytes 24584 | tf_op jit(solution)/shard_map/ppermute | solution.py:483
  21.6 4.5 %collective-permute-start.2 = (f32[3,16,128]{2,1,0:T(8,128)S(1)}, f32[3,16,128]{2,1,0:T(8,128)S(1)}, u32[]{:S(2)}, u32[]{:S(2)}) collective-permute-start(f32[3,16,128]{2,1,0:T(8,128)S(1)} %get-tuple-element.32), channel_id=1, source_target_pairs={{0,32},{16,48},{32,0},{48,16},{1,33},{17,49},{33,1},{49,17},{2,34}... | collective-permute-start | bytes 73736 | tf_op jit(solution)/shard_map/ppermute | solution.py:431
  21.6 4.5 %collective-permute-start.4 = (f32[3,16,128]{2,1,0:T(8,128)S(1)}, f32[3,16,128]{2,1,0:T(8,128)S(1)}, u32[]{:S(2)}, u32[]{:S(2)}) collective-permute-start(f32[3,16,128]{2,1,0:T(8,128)S(1)} %get-tuple-element.35), channel_id=1, source_target_pairs={{0,128},{64,192},{128,0},{192,64},{1,129},{65,193},{129,1},{193,65... | collective-permute-start | bytes 73736 | tf_op jit(solution)/shard_map/ppermute | solution.py:431
  54.3 6.3 %collective-permute-start.5 = (f32[44,8,128]{2,1,0:T(8,128)S(1)}, f32[44,8,128]{2,1,0:T(8,128)S(1)}, u32[]{:S(2)}, u32[]{:S(2)}) collective-permute-start(f32[44,8,128]{2,1,0:T(8,128)S(1)} %pad_maximum_fusion), channel_id=1, source_target_pairs={{0,16},{16,32},{32,48},{48,0},{1,17},{17,33},{33,49},{49,1},{2,18}... | collective-permute-start | bytes 540680 | tf_op jit(solution)/shard_map/ppermute | solution.py:426
  55.7 4.9 %collective-permute-start.6 = (f32[44,8,128]{2,1,0:T(8,128)S(1)}, f32[44,8,128]{2,1,0:T(8,128)S(1)}, u32[]{:S(2)}, u32[]{:S(2)}) collective-permute-start(f32[44,8,128]{2,1,0:T(8,128)S(1)} %pad_maximum_fusion.1), channel_id=1, source_target_pairs={{16,0},{32,16},{48,32},{0,48},{17,1},{33,17},{49,33},{1,49},{18,2}... | collective-permute-start | bytes 540680 | tf_op jit(solution)/shard_map/ppermute | solution.py:426
  61.8 4.8 %collective-permute-start.7 = (f32[208,128]{1,0:T(8,128)S(1)}, f32[208,128]{1,0:T(8,128)S(1)}, u32[]{:S(2)}, u32[]{:S(2)}) collective-permute-start(f32[208,128]{1,0:T(8,128)S(1)} %get-tuple-element.39), channel_id=1, source_target_pairs={{0,64},{64,128},{128,192},{192,0},{1,65},{65,129},{129,193},{193,1... | collective-permute-start | bytes 319496 | tf_op jit(solution)/shard_map/ppermute | solution.py:426
  63.1 3.6 %collective-permute-start.8 = (f32[208,128]{1,0:T(8,128)S(1)}, f32[208,128]{1,0:T(8,128)S(1)}, u32[]{:S(2)}, u32[]{:S(2)}) collective-permute-start(f32[208,128]{1,0:T(8,128)S(1)} %get-tuple-element.40), channel_id=1, source_target_pairs={{64,0},{128,64},{192,128},{0,192},{65,1},{129,65},{193,129},{1,193... | collective-permute-start | bytes 319496 | tf_op jit(solution)/shard_map/ppermute | solution.py:426
  71.7 4.5 %collective-permute-start.9 = (f32[144,128]{1,0:T(8,128)S(1)}, f32[144,128]{1,0:T(8,128)S(1)}, u32[]{:S(2)}, u32[]{:S(2)}) collective-permute-start(f32[144,128]{1,0:T(8,128)S(1)} %get-tuple-element.47), channel_id=1, source_target_pairs={{0,64},{64,128},{128,192},{192,0},{1,65},{65,129},{129,193},{193,1... | collective-permute-start | bytes 221192 | tf_op jit(solution)/shard_map/ppermute | solution.py:426
  73.0 3.2 %collective-permute-start.10 = (f32[144,128]{1,0:T(8,128)S(1)}, f32[144,128]{1,0:T(8,128)S(1)}, u32[]{:S(2)}, u32[]{:S(2)}) collective-permute-start(f32[144,128]{1,0:T(8,128)S(1)} %get-tuple-element.48), channel_id=1, source_target_pairs={{64,0},{128,64},{192,128},{0,192},{65,1},{129,65},{193,129},{1,193... | collective-permute-start | bytes 221192 | tf_op jit(solution)/shard_map/ppermute | solution.py:426
  77.4 4.7 %collective-permute-start.12 = (f32[2,18,8,128]{3,2,1,0:T(8,128)S(1)}, f32[2,18,8,128]{3,2,1,0:T(8,128)S(1)}, u32[]{:S(2)}, u32[]{:S(2)}) collective-permute-start(f32[2,18,8,128]{3,2,1,0:T(8,128)S(1)} %get-tuple-element.53), channel_id=1, source_target_pairs={{16,0},{32,16},{48,32},{0,48},{17,1},{33,17},{49,33},{1,49},{18,2}... | collective-permute-start | bytes 442376 | tf_op jit(solution)/shard_map/ppermute | solution.py:426
  80.0 5.2 %collective-permute-start.11 = (f32[2,18,8,128]{3,2,1,0:T(8,128)S(1)}, f32[2,18,8,128]{3,2,1,0:T(8,128)S(1)}, u32[]{:S(2)}, u32[]{:S(2)}) collective-permute-start(f32[2,18,8,128]{3,2,1,0:T(8,128)S(1)} %get-tuple-element.54), channel_id=1, source_target_pairs={{0,16},{16,32},{32,48},{48,0},{1,17},{17,33},{33,49},{49,1},{2,18}... | collective-permute-start | bytes 442376 | tf_op jit(solution)/shard_map/ppermute | solution.py:426
  117.5 9.9 %collective-permute-start.13 = (f32[8,9,8,128]{3,2,1,0:T(8,128)S(1)}, f32[8,9,8,128]{3,2,1,0:T(8,128)S(1)}, u32[]{:S(2)}, u32[]{:S(2)}) collective-permute-start(f32[8,9,8,128]{3,2,1,0:T(8,128)S(1)} %get-tuple-element.51), channel_id=1, source_target_pairs={{0,1},{1,0},{2,3},{3,2},{4,5},{5,4},{6,7},{7,6},{8,9},{9,8},{10,11... | collective-permute-start | bytes 884744 | tf_op jit(solution)/shard_map/ppermute | solution.py:436

commit v5 on v4

--- a/solution.py
+++ b/solution.py
@@ -164,7 +164,7 @@
                 weight[p] = row[:, WEIGHT_AT:]
         return carry
 
-    lax.fori_loop(0, 3, one, 0)
+    lax.fori_loop(0, 3, one, 0, unroll=True)
 
 
 def lat_filter(p, rows, before, after, high, low):
@@ -255,7 +255,7 @@
         last[rows_at(v), :], lead[rows_at(v), :] = packed(fields)
         return carry
 
-    lax.fori_loop(0, nv, one, 0)
+    lax.fori_loop(0, nv, one, 0, unroll=True)
     for d, (target, block) in enumerate(((own_rows, None), (last, nv), (lead, nv), (far_rows, None))):
         first = 2 * planes + 2 * d
         came = jnp.concatenate(
@@ -282,7 +282,7 @@
             out[:, p] = lat_filter(p, rows, *ends, high, low).reshape(RINGS, 8, COLS)
         return carry
 
-    lax.fori_loop(0, nv, one, 0)
+    lax.fori_loop(0, nv, one, 0, unroll=True)
 
 
 def back_lon_body(nv, field, left, right, high, low, out):
@@ -293,7 +293,7 @@
             out[:, p] = value.reshape(RINGS, 8, COLS)
         return carry
 
-    lax.fori_loop(0, nv, one, 0)
+    lax.fori_loop(0, nv, one, 0, unroll=True)
 
 
 def observe_body(
@@ -312,7 +312,7 @@
             parts[p] = jnp.concatenate([t_high, t_low], axis=1)
         return carry
 
-    lax.fori_loop(0, nv, filtered, 0)
+    lax.fori_loop(0, nv, filtered, 0, unroll=True)
 
     def gathered(v, carry):
         block = parts[pl.ds(v * OWN, OWN)].reshape(OWN * ROWS, 2 * COLS)
@@ -326,7 +326,7 @@
             misfit_low[p] = m_low.astype(F32)
         return carry
 
-    lax.fori_loop(0, nv, gathered, 0)
+    lax.fori_loop(0, nv, gathered, 0, unroll=True)
 
     def scattered(v, carry):
         placed = []
@@ -343,7 +343,7 @@
         last[rows_at(v), :], first[rows_at(v), :] = packed(fields)
         return carry
 
-    lax.fori_loop(0, nv, scattered, 0)
+    lax.fori_loop(0, nv, scattered, 0, unroll=True)
 
 
 def route_body(core, longitude, latitude, kept, mate, tile, cell, out, by_lon, by_lat, by_both):

time: 129 us -> 126 us (0.977)
  Pallas kernels: 14.1 us -> 11.1 us
    pallas_call x12, Pallas kernels: 14.1 us -> 11.1 us  [kernel_call(): pl.pallas_call(lambda *refs: body(*refs[count:]), out_shape=list(outs), i...]
where the time goes in v5:
time: 126 us
  blocking collectives  51.9 us (41%)
  starting transfers between devices  36.4 us (29%)
  waiting for transfers between devices  25 us (20%)
  Pallas kernels  11.1 us (9%)
    all_to_all x3, blocking collectives, over_rings(): lax.all_to_all(value, 'lev', 0, 0, tiled=True, axis_index_groups=groups)  51.9 us
    ppermute x3, starting transfers between devices, with_mate(): return lax.ppermute(value, 'lev', pairs)  12.7 us
    ppermute x8, starting transfers between devices, exchanged(): return (lax.ppermute(last, axis, up), lax.ppermute(first, axis, down))  11.3 us
    ppermute x8, waiting for transfers between devices, exchanged(): return (lax.ppermute(last, axis, up), lax.ppermute(first, axis, down))  11.3 us
    pallas_call x12, Pallas kernels, kernel_call(): pl.pallas_call(lambda *refs: body(*refs[count:]), out_shape=list(outs), i...  11.1 us
    all_to_all x1, starting transfers between devices, over_rings(): lax.all_to_all(value, 'lev', 0, 0, tiled=True, axis_index_groups=groups)  6.58 us
    all_to_all x1, waiting for transfers between devices, over_rings(): lax.all_to_all(value, 'lev', 0, 0, tiled=True, axis_index_groups=groups)  6.31 us
    ppermute x1, starting transfers between devices, local(): by_both = lax.ppermute(by_both, ('lon', 'lat'), opposite)  5.46 us
  transfers between devices with their start and end apart: 15, of which 10 were waited for; matrix products, arithmetic and copies ran while one was open for 0% of the time, Pallas kernels for 2%

profile of v5, /device:TPU:1, one launch (start us, length us, event | category | flops | bytes accessed | tf_op | source)
XLA Modules:
  0.0 125.7 jit_solution(13916389058317833368)
XLA Ops:
  0.0 1.1 copy-done.1
  1.1 3.3 %collective-permute-start = (f32[9,64,128]{2,1,0:T(8,128)S(1)}, f32[9,64,128]{2,1,0:T(8,128)S(1)}, u32[]{:S(2)}, u32[]{:S(2)}) collective-permute-start(f32[9,64,128]{2,1,0:T(8,128)S(1)} %get-tuple-element.29), channel_id=1, source_target_pairs={{0,1},{1,0},{2,3},{3,2},{4,5},{5,4},{6,7},{7,6},{8,9},{9,8},{10,11... | collective-permute-start | bytes 884744 | tf_op jit(solution)/shard_map/ppermute | solution.py:436
  4.4 1.2 collective-permute-done.refs_1_
  5.7 0.9 shard_map.83.refs_0_
  6.5 6.6 %all-to-all-start = ((f32[8,18,8,128]{3,2,1,0:T(8,128)}), f32[8,18,8,128]{3,2,1,0:T(8,128)S(1)}, u32[]{:S(2)}, u32[]{:S(2)}) async-start(f32[8,18,8,128]{3,2,1,0:T(8,128)} %shard_map.83.refs_0_), calls=%async_computation | async-start | bytes 1179648 | tf_op jit(solution)/shard_map/all_to_all | solution.py:442
  13.7 0.7 collective-permute-start.1
  14.5 0.9 collective-permute-done.1.refs_4_.refs_3_
  15.4 0.7 shard_map.85
  16.1 5.5 %collective-permute-start.3 = (f32[16,128]{1,0:T(8,128)S(1)}, f32[16,128]{1,0:T(8,128)S(1)}, u32[]{:S(2)}, u32[]{:S(2)}) collective-permute-start(f32[16,128]{1,0:T(8,128)S(1)} %get-tuple-element.33), channel_id=1, source_target_pairs={{0,160},{16,176},{32,128},{48,144},{64,224},{80,240},{96,192},{112... | collective-permute-start | bytes 24584 | tf_op jit(solution)/shard_map/ppermute | solution.py:483
  22.0 4.1 %collective-permute-done.4 = f32[3,16,128]{2,1,0:T(8,128)S(1)} collective-permute-done((f32[3,16,128]{2,1,0:T(8,128)S(1)}, f32[3,16,128]{2,1,0:T(8,128)S(1)}, u32[]{:S(2)}, u32[]{:S(2)}) %collective-permute-start.4) | collective-permute-done | bytes 24608 | tf_op jit(solution)/shard_map/ppermute | solution.py:431
  26.1 6.3 %all-to-all-done.refs_5_.refs_3_ = f32[8,18,8,128]{3,2,1,0:T(8,128)S(1)} async-done(((f32[8,18,8,128]{3,2,1,0:T(8,128)}), f32[8,18,8,128]{3,2,1,0:T(8,128)S(1)}, u32[]{:S(2)}, u32[]{:S(2)}) %all-to-all-start) | async-done | bytes 589856 | tf_op jit(solution)/shard_map/all_to_all | solution.py:442
  33.2 21.1 %all_to_all.20.refs_0_.refs_1_ = f32[8,18,8,128]{3,2,1,0:T(8,128)S(1)} all-to-all(f32[8,18,8,128]{3,2,1,0:T(8,128)S(1)} %shard_map.86), channel_id=1, replica_groups={{0,2,4,6,8,10,12,14},{1,3,5,7,9,11,13,15},{16,18,20,22,24,26,28,30},{17..., dimensions={0} | all-to-all | bytes 1179648 | tf_op jit(solution)/shard_map/all_to_all | solution.py:442
  54.3 1.4 %collective-permute-start.5 = (f32[44,8,128]{2,1,0:T(8,128)S(1)}, f32[44,8,128]{2,1,0:T(8,128)S(1)}, u32[]{:S(2)}, u32[]{:S(2)}) collective-permute-start(f32[44,8,128]{2,1,0:T(8,128)S(1)} %pad_maximum_fusion), channel_id=1, source_target_pairs={{0,16},{16,32},{32,48},{48,0},{1,17},{17,33},{33,49},{49,1},{2,18}... | collective-permute-start | bytes 540680 | tf_op jit(solution)/shard_map/ppermute | solution.py:426
  55.7 1.5 %collective-permute-start.6 = (f32[44,8,128]{2,1,0:T(8,128)S(1)}, f32[44,8,128]{2,1,0:T(8,128)S(1)}, u32[]{:S(2)}, u32[]{:S(2)}) collective-permute-start(f32[44,8,128]{2,1,0:T(8,128)S(1)} %pad_maximum_fusion.1), channel_id=1, source_target_pairs={{16,0},{32,16},{48,32},{0,48},{17,1},{33,17},{49,33},{1,49},{18,2}... | collective-permute-start | bytes 540680 | tf_op jit(solution)/shard_map/ppermute | solution.py:426
  57.2 1.1 shard_map.87
  58.3 2.3 %collective-permute-done.5.refs_2_ = f32[44,8,128]{2,1,0:T(8,128)S(1)} collective-permute-done((f32[44,8,128]{2,1,0:T(8,128)S(1)}, f32[44,8,128]{2,1,0:T(8,128)S(1)}, u32[]{:S(2)}, u32[]{:S(2)}) %collective-permute-start.5) | collective-permute-done | bytes 180256 | tf_op jit(solution)/shard_map/ppermute | solution.py:426
  61.3 1.3 %collective-permute-start.7 = (f32[208,128]{1,0:T(8,128)S(1)}, f32[208,128]{1,0:T(8,128)S(1)}, u32[]{:S(2)}, u32[]{:S(2)}) collective-permute-start(f32[208,128]{1,0:T(8,128)S(1)} %get-tuple-element.39), channel_id=1, source_target_pairs={{0,64},{64,128},{128,192},{192,0},{1,65},{65,129},{129,193},{193,1... | collective-permute-start | bytes 319496 | tf_op jit(solution)/shard_map/ppermute | solution.py:426
  62.6 1.5 %collective-permute-start.8 = (f32[208,128]{1,0:T(8,128)S(1)}, f32[208,128]{1,0:T(8,128)S(1)}, u32[]{:S(2)}, u32[]{:S(2)}) collective-permute-start(f32[208,128]{1,0:T(8,128)S(1)} %get-tuple-element.40), channel_id=1, source_target_pairs={{64,0},{128,64},{192,128},{0,192},{65,1},{129,65},{193,129},{1,193... | collective-permute-start | bytes 319496 | tf_op jit(solution)/shard_map/ppermute | solution.py:426
  64.0 2.1 %collective-permute-done.7.refs_1_ = f32[208,128]{1,0:T(8,128)S(1)} collective-permute-done((f32[208,128]{1,0:T(8,128)S(1)}, f32[208,128]{1,0:T(8,128)S(1)}, u32[]{:S(2)}, u32[]{:S(2)}) %collective-permute-start.7) | collective-permute-done | bytes 106528 | tf_op jit(solution)/shard_map/ppermute | solution.py:426
  66.1 3.5 %shard_map.89 = (f32[18,64,128]{2,1,0:T(8,128)S(1)}, f32[144,128]{1,0:T(8,128)S(1)}, f32[144,128]{1,0:T(8,128)S(1)}) custom-call(f32[18,64,128]{2,1,0:T(8,128)S(1)} %get-tuple-element.38.refs_0_, f32[208,128]{1,0:T(8,128)S(1)} %collective-permute-done.7.refs_1_, f32[208,128]{1,0:T(8,128)S(1)} %collective-permute-done.8.refs_2_, ...), custom_call_target="tpu_custom_call" | custom-call | flops 1207959552 | bytes 3974144 | tf_op jit(solution)/shard_map/pallas_call | solution.py:30
  69.7 1.5 %collective-permute-start.9 = (f32[144,128]{1,0:T(8,128)S(1)}, f32[144,128]{1,0:T(8,128)S(1)}, u32[]{:S(2)}, u32[]{:S(2)}) collective-permute-start(f32[144,128]{1,0:T(8,128)S(1)} %get-tuple-element.47), channel_id=1, source_target_pairs={{0,64},{64,128},{128,192},{192,0},{1,65},{65,129},{129,193},{193,1... | collective-permute-start | bytes 221192 | tf_op jit(solution)/shard_map/ppermute | solution.py:426
  71.1 1.6 %collective-permute-start.10 = (f32[144,128]{1,0:T(8,128)S(1)}, f32[144,128]{1,0:T(8,128)S(1)}, u32[]{:S(2)}, u32[]{:S(2)}) collective-permute-start(f32[144,128]{1,0:T(8,128)S(1)} %get-tuple-element.48), channel_id=1, source_target_pairs={{64,0},{128,64},{192,128},{0,192},{65,1},{129,65},{193,129},{1,193... | collective-permute-start | bytes 221192 | tf_op jit(solution)/shard_map/ppermute | solution.py:426
  72.7 1.7 %collective-permute-done.9.refs_1_ = f32[144,128]{1,0:T(8,128)S(1)} collective-permute-done((f32[144,128]{1,0:T(8,128)S(1)}, f32[144,128]{1,0:T(8,128)S(1)}, u32[]{:S(2)}, u32[]{:S(2)}) %collective-permute-start.9) | collective-permute-done | bytes 73760 | tf_op jit(solution)/shard_map/ppermute | solution.py:426
  75.1 2.6 %collective-permute-start.12 = (f32[2,18,8,128]{3,2,1,0:T(8,128)S(1)}, f32[2,18,8,128]{3,2,1,0:T(8,128)S(1)}, u32[]{:S(2)}, u32[]{:S(2)}) collective-permute-start(f32[2,18,8,128]{3,2,1,0:T(8,128)S(1)} %get-tuple-element.53), channel_id=1, source_target_pairs={{16,0},{32,16},{48,32},{0,48},{17,1},{33,17},{49,33},{1,49},{18,2}... | collective-permute-start | bytes 442376 | tf_op jit(solution)/shard_map/ppermute | solution.py:426
  77.7 2.1 %collective-permute-done.12.refs_3_ = f32[2,18,8,128]{3,2,1,0:T(8,128)S(1)} collective-permute-done((f32[2,18,8,128]{3,2,1,0:T(8,128)S(1)}, f32[2,18,8,128]{3,2,1,0:T(8,128)S(1)}, u32[]{:S(2)}, u32[]{:S(2)}) %collective-permute-start.12) | collective-permute-done | bytes 147488 | tf_op jit(solution)/shard_map/ppermute | solution.py:426
  79.8 3.1 %collective-permute-done.11.refs_2_ = f32[2,18,8,128]{3,2,1,0:T(8,128)S(1)} collective-permute-done((f32[2,18,8,128]{3,2,1,0:T(8,128)S(1)}, f32[2,18,8,128]{3,2,1,0:T(8,128)S(1)}, u32[]{:S(2)}, u32[]{:S(2)}) %collective-permute-start.11) | collective-permute-done | bytes 147488 | tf_op jit(solution)/shard_map/ppermute | solution.py:426
  83.5 15.4 %all_to_all.21.refs_1_ = f32[8,18,8,128]{3,2,1,0:T(8,128)S(1)} all-to-all(f32[8,18,8,128]{3,2,1,0:T(8,128)S(1)} %shard_map.91), channel_id=1, replica_groups={{0,2,4,6,8,10,12,14},{1,3,5,7,9,11,13,15},{16,18,20,22,24,26,28,30},{17..., dimensions={0} | all-to-all | bytes 1179648 | tf_op jit(solution)/shard_map/all_to_all | solution.py:442
  98.9 0.7 shard_map.92
  99.6 15.4 %all_to_all.22 = f32[8,18,8,128]{3,2,1,0:T(8,128)S(1)} all-to-all(f32[8,18,8,128]{3,2,1,0:T(8,128)S(1)} %shard_map.92), channel_id=1, replica_groups={{0,2,4,6,8,10,12,14},{1,3,5,7,9,11,13,15},{16,18,20,22,24,26,28,30},{17..., dimensions={0} | all-to-all | bytes 1179648 | tf_op jit(solution)/shard_map/all_to_all | solution.py:442
  115.0 8.6 %collective-permute-start.13 = (f32[8,9,8,128]{3,2,1,0:T(8,128)S(1)}, f32[8,9,8,128]{3,2,1,0:T(8,128)S(1)}, u32[]{:S(2)}, u32[]{:S(2)}) collective-permute-start(f32[8,9,8,128]{3,2,1,0:T(8,128)S(1)} %get-tuple-element.51), channel_id=1, source_target_pairs={{0,1},{1,0},{2,3},{3,2},{4,5},{5,4},{6,7},{7,6},{8,9},{9,8},{10,11... | collective-permute-start | bytes 884744 | tf_op jit(solution)/shard_map/ppermute | solution.py:436
  123.6 1.2 collective-permute-done.13.refs_2_
  124.8 0.9 shard_map.93
  (39 shorter events, 3.9 us)
Async XLA Ops:
  0.0 1.1 copy-start.1
  1.1 4.5 %collective-permute-start = (f32[9,64,128]{2,1,0:T(8,128)S(1)}, f32[9,64,128]{2,1,0:T(8,128)S(1)}, u32[]{:S(2)}, u32[]{:S(2)}) collective-permute-start(f32[9,64,128]{2,1,0:T(8,128)S(1)} %get-tuple-element.29), channel_id=1, source_target_pairs={{0,1},{1,0},{2,3},{3,2},{4,5},{5,4},{6,7},{7,6},{8,9},{9,8},{10,11... | collective-permute-start | bytes 884744 | tf_op jit(solution)/shard_map/ppermute | solution.py:436
  5.6 7.5 %copy-start.2 = (f32[6,3,512]{2,1,0:T(4,128)S(1)}, f32[6,3,512]{2,1,0:T(4,128)}, u32[]{:S(2)}) copy-start(f32[6,3,512]{2,1,0:T(4,128)} %refs_2_.2) | copy-start | bytes 110596
  5.6 7.5 %copy-start.3 = (f32[6,3,31]{2,1,0:T(4,128)S(1)}, f32[6,3,31]{2,1,0:T(4,128)}, u32[]{:S(2)}) copy-start(f32[6,3,31]{2,1,0:T(4,128)} %refs_3_.1) | copy-start | bytes 6700
  5.6 7.5 %copy-start.4 = (f32[6,3,31]{2,1,0:T(4,128)S(1)}, f32[6,3,31]{2,1,0:T(4,128)}, u32[]{:S(2)}) copy-start(f32[6,3,31]{2,1,0:T(4,128)} %refs_4_.1) | copy-start | bytes 6700
  5.7 7.5 %copy-start.5 = (f32[6,3]{0,1:T(4,128)S(1)}, f32[6,3]{0,1:T(4,128)}, u32[]{:S(2)}) copy-start(f32[6,3]{0,1:T(4,128)} %param.13) | copy-start | bytes 220
  6.5 8.8 %copy-start.6 = (s32[512]{0:T(512)S(1)}, s32[512]{0:T(512)}, u32[]{:S(2)}) copy-start(s32[512]{0:T(512)} %param.14) | copy-start | bytes 6148
  6.5 8.8 %copy-start.7 = (s32[512]{0:T(512)S(1)}, s32[512]{0:T(512)}, u32[]{:S(2)}) copy-start(s32[512]{0:T(512)} %param.15) | copy-start | bytes 6148
  6.5 25.9 %copy-start = (f32[6,48,48]{2,1,0:T(8,128)S(1)}, f32[6,48,48]{2,1,0:T(8,128)}, u32[]{:S(2)}) copy-start(f32[6,48,48]{2,1,0:T(8,128)} %refs_2_.3) | copy-start | bytes 165892
  6.5 25.9 %all-to-all-start = ((f32[8,18,8,128]{3,2,1,0:T(8,128)}), f32[8,18,8,128]{3,2,1,0:T(8,128)S(1)}, u32[]{:S(2)}, u32[]{:S(2)}) async-start(f32[8,18,8,128]{3,2,1,0:T(8,128)} %shard_map.83.refs_0_), calls=%async_computation | async-start | bytes 1179648 | tf_op jit(solution)/shard_map/all_to_all | solution.py:442
  13.7 1.6 %collective-permute-start.1 = (f32[9,1,896]{2,1,0:T(1,128)S(1)}, f32[9,1,896]{2,1,0:T(1,128)S(1)}, u32[]{:S(2)}, u32[]{:S(2)}) collective-permute-start(f32[9,1,896]{2,1,0:T(1,128)S(1)} %get-tuple-element.31), channel_id=1, source_target_pairs={{0,1},{1,0},{2,3},{3,2},{4,5},{5,4},{6,7},{7,6},{8,9},{9,8},{10,11... | collective-permute-start | bytes 96776 | tf_op jit(solution)/shard_map/ppermute | solution.py:436
  16.1 10.0 %collective-permute-start.3 = (f32[16,128]{1,0:T(8,128)S(1)}, f32[16,128]{1,0:T(8,128)S(1)}, u32[]{:S(2)}, u32[]{:S(2)}) collective-permute-start(f32[16,128]{1,0:T(8,128)S(1)} %get-tuple-element.33), channel_id=1, source_target_pairs={{0,160},{16,176},{32,128},{48,144},{64,224},{80,240},{96,192},{112... | collective-permute-start | bytes 24584 | tf_op jit(solution)/shard_map/ppermute | solution.py:483
  21.6 4.5 %collective-permute-start.2 = (f32[3,16,128]{2,1,0:T(8,128)S(1)}, f32[3,16,128]{2,1,0:T(8,128)S(1)}, u32[]{:S(2)}, u32[]{:S(2)}) collective-permute-start(f32[3,16,128]{2,1,0:T(8,128)S(1)} %get-tuple-element.32), channel_id=1, source_target_pairs={{0,32},{16,48},{32,0},{48,16},{1,33},{17,49},{33,1},{49,17},{2,34}... | collective-permute-start | bytes 73736 | tf_op jit(solution)/shard_map/ppermute | solution.py:431
  21.6 4.5 %collective-permute-start.4 = (f32[3,16,128]{2,1,0:T(8,128)S(1)}, f32[3,16,128]{2,1,0:T(8,128)S(1)}, u32[]{:S(2)}, u32[]{:S(2)}) collective-permute-start(f32[3,16,128]{2,1,0:T(8,128)S(1)} %get-tuple-element.35), channel_id=1, source_target_pairs={{0,128},{64,192},{128,0},{192,64},{1,129},{65,193},{129,1},{193,65... | collective-permute-start | bytes 73736 | tf_op jit(solution)/shard_map/ppermute | solution.py:431
  54.3 6.3 %collective-permute-start.5 = (f32[44,8,128]{2,1,0:T(8,128)S(1)}, f32[44,8,128]{2,1,0:T(8,128)S(1)}, u32[]{:S(2)}, u32[]{:S(2)}) collective-permute-start(f32[44,8,128]{2,1,0:T(8,128)S(1)} %pad_maximum_fusion), channel_id=1, source_target_pairs={{0,16},{16,32},{32,48},{48,0},{1,17},{17,33},{33,49},{49,1},{2,18}... | collective-permute-start | bytes 540680 | tf_op jit(solution)/shard_map/ppermute | solution.py:426
  55.7 4.9 %collective-permute-start.6 = (f32[44,8,128]{2,1,0:T(8,128)S(1)}, f32[44,8,128]{2,1,0:T(8,128)S(1)}, u32[]{:S(2)}, u32[]{:S(2)}) collective-permute-start(f32[44,8,128]{2,1,0:T(8,128)S(1)} %pad_maximum_fusion.1), channel_id=1, source_target_pairs={{16,0},{32,16},{48,32},{0,48},{17,1},{33,17},{49,33},{1,49},{18,2}... | collective-permute-start | bytes 540680 | tf_op jit(solution)/shard_map/ppermute | solution.py:426
  61.3 4.8 %collective-permute-start.7 = (f32[208,128]{1,0:T(8,128)S(1)}, f32[208,128]{1,0:T(8,128)S(1)}, u32[]{:S(2)}, u32[]{:S(2)}) collective-permute-start(f32[208,128]{1,0:T(8,128)S(1)} %get-tuple-element.39), channel_id=1, source_target_pairs={{0,64},{64,128},{128,192},{192,0},{1,65},{65,129},{129,193},{193,1... | collective-permute-start | bytes 319496 | tf_op jit(solution)/shard_map/ppermute | solution.py:426
  62.6 3.6 %collective-permute-start.8 = (f32[208,128]{1,0:T(8,128)S(1)}, f32[208,128]{1,0:T(8,128)S(1)}, u32[]{:S(2)}, u32[]{:S(2)}) collective-permute-start(f32[208,128]{1,0:T(8,128)S(1)} %get-tuple-element.40), channel_id=1, source_target_pairs={{64,0},{128,64},{192,128},{0,192},{65,1},{129,65},{193,129},{1,193... | collective-permute-start | bytes 319496 | tf_op jit(solution)/shard_map/ppermute | solution.py:426
  69.7 4.7 %collective-permute-start.9 = (f32[144,128]{1,0:T(8,128)S(1)}, f32[144,128]{1,0:T(8,128)S(1)}, u32[]{:S(2)}, u32[]{:S(2)}) collective-permute-start(f32[144,128]{1,0:T(8,128)S(1)} %get-tuple-element.47), channel_id=1, source_target_pairs={{0,64},{64,128},{128,192},{192,0},{1,65},{65,129},{129,193},{193,1... | collective-permute-start | bytes 221192 | tf_op jit(solution)/shard_map/ppermute | solution.py:426
  71.1 3.2 %collective-permute-start.10 = (f32[144,128]{1,0:T(8,128)S(1)}, f32[144,128]{1,0:T(8,128)S(1)}, u32[]{:S(2)}, u32[]{:S(2)}) collective-permute-start(f32[144,128]{1,0:T(8,128)S(1)} %get-tuple-element.48), channel_id=1, source_target_pairs={{64,0},{128,64},{192,128},{0,192},{65,1},{129,65},{193,129},{1,193... | collective-permute-start | bytes 221192 | tf_op jit(solution)/shard_map/ppermute | solution.py:426
  75.1 4.7 %collective-permute-start.12 = (f32[2,18,8,128]{3,2,1,0:T(8,128)S(1)}, f32[2,18,8,128]{3,2,1,0:T(8,128)S(1)}, u32[]{:S(2)}, u32[]{:S(2)}) collective-permute-start(f32[2,18,8,128]{3,2,1,0:T(8,128)S(1)} %get-tuple-element.53), channel_id=1, source_target_pairs={{16,0},{32,16},{48,32},{0,48},{17,1},{33,17},{49,33},{1,49},{18,2}... | collective-permute-start | bytes 442376 | tf_op jit(solution)/shard_map/ppermute | solution.py:426
  77.6 5.2 %collective-permute-start.11 = (f32[2,18,8,128]{3,2,1,0:T(8,128)S(1)}, f32[2,18,8,128]{3,2,1,0:T(8,128)S(1)}, u32[]{:S(2)}, u32[]{:S(2)}) collective-permute-start(f32[2,18,8,128]{3,2,1,0:T(8,128)S(1)} %get-tuple-element.54), channel_id=1, source_target_pairs={{0,16},{16,32},{32,48},{48,0},{1,17},{17,33},{33,49},{49,1},{2,18}... | collective-permute-start | bytes 442376 | tf_op jit(solution)/shard_map/ppermute | solution.py:426
  115.0 9.8 %collective-permute-start.13 = (f32[8,9,8,128]{3,2,1,0:T(8,128)S(1)}, f32[8,9,8,128]{3,2,1,0:T(8,128)S(1)}, u32[]{:S(2)}, u32[]{:S(2)}) collective-permute-start(f32[8,9,8,128]{3,2,1,0:T(8,128)S(1)} %get-tuple-element.51), channel_id=1, source_target_pairs={{0,1},{1,0},{2,3},{3,2},{4,5},{5,4},{6,7},{7,6},{8,9},{9,8},{10,11... | collective-permute-start | bytes 884744 | tf_op jit(solution)/shard_map/ppermute | solution.py:436

commit v6 on v5

--- a/solution.py
+++ b/solution.py
@@ -92,10 +92,8 @@
 def mixed(matrix, held, v, side):
     at = [pl.ds(v * LEVELS * 8 + s, LEVELS, stride=8) for s in range(8)]
     columns = jnp.concatenate([held[a, :] for a in at], axis=1)
-    result = lax.dot_general(
-        matrix, columns, (((side,), (0,)), ((), ())),
-        precision=lax.Precision.HIGHEST, preferred_element_type=F32,
-    )
+    (m_high, m_low), (c_high, c_low) = split(matrix.T if side == 0 else matrix), split(columns)
+    result = mm(m_high, c_high) + (mm(m_high, c_low) + mm(m_low, c_high))
     for s in range(8):
         held[at[s], :] = result[:, s * COLS : (s + 1) * COLS]
 
@@ -285,12 +283,14 @@
     lax.fori_loop(0, nv, one, 0, unroll=True)
 
 
-def back_lon_body(nv, field, left, right, high, low, out):
+def back_lon_body(nv, field, left, right, high, low, out, last, lead):
     def one(v, carry):
         for l in range(OWN):
             p = v * OWN + l
             value = back_lon_filter(p, l, field[p], left[rows_at(v), :], right[rows_at(v), :], high, low)
             out[:, p] = value.reshape(RINGS, 8, COLS)
+            last[:, p] = value[ROWS - STRIP :].reshape(2, 8, COLS)
+            lead[:, p] = value[:STRIP].reshape(2, 8, COLS)
         return carry
 
     lax.fori_loop(0, nv, one, 0, unroll=True)
@@ -530,13 +530,14 @@
         flops=2 * planes * ROWS * slots * 256 * 2,
     )
     left, right = exchanged(last, lead, "lon")
-    back = kernel_call(
+    strip_shape = shape(2, planes, 8, COLS)
+    back, last, lead = kernel_call(
         functools.partial(back_lon_body, nv),
-        [shape(RINGS, planes, 8, COLS)],
+        [shape(RINGS, planes, 8, COLS), strip_shape, strip_shape],
         [placed, left, right, lon_high, lon_low],
         flops=2 * lat_flops,
-    )[0]
-    before, after = exchanged(back[6:8], back[0:2], "lat")
+    )
+    before, after = exchanged(last, lead, "lat")
     back = kernel_call(
         functools.partial(back_lat_body, nv),
         [shape(RINGS, planes, 8, COLS)],

time: 126 us -> 123 us (0.976)
  waiting for transfers between devices: 25 us -> 22.3 us
    ppermute x8, waiting for transfers between devices: 11.3 us -> 8.6 us  [exchanged(): return (lax.ppermute(last, axis, up), lax.ppermute(first, axis, down))]
  transfers between devices with their start and end apart: 15 -> 15, of which waited for: 10 -> 9; matrix products, arithmetic and copies ran while one was open for 0% -> 0% of each run, Pallas kernels for 2% -> 2%
where the time goes in v6:
time: 123 us
  blocking collectives  51.7 us (42%)
  starting transfers between devices  36.6 us (30%)
  waiting for transfers between devices  22.3 us (18%)
  Pallas kernels  10.5 us (9%)
    all_to_all x3, blocking collectives, over_rings(): lax.all_to_all(value, 'lev', 0, 0, tiled=True, axis_index_groups=groups)  51.7 us
    ppermute x3, starting transfers between devices, with_mate(): return lax.ppermute(value, 'lev', pairs)  12.7 us
    ppermute x8, starting transfers between devices, exchanged(): return (lax.ppermute(last, axis, up), lax.ppermute(first, axis, down))  11.5 us
    pallas_call x12, Pallas kernels, kernel_call(): pl.pallas_call(lambda *refs: body(*refs[count:]), out_shape=list(outs), i...  10.5 us
    ppermute x8, waiting for transfers between devices, exchanged(): return (lax.ppermute(last, axis, up), lax.ppermute(first, axis, down))  8.6 us
    all_to_all x1, starting transfers between devices, over_rings(): lax.all_to_all(value, 'lev', 0, 0, tiled=True, axis_index_groups=groups)  6.58 us
    all_to_all x1, waiting for transfers between devices, over_rings(): lax.all_to_all(value, 'lev', 0, 0, tiled=True, axis_index_groups=groups)  6.31 us
    ppermute x1, starting transfers between devices, local(): by_both = lax.ppermute(by_both, ('lon', 'lat'), opposite)  5.46 us
  transfers between devices with their start and end apart: 15, of which 9 were waited for; matrix products, arithmetic and copies ran while one was open for 0% of the time, Pallas kernels for 2%

profile of v6, /device:TPU:1, one launch (start us, length us, event | category | flops | bytes accessed | tf_op | source)
XLA Modules:
  0.0 122.5 jit_solution(7220989734989260328)
XLA Ops:
  0.0 1.1 copy-done.1
  1.1 3.3 %collective-permute-start = (f32[9,64,128]{2,1,0:T(8,128)S(1)}, f32[9,64,128]{2,1,0:T(8,128)S(1)}, u32[]{:S(2)}, u32[]{:S(2)}) collective-permute-start(f32[9,64,128]{2,1,0:T(8,128)S(1)} %get-tuple-element.32), channel_id=1, source_target_pairs={{0,1},{1,0},{2,3},{3,2},{4,5},{5,4},{6,7},{7,6},{8,9},{9,8},{10,11... | collective-permute-start | bytes 884744 | tf_op jit(solution)/shard_map/ppermute | solution.py:436
  4.4 1.2 collective-permute-done.refs_1_
  5.7 0.9 shard_map.83.refs_0_
  6.5 6.6 %all-to-all-start = ((f32[8,18,8,128]{3,2,1,0:T(8,128)}), f32[8,18,8,128]{3,2,1,0:T(8,128)S(1)}, u32[]{:S(2)}, u32[]{:S(2)}) async-start(f32[8,18,8,128]{3,2,1,0:T(8,128)} %shard_map.83.refs_0_), calls=%async_computation | async-start | bytes 1179648 | tf_op jit(solution)/shard_map/all_to_all | solution.py:442
  13.7 0.7 collective-permute-start.1
  14.5 0.9 collective-permute-done.1.refs_4_.refs_3_
  15.4 0.7 shard_map.85
  16.1 5.5 %collective-permute-start.3 = (f32[16,128]{1,0:T(8,128)S(1)}, f32[16,128]{1,0:T(8,128)S(1)}, u32[]{:S(2)}, u32[]{:S(2)}) collective-permute-start(f32[16,128]{1,0:T(8,128)S(1)} %get-tuple-element.36), channel_id=1, source_target_pairs={{0,160},{16,176},{32,128},{48,144},{64,224},{80,240},{96,192},{112... | collective-permute-start | bytes 24584 | tf_op jit(solution)/shard_map/ppermute | solution.py:483
  22.0 4.1 %collective-permute-done.4 = f32[3,16,128]{2,1,0:T(8,128)S(1)} collective-permute-done((f32[3,16,128]{2,1,0:T(8,128)S(1)}, f32[3,16,128]{2,1,0:T(8,128)S(1)}, u32[]{:S(2)}, u32[]{:S(2)}) %collective-permute-start.4) | collective-permute-done | bytes 24608 | tf_op jit(solution)/shard_map/ppermute | solution.py:431
  26.1 6.3 %all-to-all-done.refs_5_.refs_3_ = f32[8,18,8,128]{3,2,1,0:T(8,128)S(1)} async-done(((f32[8,18,8,128]{3,2,1,0:T(8,128)}), f32[8,18,8,128]{3,2,1,0:T(8,128)S(1)}, u32[]{:S(2)}, u32[]{:S(2)}) %all-to-all-start) | async-done | bytes 589856 | tf_op jit(solution)/shard_map/all_to_all | solution.py:442
  32.9 21.0 %all_to_all.20.refs_0_.refs_1_ = f32[8,18,8,128]{3,2,1,0:T(8,128)S(1)} all-to-all(f32[8,18,8,128]{3,2,1,0:T(8,128)S(1)} %shard_map.86), channel_id=1, replica_groups={{0,2,4,6,8,10,12,14},{1,3,5,7,9,11,13,15},{16,18,20,22,24,26,28,30},{17..., dimensions={0} | all-to-all | bytes 1179648 | tf_op jit(solution)/shard_map/all_to_all | solution.py:442
  54.0 1.4 %collective-permute-start.5 = (f32[44,8,128]{2,1,0:T(8,128)S(1)}, f32[44,8,128]{2,1,0:T(8,128)S(1)}, u32[]{:S(2)}, u32[]{:S(2)}) collective-permute-start(f32[44,8,128]{2,1,0:T(8,128)S(1)} %pad_maximum_fusion), channel_id=1, source_target_pairs={{0,16},{16,32},{32,48},{48,0},{1,17},{17,33},{33,49},{49,1},{2,18}... | collective-permute-start | bytes 540680 | tf_op jit(solution)/shard_map/ppermute | solution.py:426
  55.3 1.6 %collective-permute-start.6 = (f32[44,8,128]{2,1,0:T(8,128)S(1)}, f32[44,8,128]{2,1,0:T(8,128)S(1)}, u32[]{:S(2)}, u32[]{:S(2)}) collective-permute-start(f32[44,8,128]{2,1,0:T(8,128)S(1)} %pad_maximum_fusion.1), channel_id=1, source_target_pairs={{16,0},{32,16},{48,32},{0,48},{17,1},{33,17},{49,33},{1,49},{18,2}... | collective-permute-start | bytes 540680 | tf_op jit(solution)/shard_map/ppermute | solution.py:426
  57.0 1.1 shard_map.87
  58.0 2.3 %collective-permute-done.5.refs_2_ = f32[44,8,128]{2,1,0:T(8,128)S(1)} collective-permute-done((f32[44,8,128]{2,1,0:T(8,128)S(1)}, f32[44,8,128]{2,1,0:T(8,128)S(1)}, u32[]{:S(2)}, u32[]{:S(2)}) %collective-permute-start.5) | collective-permute-done | bytes 180256 | tf_op jit(solution)/shard_map/ppermute | solution.py:426
  60.3 0.7 shard_map.88
  61.0 1.1 collective-permute-start.7
  62.2 1.6 %collective-permute-start.8 = (f32[208,128]{1,0:T(8,128)S(1)}, f32[208,128]{1,0:T(8,128)S(1)}, u32[]{:S(2)}, u32[]{:S(2)}) collective-permute-start(f32[208,128]{1,0:T(8,128)S(1)} %get-tuple-element.43), channel_id=1, source_target_pairs={{64,0},{128,64},{192,128},{0,192},{65,1},{129,65},{193,129},{1,193... | collective-permute-start | bytes 319496 | tf_op jit(solution)/shard_map/ppermute | solution.py:426
  63.8 2.1 %collective-permute-done.7.refs_1_ = f32[208,128]{1,0:T(8,128)S(1)} collective-permute-done((f32[208,128]{1,0:T(8,128)S(1)}, f32[208,128]{1,0:T(8,128)S(1)}, u32[]{:S(2)}, u32[]{:S(2)}) %collective-permute-start.7) | collective-permute-done | bytes 106528 | tf_op jit(solution)/shard_map/ppermute | solution.py:426
  65.9 3.5 %shard_map.89 = (f32[18,64,128]{2,1,0:T(8,128)S(1)}, f32[144,128]{1,0:T(8,128)S(1)}, f32[144,128]{1,0:T(8,128)S(1)}) custom-call(f32[18,64,128]{2,1,0:T(8,128)S(1)} %get-tuple-element.41.refs_0_, f32[208,128]{1,0:T(8,128)S(1)} %collective-permute-done.7.refs_1_, f32[208,128]{1,0:T(8,128)S(1)} %collective-permute-done.8.refs_2_, ...), custom_call_target="tpu_custom_call" | custom-call | flops 1207959552 | bytes 3974144 | tf_op jit(solution)/shard_map/pallas_call | solution.py:30
  69.4 1.4 %collective-permute-start.9 = (f32[144,128]{1,0:T(8,128)S(1)}, f32[144,128]{1,0:T(8,128)S(1)}, u32[]{:S(2)}, u32[]{:S(2)}) collective-permute-start(f32[144,128]{1,0:T(8,128)S(1)} %get-tuple-element.50), channel_id=1, source_target_pairs={{0,64},{64,128},{128,192},{192,0},{1,65},{65,129},{129,193},{193,1... | collective-permute-start | bytes 221192 | tf_op jit(solution)/shard_map/ppermute | solution.py:426
  70.8 1.6 %collective-permute-start.10 = (f32[144,128]{1,0:T(8,128)S(1)}, f32[144,128]{1,0:T(8,128)S(1)}, u32[]{:S(2)}, u32[]{:S(2)}) collective-permute-start(f32[144,128]{1,0:T(8,128)S(1)} %get-tuple-element.51), channel_id=1, source_target_pairs={{64,0},{128,64},{192,128},{0,192},{65,1},{129,65},{193,129},{1,193... | collective-permute-start | bytes 221192 | tf_op jit(solution)/shard_map/ppermute | solution.py:426
  72.4 1.7 %collective-permute-done.9.refs_1_ = f32[144,128]{1,0:T(8,128)S(1)} collective-permute-done((f32[144,128]{1,0:T(8,128)S(1)}, f32[144,128]{1,0:T(8,128)S(1)}, u32[]{:S(2)}, u32[]{:S(2)}) %collective-permute-start.9) | collective-permute-done | bytes 73760 | tf_op jit(solution)/shard_map/ppermute | solution.py:426
  74.7 1.2 collective-permute-start.11
  75.9 1.6 %collective-permute-start.12 = (f32[2,18,8,128]{3,2,1,0:T(8,128)S(1)}, f32[2,18,8,128]{3,2,1,0:T(8,128)S(1)}, u32[]{:S(2)}, u32[]{:S(2)}) collective-permute-start(f32[2,18,8,128]{3,2,1,0:T(8,128)S(1)} %get-tuple-element.54), channel_id=1, source_target_pairs={{16,0},{32,16},{48,32},{0,48},{17,1},{33,17},{49,33},{1,49},{18,2}... | collective-permute-start | bytes 442376 | tf_op jit(solution)/shard_map/ppermute | solution.py:426
  77.5 2.5 %collective-permute-done.11.refs_2_ = f32[2,18,8,128]{3,2,1,0:T(8,128)S(1)} collective-permute-done((f32[2,18,8,128]{3,2,1,0:T(8,128)S(1)}, f32[2,18,8,128]{3,2,1,0:T(8,128)S(1)}, u32[]{:S(2)}, u32[]{:S(2)}) %collective-permute-start.11) | collective-permute-done | bytes 147488 | tf_op jit(solution)/shard_map/ppermute | solution.py:426
  80.6 15.3 %all_to_all.21.refs_1_ = f32[8,18,8,128]{3,2,1,0:T(8,128)S(1)} all-to-all(f32[8,18,8,128]{3,2,1,0:T(8,128)S(1)} %shard_map.91), channel_id=1, replica_groups={{0,2,4,6,8,10,12,14},{1,3,5,7,9,11,13,15},{16,18,20,22,24,26,28,30},{17..., dimensions={0} | all-to-all | bytes 1179648 | tf_op jit(solution)/shard_map/all_to_all | solution.py:442
  96.5 15.3 %all_to_all.22 = f32[8,18,8,128]{3,2,1,0:T(8,128)S(1)} all-to-all(f32[8,18,8,128]{3,2,1,0:T(8,128)S(1)} %shard_map.92), channel_id=1, replica_groups={{0,2,4,6,8,10,12,14},{1,3,5,7,9,11,13,15},{16,18,20,22,24,26,28,30},{17..., dimensions={0} | all-to-all | bytes 1179648 | tf_op jit(solution)/shard_map/all_to_all | solution.py:442
  111.9 8.6 %collective-permute-start.13 = (f32[8,9,8,128]{3,2,1,0:T(8,128)S(1)}, f32[8,9,8,128]{3,2,1,0:T(8,128)S(1)}, u32[]{:S(2)}, u32[]{:S(2)}) collective-permute-start(f32[8,9,8,128]{3,2,1,0:T(8,128)S(1)} %get-tuple-element.57), channel_id=1, source_target_pairs={{0,1},{1,0},{2,3},{3,2},{4,5},{5,4},{6,7},{7,6},{8,9},{9,8},{10,11... | collective-permute-start | bytes 884744 | tf_op jit(solution)/shard_map/ppermute | solution.py:436
  120.5 1.2 collective-permute-done.13.refs_2_
  121.7 0.9 shard_map.93
  (38 shorter events, 3.4 us)
Async XLA Ops:
  0.0 1.1 copy-start.1
  1.1 4.5 %collective-permute-start = (f32[9,64,128]{2,1,0:T(8,128)S(1)}, f32[9,64,128]{2,1,0:T(8,128)S(1)}, u32[]{:S(2)}, u32[]{:S(2)}) collective-permute-start(f32[9,64,128]{2,1,0:T(8,128)S(1)} %get-tuple-element.32), channel_id=1, source_target_pairs={{0,1},{1,0},{2,3},{3,2},{4,5},{5,4},{6,7},{7,6},{8,9},{9,8},{10,11... | collective-permute-start | bytes 884744 | tf_op jit(solution)/shard_map/ppermute | solution.py:436
  5.6 7.5 %copy-start.2 = (f32[6,3,512]{2,1,0:T(4,128)S(1)}, f32[6,3,512]{2,1,0:T(4,128)}, u32[]{:S(2)}) copy-start(f32[6,3,512]{2,1,0:T(4,128)} %refs_2_.2) | copy-start | bytes 110596
  5.6 7.5 %copy-start.3 = (f32[6,3,31]{2,1,0:T(4,128)S(1)}, f32[6,3,31]{2,1,0:T(4,128)}, u32[]{:S(2)}) copy-start(f32[6,3,31]{2,1,0:T(4,128)} %refs_3_.1) | copy-start | bytes 6700
  5.6 7.5 %copy-start.4 = (f32[6,3,31]{2,1,0:T(4,128)S(1)}, f32[6,3,31]{2,1,0:T(4,128)}, u32[]{:S(2)}) copy-start(f32[6,3,31]{2,1,0:T(4,128)} %refs_4_.1) | copy-start | bytes 6700
  5.7 7.5 %copy-start.5 = (f32[6,3]{0,1:T(4,128)S(1)}, f32[6,3]{0,1:T(4,128)}, u32[]{:S(2)}) copy-start(f32[6,3]{0,1:T(4,128)} %param.13) | copy-start | bytes 220
  6.5 8.8 %copy-start.6 = (s32[512]{0:T(512)S(1)}, s32[512]{0:T(512)}, u32[]{:S(2)}) copy-start(s32[512]{0:T(512)} %param.14) | copy-start | bytes 6148
  6.5 8.8 %copy-start.7 = (s32[512]{0:T(512)S(1)}, s32[512]{0:T(512)}, u32[]{:S(2)}) copy-start(s32[512]{0:T(512)} %param.15) | copy-start | bytes 6148
  6.5 25.9 %copy-start = (f32[6,48,48]{2,1,0:T(8,128)S(1)}, f32[6,48,48]{2,1,0:T(8,128)}, u32[]{:S(2)}) copy-start(f32[6,48,48]{2,1,0:T(8,128)} %refs_2_.3) | copy-start | bytes 165892
  6.5 25.9 %all-to-all-start = ((f32[8,18,8,128]{3,2,1,0:T(8,128)}), f32[8,18,8,128]{3,2,1,0:T(8,128)S(1)}, u32[]{:S(2)}, u32[]{:S(2)}) async-start(f32[8,18,8,128]{3,2,1,0:T(8,128)} %shard_map.83.refs_0_), calls=%async_computation | async-start | bytes 1179648 | tf_op jit(solution)/shard_map/all_to_all | solution.py:442
  13.7 1.6 %collective-permute-start.1 = (f32[9,1,896]{2,1,0:T(1,128)S(1)}, f32[9,1,896]{2,1,0:T(1,128)S(1)}, u32[]{:S(2)}, u32[]{:S(2)}) collective-permute-start(f32[9,1,896]{2,1,0:T(1,128)S(1)} %get-tuple-element.34), channel_id=1, source_target_pairs={{0,1},{1,0},{2,3},{3,2},{4,5},{5,4},{6,7},{7,6},{8,9},{9,8},{10,11... | collective-permute-start | bytes 96776 | tf_op jit(solution)/shard_map/ppermute | solution.py:436
  16.1 10.0 %collective-permute-start.3 = (f32[16,128]{1,0:T(8,128)S(1)}, f32[16,128]{1,0:T(8,128)S(1)}, u32[]{:S(2)}, u32[]{:S(2)}) collective-permute-start(f32[16,128]{1,0:T(8,128)S(1)} %get-tuple-element.36), channel_id=1, source_target_pairs={{0,160},{16,176},{32,128},{48,144},{64,224},{80,240},{96,192},{112... | collective-permute-start | bytes 24584 | tf_op jit(solution)/shard_map/ppermute | solution.py:483
  21.6 4.5 %collective-permute-start.2 = (f32[3,16,128]{2,1,0:T(8,128)S(1)}, f32[3,16,128]{2,1,0:T(8,128)S(1)}, u32[]{:S(2)}, u32[]{:S(2)}) collective-permute-start(f32[3,16,128]{2,1,0:T(8,128)S(1)} %get-tuple-element.35), channel_id=1, source_target_pairs={{0,32},{16,48},{32,0},{48,16},{1,33},{17,49},{33,1},{49,17},{2,34}... | collective-permute-start | bytes 73736 | tf_op jit(solution)/shard_map/ppermute | solution.py:431
  21.6 4.5 %collective-permute-start.4 = (f32[3,16,128]{2,1,0:T(8,128)S(1)}, f32[3,16,128]{2,1,0:T(8,128)S(1)}, u32[]{:S(2)}, u32[]{:S(2)}) collective-permute-start(f32[3,16,128]{2,1,0:T(8,128)S(1)} %get-tuple-element.38), channel_id=1, source_target_pairs={{0,128},{64,192},{128,0},{192,64},{1,129},{65,193},{129,1},{193,65... | collective-permute-start | bytes 73736 | tf_op jit(solution)/shard_map/ppermute | solution.py:431
  54.0 6.4 %collective-permute-start.5 = (f32[44,8,128]{2,1,0:T(8,128)S(1)}, f32[44,8,128]{2,1,0:T(8,128)S(1)}, u32[]{:S(2)}, u32[]{:S(2)}) collective-permute-start(f32[44,8,128]{2,1,0:T(8,128)S(1)} %pad_maximum_fusion), channel_id=1, source_target_pairs={{0,16},{16,32},{32,48},{48,0},{1,17},{17,33},{33,49},{49,1},{2,18}... | collective-permute-start | bytes 540680 | tf_op jit(solution)/shard_map/ppermute | solution.py:426
  55.3 5.0 %collective-permute-start.6 = (f32[44,8,128]{2,1,0:T(8,128)S(1)}, f32[44,8,128]{2,1,0:T(8,128)S(1)}, u32[]{:S(2)}, u32[]{:S(2)}) collective-permute-start(f32[44,8,128]{2,1,0:T(8,128)S(1)} %pad_maximum_fusion.1), channel_id=1, source_target_pairs={{16,0},{32,16},{48,32},{0,48},{17,1},{33,17},{49,33},{1,49},{18,2}... | collective-permute-start | bytes 540680 | tf_op jit(solution)/shard_map/ppermute | solution.py:426
  61.0 4.8 %collective-permute-start.7 = (f32[208,128]{1,0:T(8,128)S(1)}, f32[208,128]{1,0:T(8,128)S(1)}, u32[]{:S(2)}, u32[]{:S(2)}) collective-permute-start(f32[208,128]{1,0:T(8,128)S(1)} %get-tuple-element.42), channel_id=1, source_target_pairs={{0,64},{64,128},{128,192},{192,0},{1,65},{65,129},{129,193},{193,1... | collective-permute-start | bytes 319496 | tf_op jit(solution)/shard_map/ppermute | solution.py:426
  62.2 3.7 %collective-permute-start.8 = (f32[208,128]{1,0:T(8,128)S(1)}, f32[208,128]{1,0:T(8,128)S(1)}, u32[]{:S(2)}, u32[]{:S(2)}) collective-permute-start(f32[208,128]{1,0:T(8,128)S(1)} %get-tuple-element.43), channel_id=1, source_target_pairs={{64,0},{128,64},{192,128},{0,192},{65,1},{129,65},{193,129},{1,193... | collective-permute-start | bytes 319496 | tf_op jit(solution)/shard_map/ppermute | solution.py:426
  69.4 4.7 %collective-permute-start.9 = (f32[144,128]{1,0:T(8,128)S(1)}, f32[144,128]{1,0:T(8,128)S(1)}, u32[]{:S(2)}, u32[]{:S(2)}) collective-permute-start(f32[144,128]{1,0:T(8,128)S(1)} %get-tuple-element.50), channel_id=1, source_target_pairs={{0,64},{64,128},{128,192},{192,0},{1,65},{65,129},{129,193},{193,1... | collective-permute-start | bytes 221192 | tf_op jit(solution)/shard_map/ppermute | solution.py:426
  70.8 3.2 %collective-permute-start.10 = (f32[144,128]{1,0:T(8,128)S(1)}, f32[144,128]{1,0:T(8,128)S(1)}, u32[]{:S(2)}, u32[]{:S(2)}) collective-permute-start(f32[144,128]{1,0:T(8,128)S(1)} %get-tuple-element.51), channel_id=1, source_target_pairs={{64,0},{128,64},{192,128},{0,192},{65,1},{129,65},{193,129},{1,193... | collective-permute-start | bytes 221192 | tf_op jit(solution)/shard_map/ppermute | solution.py:426
  74.7 5.3 %collective-permute-start.11 = (f32[2,18,8,128]{3,2,1,0:T(8,128)S(1)}, f32[2,18,8,128]{3,2,1,0:T(8,128)S(1)}, u32[]{:S(2)}, u32[]{:S(2)}) collective-permute-start(f32[2,18,8,128]{3,2,1,0:T(8,128)S(1)} %get-tuple-element.53), channel_id=1, source_target_pairs={{0,16},{16,32},{32,48},{48,0},{1,17},{17,33},{33,49},{49,1},{2,18}... | collective-permute-start | bytes 442376 | tf_op jit(solution)/shard_map/ppermute | solution.py:426
  75.9 4.1 %collective-permute-start.12 = (f32[2,18,8,128]{3,2,1,0:T(8,128)S(1)}, f32[2,18,8,128]{3,2,1,0:T(8,128)S(1)}, u32[]{:S(2)}, u32[]{:S(2)}) collective-permute-start(f32[2,18,8,128]{3,2,1,0:T(8,128)S(1)} %get-tuple-element.54), channel_id=1, source_target_pairs={{16,0},{32,16},{48,32},{0,48},{17,1},{33,17},{49,33},{1,49},{18,2}... | collective-permute-start | bytes 442376 | tf_op jit(solution)/shard_map/ppermute | solution.py:426
  111.9 9.8 %collective-permute-start.13 = (f32[8,9,8,128]{3,2,1,0:T(8,128)S(1)}, f32[8,9,8,128]{3,2,1,0:T(8,128)S(1)}, u32[]{:S(2)}, u32[]{:S(2)}) collective-permute-start(f32[8,9,8,128]{3,2,1,0:T(8,128)S(1)} %get-tuple-element.57), channel_id=1, source_target_pairs={{0,1},{1,0},{2,3},{3,2},{4,5},{5,4},{6,7},{7,6},{8,9},{9,8},{10,11... | collective-permute-start | bytes 884744 | tf_op jit(solution)/shard_map/ppermute | solution.py:436

commit v7 on v6

--- a/solution.py
+++ b/solution.py
@@ -547,11 +547,11 @@
     )[0]
     result = over_rings(column_call(unmix_body, core, over_rings(back), vertical, columns))
 
-    mine, other = result[:, :9], with_mate(result[:, 9:])
+    other = with_mate(result[:, 9:])
     return kernel_call(
         finish_body,
         [shape(6, 3, ROWS, COLS)],
-        [core, mine, other],
+        [core, result, other],
         smem=(0,),
     )[0]
 

time: 123 us -> 123 us (level)
  no operation moved by 1% of the time
where the time goes in v7:
time: 123 us
  blocking collectives  51.7 us (42%)
  starting transfers between devices  36.6 us (30%)
  waiting for transfers between devices  22.3 us (18%)
  Pallas kernels  10.5 us (9%)
    all_to_all x3, blocking collectives, over_rings(): lax.all_to_all(value, 'lev', 0, 0, tiled=True, axis_index_groups=groups)  51.7 us
    ppermute x3, starting transfers between devices, with_mate(): return lax.ppermute(value, 'lev', pairs)  12.7 us
    ppermute x8, starting transfers between devices, exchanged(): return (lax.ppermute(last, axis, up), lax.ppermute(first, axis, down))  11.5 us
    pallas_call x12, Pallas kernels, kernel_call(): pl.pallas_call(lambda *refs: body(*refs[count:]), out_shape=list(outs), i...  10.5 us
    ppermute x8, waiting for transfers between devices, exchanged(): return (lax.ppermute(last, axis, up), lax.ppermute(first, axis, down))  8.6 us
    all_to_all x1, starting transfers between devices, over_rings(): lax.all_to_all(value, 'lev', 0, 0, tiled=True, axis_index_groups=groups)  6.58 us
    all_to_all x1, waiting for transfers between devices, over_rings(): lax.all_to_all(value, 'lev', 0, 0, tiled=True, axis_index_groups=groups)  6.31 us
    ppermute x1, starting transfers between devices, local(): by_both = lax.ppermute(by_both, ('lon', 'lat'), opposite)  5.46 us
  transfers between devices with their start and end apart: 15, of which 9 were waited for; matrix products, arithmetic and copies ran while one was open for 0% of the time, Pallas kernels for 2%

profile of v7, /device:TPU:1, one launch (start us, length us, event | category | flops | bytes accessed | tf_op | source)
XLA Modules:
  0.0 122.5 jit_solution(4794676366851867270)
XLA Ops:
  0.0 1.1 copy-done.1
  1.1 3.3 %collective-permute-start = (f32[9,64,128]{2,1,0:T(8,128)S(1)}, f32[9,64,128]{2,1,0:T(8,128)S(1)}, u32[]{:S(2)}, u32[]{:S(2)}) collective-permute-start(f32[9,64,128]{2,1,0:T(8,128)S(1)} %get-tuple-element.32), channel_id=1, source_target_pairs={{0,1},{1,0},{2,3},{3,2},{4,5},{5,4},{6,7},{7,6},{8,9},{9,8},{10,11... | collective-permute-start | bytes 884744 | tf_op jit(solution)/shard_map/ppermute | solution.py:436
  4.4 1.2 collective-permute-done.refs_1_
  5.7 0.9 shard_map.83.refs_0_
  6.5 6.6 %all-to-all-start = ((f32[8,18,8,128]{3,2,1,0:T(8,128)}), f32[8,18,8,128]{3,2,1,0:T(8,128)S(1)}, u32[]{:S(2)}, u32[]{:S(2)}) async-start(f32[8,18,8,128]{3,2,1,0:T(8,128)} %shard_map.83.refs_0_), calls=%async_computation | async-start | bytes 1179648 | tf_op jit(solution)/shard_map/all_to_all | solution.py:442
  13.7 0.7 collective-permute-start.1
  14.5 0.9 collective-permute-done.1.refs_4_.refs_3_
  15.4 0.7 shard_map.85
  16.1 5.5 %collective-permute-start.3 = (f32[16,128]{1,0:T(8,128)S(1)}, f32[16,128]{1,0:T(8,128)S(1)}, u32[]{:S(2)}, u32[]{:S(2)}) collective-permute-start(f32[16,128]{1,0:T(8,128)S(1)} %get-tuple-element.36), channel_id=1, source_target_pairs={{0,160},{16,176},{32,128},{48,144},{64,224},{80,240},{96,192},{112... | collective-permute-start | bytes 24584 | tf_op jit(solution)/shard_map/ppermute | solution.py:483
  22.0 4.1 %collective-permute-done.4 = f32[3,16,128]{2,1,0:T(8,128)S(1)} collective-permute-done((f32[3,16,128]{2,1,0:T(8,128)S(1)}, f32[3,16,128]{2,1,0:T(8,128)S(1)}, u32[]{:S(2)}, u32[]{:S(2)}) %collective-permute-start.4) | collective-permute-done | bytes 24608 | tf_op jit(solution)/shard_map/ppermute | solution.py:431
  26.1 6.3 %all-to-all-done.refs_5_.refs_3_ = f32[8,18,8,128]{3,2,1,0:T(8,128)S(1)} async-done(((f32[8,18,8,128]{3,2,1,0:T(8,128)}), f32[8,18,8,128]{3,2,1,0:T(8,128)S(1)}, u32[]{:S(2)}, u32[]{:S(2)}) %all-to-all-start) | async-done | bytes 589856 | tf_op jit(solution)/shard_map/all_to_all | solution.py:442
  32.9 21.0 %all_to_all.20.refs_0_.refs_1_ = f32[8,18,8,128]{3,2,1,0:T(8,128)S(1)} all-to-all(f32[8,18,8,128]{3,2,1,0:T(8,128)S(1)} %shard_map.86), channel_id=1, replica_groups={{0,2,4,6,8,10,12,14},{1,3,5,7,9,11,13,15},{16,18,20,22,24,26,28,30},{17..., dimensions={0} | all-to-all | bytes 1179648 | tf_op jit(solution)/shard_map/all_to_all | solution.py:442
  54.0 1.4 %collective-permute-start.5 = (f32[44,8,128]{2,1,0:T(8,128)S(1)}, f32[44,8,128]{2,1,0:T(8,128)S(1)}, u32[]{:S(2)}, u32[]{:S(2)}) collective-permute-start(f32[44,8,128]{2,1,0:T(8,128)S(1)} %pad_maximum_fusion), channel_id=1, source_target_pairs={{0,16},{16,32},{32,48},{48,0},{1,17},{17,33},{33,49},{49,1},{2,18}... | collective-permute-start | bytes 540680 | tf_op jit(solution)/shard_map/ppermute | solution.py:426
  55.3 1.6 %collective-permute-start.6 = (f32[44,8,128]{2,1,0:T(8,128)S(1)}, f32[44,8,128]{2,1,0:T(8,128)S(1)}, u32[]{:S(2)}, u32[]{:S(2)}) collective-permute-start(f32[44,8,128]{2,1,0:T(8,128)S(1)} %pad_maximum_fusion.1), channel_id=1, source_target_pairs={{16,0},{32,16},{48,32},{0,48},{17,1},{33,17},{49,33},{1,49},{18,2}... | collective-permute-start | bytes 540680 | tf_op jit(solution)/shard_map/ppermute | solution.py:426
  57.0 1.1 shard_map.87
  58.0 2.3 %collective-permute-done.5.refs_2_ = f32[44,8,128]{2,1,0:T(8,128)S(1)} collective-permute-done((f32[44,8,128]{2,1,0:T(8,128)S(1)}, f32[44,8,128]{2,1,0:T(8,128)S(1)}, u32[]{:S(2)}, u32[]{:S(2)}) %collective-permute-start.5) | collective-permute-done | bytes 180256 | tf_op jit(solution)/shard_map/ppermute | solution.py:426
  60.3 0.7 shard_map.88
  61.0 1.1 collective-permute-start.7
  62.2 1.6 %collective-permute-start.8 = (f32[208,128]{1,0:T(8,128)S(1)}, f32[208,128]{1,0:T(8,128)S(1)}, u32[]{:S(2)}, u32[]{:S(2)}) collective-permute-start(f32[208,128]{1,0:T(8,128)S(1)} %get-tuple-element.43), channel_id=1, source_target_pairs={{64,0},{128,64},{192,128},{0,192},{65,1},{129,65},{193,129},{1,193... | collective-permute-start | bytes 319496 | tf_op jit(solution)/shard_map/ppermute | solution.py:426
  63.8 2.1 %collective-permute-done.7.refs_1_ = f32[208,128]{1,0:T(8,128)S(1)} collective-permute-done((f32[208,128]{1,0:T(8,128)S(1)}, f32[208,128]{1,0:T(8,128)S(1)}, u32[]{:S(2)}, u32[]{:S(2)}) %collective-permute-start.7) | collective-permute-done | bytes 106528 | tf_op jit(solution)/shard_map/ppermute | solution.py:426
  65.9 3.5 %shard_map.89 = (f32[18,64,128]{2,1,0:T(8,128)S(1)}, f32[144,128]{1,0:T(8,128)S(1)}, f32[144,128]{1,0:T(8,128)S(1)}) custom-call(f32[18,64,128]{2,1,0:T(8,128)S(1)} %get-tuple-element.41.refs_0_, f32[208,128]{1,0:T(8,128)S(1)} %collective-permute-done.7.refs_1_, f32[208,128]{1,0:T(8,128)S(1)} %collective-permute-done.8.refs_2_, ...), custom_call_target="tpu_custom_call" | custom-call | flops 1207959552 | bytes 3974144 | tf_op jit(solution)/shard_map/pallas_call | solution.py:30
  69.4 1.4 %collective-permute-start.9 = (f32[144,128]{1,0:T(8,128)S(1)}, f32[144,128]{1,0:T(8,128)S(1)}, u32[]{:S(2)}, u32[]{:S(2)}) collective-permute-start(f32[144,128]{1,0:T(8,128)S(1)} %get-tuple-element.50), channel_id=1, source_target_pairs={{0,64},{64,128},{128,192},{192,0},{1,65},{65,129},{129,193},{193,1... | collective-permute-start | bytes 221192 | tf_op jit(solution)/shard_map/ppermute | solution.py:426
  70.8 1.6 %collective-permute-start.10 = (f32[144,128]{1,0:T(8,128)S(1)}, f32[144,128]{1,0:T(8,128)S(1)}, u32[]{:S(2)}, u32[]{:S(2)}) collective-permute-start(f32[144,128]{1,0:T(8,128)S(1)} %get-tuple-element.51), channel_id=1, source_target_pairs={{64,0},{128,64},{192,128},{0,192},{65,1},{129,65},{193,129},{1,193... | collective-permute-start | bytes 221192 | tf_op jit(solution)/shard_map/ppermute | solution.py:426
  72.4 1.7 %collective-permute-done.9.refs_1_ = f32[144,128]{1,0:T(8,128)S(1)} collective-permute-done((f32[144,128]{1,0:T(8,128)S(1)}, f32[144,128]{1,0:T(8,128)S(1)}, u32[]{:S(2)}, u32[]{:S(2)}) %collective-permute-start.9) | collective-permute-done | bytes 73760 | tf_op jit(solution)/shard_map/ppermute | solution.py:426
  74.7 1.2 collective-permute-start.11
  75.9 1.6 %collective-permute-start.12 = (f32[2,18,8,128]{3,2,1,0:T(8,128)S(1)}, f32[2,18,8,128]{3,2,1,0:T(8,128)S(1)}, u32[]{:S(2)}, u32[]{:S(2)}) collective-permute-start(f32[2,18,8,128]{3,2,1,0:T(8,128)S(1)} %get-tuple-element.54), channel_id=1, source_target_pairs={{16,0},{32,16},{48,32},{0,48},{17,1},{33,17},{49,33},{1,49},{18,2}... | collective-permute-start | bytes 442376 | tf_op jit(solution)/shard_map/ppermute | solution.py:426
  77.5 2.5 %collective-permute-done.11.refs_2_ = f32[2,18,8,128]{3,2,1,0:T(8,128)S(1)} collective-permute-done((f32[2,18,8,128]{3,2,1,0:T(8,128)S(1)}, f32[2,18,8,128]{3,2,1,0:T(8,128)S(1)}, u32[]{:S(2)}, u32[]{:S(2)}) %collective-permute-start.11) | collective-permute-done | bytes 147488 | tf_op jit(solution)/shard_map/ppermute | solution.py:426
  80.6 15.3 %all_to_all.21.refs_1_ = f32[8,18,8,128]{3,2,1,0:T(8,128)S(1)} all-to-all(f32[8,18,8,128]{3,2,1,0:T(8,128)S(1)} %shard_map.91), channel_id=1, replica_groups={{0,2,4,6,8,10,12,14},{1,3,5,7,9,11,13,15},{16,18,20,22,24,26,28,30},{17..., dimensions={0} | all-to-all | bytes 1179648 | tf_op jit(solution)/shard_map/all_to_all | solution.py:442
  96.5 15.3 %all_to_all.22.refs_1_ = f32[8,18,8,128]{3,2,1,0:T(8,128)S(1)} all-to-all(f32[8,18,8,128]{3,2,1,0:T(8,128)S(1)} %shard_map.92), channel_id=1, replica_groups={{0,2,4,6,8,10,12,14},{1,3,5,7,9,11,13,15},{16,18,20,22,24,26,28,30},{17..., dimensions={0} | all-to-all | bytes 1179648 | tf_op jit(solution)/shard_map/all_to_all | solution.py:442
  111.8 8.6 %collective-permute-start.13 = (f32[8,9,8,128]{3,2,1,0:T(8,128)S(1)}, f32[8,9,8,128]{3,2,1,0:T(8,128)S(1)}, u32[]{:S(2)}, u32[]{:S(2)}) collective-permute-start(f32[8,9,8,128]{3,2,1,0:T(8,128)S(1)} %slice.41), channel_id=1, source_target_pairs={{0,1},{1,0},{2,3},{3,2},{4,5},{5,4},{6,7},{7,6},{8,9},{9,8},{10,11... | collective-permute-start | bytes 884744 | tf_op jit(solution)/shard_map/ppermute | solution.py:436
  120.5 1.2 collective-permute-done.13.refs_2_
  121.7 0.9 shard_map.93
  (38 shorter events, 3.4 us)
Async XLA Ops:
  0.0 1.1 copy-start.1
  1.1 4.5 %collective-permute-start = (f32[9,64,128]{2,1,0:T(8,128)S(1)}, f32[9,64,128]{2,1,0:T(8,128)S(1)}, u32[]{:S(2)}, u32[]{:S(2)}) collective-permute-start(f32[9,64,128]{2,1,0:T(8,128)S(1)} %get-tuple-element.32), channel_id=1, source_target_pairs={{0,1},{1,0},{2,3},{3,2},{4,5},{5,4},{6,7},{7,6},{8,9},{9,8},{10,11... | collective-permute-start | bytes 884744 | tf_op jit(solution)/shard_map/ppermute | solution.py:436
  5.6 7.5 %copy-start.2 = (f32[6,3,512]{2,1,0:T(4,128)S(1)}, f32[6,3,512]{2,1,0:T(4,128)}, u32[]{:S(2)}) copy-start(f32[6,3,512]{2,1,0:T(4,128)} %refs_2_.2) | copy-start | bytes 110596
  5.6 7.5 %copy-start.3 = (f32[6,3,31]{2,1,0:T(4,128)S(1)}, f32[6,3,31]{2,1,0:T(4,128)}, u32[]{:S(2)}) copy-start(f32[6,3,31]{2,1,0:T(4,128)} %refs_3_.1) | copy-start | bytes 6700
  5.6 7.5 %copy-start.4 = (f32[6,3,31]{2,1,0:T(4,128)S(1)}, f32[6,3,31]{2,1,0:T(4,128)}, u32[]{:S(2)}) copy-start(f32[6,3,31]{2,1,0:T(4,128)} %refs_4_.1) | copy-start | bytes 6700
  5.7 7.5 %copy-start.5 = (f32[6,3]{0,1:T(4,128)S(1)}, f32[6,3]{0,1:T(4,128)}, u32[]{:S(2)}) copy-start(f32[6,3]{0,1:T(4,128)} %param.13) | copy-start | bytes 220
  6.5 8.8 %copy-start.6 = (s32[512]{0:T(512)S(1)}, s32[512]{0:T(512)}, u32[]{:S(2)}) copy-start(s32[512]{0:T(512)} %param.14) | copy-start | bytes 6148
  6.5 8.8 %copy-start.7 = (s32[512]{0:T(512)S(1)}, s32[512]{0:T(512)}, u32[]{:S(2)}) copy-start(s32[512]{0:T(512)} %param.15) | copy-start | bytes 6148
  6.5 25.9 %copy-start = (f32[6,48,48]{2,1,0:T(8,128)S(1)}, f32[6,48,48]{2,1,0:T(8,128)}, u32[]{:S(2)}) copy-start(f32[6,48,48]{2,1,0:T(8,128)} %refs_2_.3) | copy-start | bytes 165892
  6.5 25.9 %all-to-all-start = ((f32[8,18,8,128]{3,2,1,0:T(8,128)}), f32[8,18,8,128]{3,2,1,0:T(8,128)S(1)}, u32[]{:S(2)}, u32[]{:S(2)}) async-start(f32[8,18,8,128]{3,2,1,0:T(8,128)} %shard_map.83.refs_0_), calls=%async_computation | async-start | bytes 1179648 | tf_op jit(solution)/shard_map/all_to_all | solution.py:442
  13.7 1.6 %collective-permute-start.1 = (f32[9,1,896]{2,1,0:T(1,128)S(1)}, f32[9,1,896]{2,1,0:T(1,128)S(1)}, u32[]{:S(2)}, u32[]{:S(2)}) collective-permute-start(f32[9,1,896]{2,1,0:T(1,128)S(1)} %get-tuple-element.34), channel_id=1, source_target_pairs={{0,1},{1,0},{2,3},{3,2},{4,5},{5,4},{6,7},{7,6},{8,9},{9,8},{10,11... | collective-permute-start | bytes 96776 | tf_op jit(solution)/shard_map/ppermute | solution.py:436
  16.1 10.0 %collective-permute-start.3 = (f32[16,128]{1,0:T(8,128)S(1)}, f32[16,128]{1,0:T(8,128)S(1)}, u32[]{:S(2)}, u32[]{:S(2)}) collective-permute-start(f32[16,128]{1,0:T(8,128)S(1)} %get-tuple-element.36), channel_id=1, source_target_pairs={{0,160},{16,176},{32,128},{48,144},{64,224},{80,240},{96,192},{112... | collective-permute-start | bytes 24584 | tf_op jit(solution)/shard_map/ppermute | solution.py:483
  21.6 4.5 %collective-permute-start.2 = (f32[3,16,128]{2,1,0:T(8,128)S(1)}, f32[3,16,128]{2,1,0:T(8,128)S(1)}, u32[]{:S(2)}, u32[]{:S(2)}) collective-permute-start(f32[3,16,128]{2,1,0:T(8,128)S(1)} %get-tuple-element.35), channel_id=1, source_target_pairs={{0,32},{16,48},{32,0},{48,16},{1,33},{17,49},{33,1},{49,17},{2,34}... | collective-permute-start | bytes 73736 | tf_op jit(solution)/shard_map/ppermute | solution.py:431
  21.6 4.5 %collective-permute-start.4 = (f32[3,16,128]{2,1,0:T(8,128)S(1)}, f32[3,16,128]{2,1,0:T(8,128)S(1)}, u32[]{:S(2)}, u32[]{:S(2)}) collective-permute-start(f32[3,16,128]{2,1,0:T(8,128)S(1)} %get-tuple-element.38), channel_id=1, source_target_pairs={{0,128},{64,192},{128,0},{192,64},{1,129},{65,193},{129,1},{193,65... | collective-permute-start | bytes 73736 | tf_op jit(solution)/shard_map/ppermute | solution.py:431
  54.0 6.4 %collective-permute-start.5 = (f32[44,8,128]{2,1,0:T(8,128)S(1)}, f32[44,8,128]{2,1,0:T(8,128)S(1)}, u32[]{:S(2)}, u32[]{:S(2)}) collective-permute-start(f32[44,8,128]{2,1,0:T(8,128)S(1)} %pad_maximum_fusion), channel_id=1, source_target_pairs={{0,16},{16,32},{32,48},{48,0},{1,17},{17,33},{33,49},{49,1},{2,18}... | collective-permute-start | bytes 540680 | tf_op jit(solution)/shard_map/ppermute | solution.py:426
  55.3 5.0 %collective-permute-start.6 = (f32[44,8,128]{2,1,0:T(8,128)S(1)}, f32[44,8,128]{2,1,0:T(8,128)S(1)}, u32[]{:S(2)}, u32[]{:S(2)}) collective-permute-start(f32[44,8,128]{2,1,0:T(8,128)S(1)} %pad_maximum_fusion.1), channel_id=1, source_target_pairs={{16,0},{32,16},{48,32},{0,48},{17,1},{33,17},{49,33},{1,49},{18,2}... | collective-permute-start | bytes 540680 | tf_op jit(solution)/shard_map/ppermute | solution.py:426
  61.0 4.8 %collective-permute-start.7 = (f32[208,128]{1,0:T(8,128)S(1)}, f32[208,128]{1,0:T(8,128)S(1)}, u32[]{:S(2)}, u32[]{:S(2)}) collective-permute-start(f32[208,128]{1,0:T(8,128)S(1)} %get-tuple-element.42), channel_id=1, source_target_pairs={{0,64},{64,128},{128,192},{192,0},{1,65},{65,129},{129,193},{193,1... | collective-permute-start | bytes 319496 | tf_op jit(solution)/shard_map/ppermute | solution.py:426
  62.2 3.7 %collective-permute-start.8 = (f32[208,128]{1,0:T(8,128)S(1)}, f32[208,128]{1,0:T(8,128)S(1)}, u32[]{:S(2)}, u32[]{:S(2)}) collective-permute-start(f32[208,128]{1,0:T(8,128)S(1)} %get-tuple-element.43), channel_id=1, source_target_pairs={{64,0},{128,64},{192,128},{0,192},{65,1},{129,65},{193,129},{1,193... | collective-permute-start | bytes 319496 | tf_op jit(solution)/shard_map/ppermute | solution.py:426
  69.4 4.7 %collective-permute-start.9 = (f32[144,128]{1,0:T(8,128)S(1)}, f32[144,128]{1,0:T(8,128)S(1)}, u32[]{:S(2)}, u32[]{:S(2)}) collective-permute-start(f32[144,128]{1,0:T(8,128)S(1)} %get-tuple-element.50), channel_id=1, source_target_pairs={{0,64},{64,128},{128,192},{192,0},{1,65},{65,129},{129,193},{193,1... | collective-permute-start | bytes 221192 | tf_op jit(solution)/shard_map/ppermute | solution.py:426
  70.8 3.2 %collective-permute-start.10 = (f32[144,128]{1,0:T(8,128)S(1)}, f32[144,128]{1,0:T(8,128)S(1)}, u32[]{:S(2)}, u32[]{:S(2)}) collective-permute-start(f32[144,128]{1,0:T(8,128)S(1)} %get-tuple-element.51), channel_id=1, source_target_pairs={{64,0},{128,64},{192,128},{0,192},{65,1},{129,65},{193,129},{1,193... | collective-permute-start | bytes 221192 | tf_op jit(solution)/shard_map/ppermute | solution.py:426
  74.7 5.3 %collective-permute-start.11 = (f32[2,18,8,128]{3,2,1,0:T(8,128)S(1)}, f32[2,18,8,128]{3,2,1,0:T(8,128)S(1)}, u32[]{:S(2)}, u32[]{:S(2)}) collective-permute-start(f32[2,18,8,128]{3,2,1,0:T(8,128)S(1)} %get-tuple-element.53), channel_id=1, source_target_pairs={{0,16},{16,32},{32,48},{48,0},{1,17},{17,33},{33,49},{49,1},{2,18}... | collective-permute-start | bytes 442376 | tf_op jit(solution)/shard_map/ppermute | solution.py:426
  75.9 4.1 %collective-permute-start.12 = (f32[2,18,8,128]{3,2,1,0:T(8,128)S(1)}, f32[2,18,8,128]{3,2,1,0:T(8,128)S(1)}, u32[]{:S(2)}, u32[]{:S(2)}) collective-permute-start(f32[2,18,8,128]{3,2,1,0:T(8,128)S(1)} %get-tuple-element.54), channel_id=1, source_target_pairs={{16,0},{32,16},{48,32},{0,48},{17,1},{33,17},{49,33},{1,49},{18,2}... | collective-permute-start | bytes 442376 | tf_op jit(solution)/shard_map/ppermute | solution.py:426
  111.8 9.8 %collective-permute-start.13 = (f32[8,9,8,128]{3,2,1,0:T(8,128)S(1)}, f32[8,9,8,128]{3,2,1,0:T(8,128)S(1)}, u32[]{:S(2)}, u32[]{:S(2)}) collective-permute-start(f32[8,9,8,128]{3,2,1,0:T(8,128)S(1)} %slice.41), channel_id=1, source_target_pairs={{0,1},{1,0},{2,3},{3,2},{4,5},{5,4},{6,7},{7,6},{8,9},{9,8},{10,11... | collective-permute-start | bytes 884744 | tf_op jit(solution)/shard_map/ppermute | solution.py:436
